TPU v7x, 32 devices: a whole 2x2x4 slice. The times are simulated.
32 devices in a mesh: fsdp: 4 (over y, x), seq: 8 (over z, core).
Axes of the slice: x: 2, y: 2, z: 4, core: 2. Of those that a mesh axis runs over, the one named last changes fastest.
Arguments:
- tokens: bfloat16 [2, 4, 256, 8, 768], P(None, 'fsdp', None, 'seq'), may hold values from -6 to 6
- image_tokens: int32 [2, 4, 2, 3], P(None, 'fsdp'), may hold values from 0 to 1029, as said below
- ln1_gain: bfloat16 [768], P('fsdp'), may hold values from 0.099609375 to 1.8984375
- ln1_bias: bfloat16 [768], P('fsdp'), may hold values from -1.75 to 1.75
- qkv_weight: bfloat16 [768, 2304], P('fsdp'), may hold values from -0.21875 to 0.21875
- query_bias: bfloat16 [768], P('fsdp'), may hold values from -3 to 3
- value_bias: bfloat16 [768], P('fsdp'), may hold values from -3 to 3
- out_weight: bfloat16 [768, 768], P('fsdp'), may hold values from -3.5 to 3.5
- out_bias: bfloat16 [768], P('fsdp'), may hold values from -1.75 to 1.75
- scale_attn: bfloat16 [768], P('fsdp'), may hold values from 0.099609375 to 1.8984375
- ln2_gain: bfloat16 [768], P('fsdp'), may hold values from 0.099609375 to 1.8984375
- ln2_bias: bfloat16 [768], P('fsdp'), may hold values from -1.75 to 1.75
- up_weight: bfloat16 [768, 3072], P('fsdp'), may hold values from -0.21875 to 0.21875
- up_bias: bfloat16 [3072], P('fsdp'), may hold values from -3 to 3
- down_weight: bfloat16 [3072, 768], P('fsdp'), may hold values from -0.109375 to 0.109375
- down_bias: bfloat16 [768], P('fsdp'), may hold values from -1.75 to 1.75
- scale_mlp: bfloat16 [768], P('fsdp'), may hold values from 0.099609375 to 1.8984375
- cotangent: bfloat16 [2, 4, 256, 8, 768], P(None, 'fsdp', None, 'seq'), may hold values from -6 to 6
Outputs:
- output: bfloat16 [2, 4, 256, 8, 768], P(None, 'fsdp', None, 'seq')
- input_grad: bfloat16 [2, 4, 256, 8, 768], P(None, 'fsdp', None, 'seq')
- ln1_gain_grad: float32 [768], P('fsdp')
- ln1_bias_grad: float32 [768], P('fsdp')
- qkv_weight_grad: float32 [768, 2304], P('fsdp')
- query_bias_grad: float32 [768], P('fsdp')
- value_bias_grad: float32 [768], P('fsdp')
- out_weight_grad: float32 [768, 768], P('fsdp')
- out_bias_grad: float32 [768], P('fsdp')
- scale_attn_grad: float32 [768], P('fsdp')
- ln2_gain_grad: float32 [768], P('fsdp')
- ln2_bias_grad: float32 [768], P('fsdp')
- up_weight_grad: float32 [768, 3072], P('fsdp')
- up_bias_grad: float32 [3072], P('fsdp')
- down_weight_grad: float32 [3072, 768], P('fsdp')
- down_bias_grad: float32 [768], P('fsdp')
- scale_mlp_grad: float32 [768], P('fsdp')
Inputs may be any that keep to these rules, and one draw needn't show every extreme that they name: `image_tokens`: in every micro-batch and image group exactly one slot, drawn at random, holds one image of 1029 tokens and nothing else; each other slot holds 2 to 3 images of 261 tokens. A row's nonzero counts come first. So a slot has at most 1029 places, and one has exactly that.
All inputs are finite; a program needn't handle non-finite values.
Results may differ from a plain program's by a relative error of at most 0.014.
Values may be sent and summed in bfloat16 or wider, within the bound.
No kernel may reach another device: no remote copies, remote signals or barrier semaphores. Data moves between devices by JAX's collectives and lax.ppermute only.
A program may use at most 192 MiB of HBM per device.

v0:
```python
from functools import partial

import jax
import jax.numpy as jnp
from jax import lax
from jax.sharding import PartitionSpec as P

HEADS = 12
HGROUPS = 4
LONG = 1029


EPSILON = 1e-06
MASK_VALUE = -1e30


def norm_rows(values, gain, shift):
    center = values - jnp.mean(values, axis=-1, keepdims=True)
    spread = jnp.mean(center * center, axis=-1, keepdims=True)
    return center * lax.rsqrt(spread + EPSILON) * gain + shift


def slot_tables(counts):
    slot_sizes = jnp.sum(counts, axis=1)
    slot_starts = jnp.cumsum(slot_sizes) - slot_sizes
    image_ends = jnp.cumsum(counts.reshape(-1))
    return (slot_sizes, slot_starts, image_ends)


def image_of(positions, image_ends):
    return jnp.sum((image_ends[None, :] <= positions[:, None]).astype(jnp.int32), axis=1)


def inner_rows(left, right):
    return lax.dot_general(
        left, right, (((0,), (0,)), ((), ())), preferred_element_type=jnp.float32
    )


def outer_cols(left, right):
    return lax.dot_general(
        left, right, (((1,), (1,)), ((), ())), preferred_element_type=jnp.float32
    )


def masked_scores(queries, key_rows, segment, score_scale):
    scores = outer_cols(queries, key_rows) * score_scale
    same_image = segment[:, None] == segment[None, :]
    return jnp.where(same_image, scores, MASK_VALUE)


def attend_forward(queries, key_rows, value_rows, segment, score_scale):
    scores = masked_scores(queries, key_rows, segment, score_scale)
    row_peak = jnp.max(scores, axis=1, keepdims=True)
    exponent = jnp.exp(scores - row_peak)
    row_total = jnp.sum(exponent, axis=1, keepdims=True)
    weights = (exponent / row_total).astype(jnp.bfloat16)
    result = jnp.dot(weights, value_rows, preferred_element_type=jnp.float32)
    return (result.astype(jnp.bfloat16), (row_peak + jnp.log(row_total))[:, 0])


def attend_backward(queries, key_rows, value_rows, out_grad, logsum, segment, score_scale):
    scores = masked_scores(queries, key_rows, segment, score_scale)
    probability = jnp.exp(scores - logsum[:, None])
    value_grad = inner_rows(probability.astype(jnp.bfloat16), out_grad)
    prob_grad = outer_cols(out_grad, value_rows)
    row_dot = jnp.sum(probability * prob_grad, axis=1, keepdims=True)
    score_grad = (probability * (prob_grad - row_dot)).astype(jnp.bfloat16)
    query_grad = jnp.dot(score_grad, key_rows, preferred_element_type=jnp.float32) * score_scale
    key_grad = inner_rows(score_grad, queries) * score_scale
    return (query_grad, key_grad, value_grad)


def body(
    tokens,
    image_tokens,
    ln1_gain,
    ln1_bias,
    qkv_weight,
    query_bias,
    value_bias,
    out_weight,
    out_bias,
    scale_attn,
    ln2_gain,
    ln2_bias,
    up_weight,
    up_bias,
    down_weight,
    down_bias,
    scale_mlp,
    cotangent,
):
    seq_count = lax.axis_size("seq")
    seq_index = lax.axis_index("seq")
    slot_count = seq_count // HGROUPS
    capacity = (LONG + seq_count - 1) // seq_count
    model_width = tokens.shape[-1]
    local_heads = HEADS // HGROUPS
    head_width = model_width // HEADS
    score_scale = head_width ** (-0.5)
    tok_count = tokens.shape[2]
    own_slot = seq_index % slot_count
    cap_steps = jnp.arange(capacity, dtype=jnp.int32)
    sources = jnp.arange(seq_count, dtype=jnp.int32)
    grad_sums = None
    outputs_list = []
    grads_list = []
    for micro_step in range(tokens.shape[0]):
        current = (
            lax.all_gather(ln1_gain, "fsdp", axis=0, tiled=True),
            lax.all_gather(ln1_bias, "fsdp", axis=0, tiled=True),
            lax.all_gather(qkv_weight, "fsdp", axis=0, tiled=True),
            lax.all_gather(query_bias, "fsdp", axis=0, tiled=True),
            lax.all_gather(value_bias, "fsdp", axis=0, tiled=True),
            lax.all_gather(out_weight, "fsdp", axis=0, tiled=True),
            lax.all_gather(out_bias, "fsdp", axis=0, tiled=True),
            lax.all_gather(scale_attn, "fsdp", axis=0, tiled=True),
            lax.all_gather(ln2_gain, "fsdp", axis=0, tiled=True),
            lax.all_gather(ln2_bias, "fsdp", axis=0, tiled=True),
            lax.all_gather(up_weight, "fsdp", axis=0, tiled=True),
            lax.all_gather(up_bias, "fsdp", axis=0, tiled=True),
            lax.all_gather(down_weight, "fsdp", axis=0, tiled=True),
            lax.all_gather(down_bias, "fsdp", axis=0, tiled=True),
            lax.all_gather(scale_mlp, "fsdp", axis=0, tiled=True),
        )
        (
            norm1_gain,
            norm1_bias,
            qkv_matrix,
            query_shift,
            value_shift,
            out_matrix,
            out_shift,
            attn_scale,
            norm2_gain,
            norm2_bias,
            up_matrix,
            up_shift,
            down_matrix,
            down_shift,
            mlp_scale,
        ) = current
        attn_scale = attn_scale.astype(jnp.float32)
        mlp_scale = mlp_scale.astype(jnp.float32)
        counts = image_tokens[micro_step, 0]
        slot_sizes, slot_starts, image_ends = slot_tables(counts)
        first_rows = (slot_starts - seq_index + seq_count - 1) // seq_count
        end_rows = (slot_starts + slot_sizes - seq_index + seq_count - 1) // seq_count
        send_rows = jnp.where(
            cap_steps[None, :] < (end_rows - first_rows)[:, None],
            first_rows[:, None] + cap_steps[None, :],
            tok_count,
        ).reshape(-1)
        my_start = slot_starts[own_slot]
        my_size = slot_sizes[own_slot]
        src_first = (my_start - sources + seq_count - 1) // seq_count
        src_end = (my_start + my_size - sources + seq_count - 1) // seq_count
        positions = (
            (src_first[:, None] + cap_steps[None, :]) * seq_count + sources[:, None]
        ).reshape(-1)
        is_valid = (cap_steps[None, :] < (src_end - src_first)[:, None]).reshape(-1)
        segment = jnp.where(is_valid, image_of(positions, image_ends), -1)
        inputs = tokens[micro_step, 0, :, 0, :].astype(jnp.float32)
        normed_first, norm1_back = jax.vjp(
            norm_rows, inputs, norm1_gain.astype(jnp.float32), norm1_bias.astype(jnp.float32)
        )
        normed_first = normed_first.astype(jnp.bfloat16)
        shifts = jnp.concatenate([query_shift, jnp.zeros_like(query_shift), value_shift]).astype(
            jnp.float32
        )
        projected = (
            jnp.dot(normed_first, qkv_matrix, preferred_element_type=jnp.float32) + shifts
        ).astype(jnp.bfloat16)
        padded = jnp.concatenate([projected, jnp.zeros((1, 3 * model_width), jnp.bfloat16)], axis=0)
        outgoing = padded[send_rows].reshape(
            slot_count, capacity, 3, HGROUPS, local_heads, head_width
        )
        outgoing = jnp.transpose(outgoing, (3, 0, 1, 2, 4, 5)).reshape(
            seq_count, capacity * 3 * local_heads * head_width
        )
        arrived = lax.all_to_all(outgoing, "seq", split_axis=0, concat_axis=0, tiled=True)
        arrived = arrived.reshape(seq_count * capacity, 3, local_heads, head_width)
        per_head = jnp.transpose(arrived, (1, 2, 0, 3))

        def forward_head(members):
            return attend_forward(members[0], members[1], members[2], segment, score_scale)

        head_out, logsum = lax.map(forward_head, (per_head[0], per_head[1], per_head[2]))
        leaving = jnp.transpose(head_out, (1, 0, 2)).reshape(
            seq_count, capacity * local_heads * head_width
        )
        returned = lax.all_to_all(leaving, "seq", split_axis=0, concat_axis=0, tiled=True)
        returned = returned.reshape(HGROUPS, slot_count, capacity, local_heads, head_width)
        returned = jnp.transpose(returned, (1, 2, 0, 3, 4)).reshape(
            slot_count * capacity, model_width
        )
        attended = (
            jnp.zeros((tok_count + 1, model_width), jnp.bfloat16)
            .at[send_rows]
            .set(returned)[:tok_count]
        )
        branch = jnp.dot(
            attended, out_matrix, preferred_element_type=jnp.float32
        ) + out_shift.astype(jnp.float32)
        middle = inputs + attn_scale * branch
        normed_second, norm2_back = jax.vjp(
            norm_rows, middle, norm2_gain.astype(jnp.float32), norm2_bias.astype(jnp.float32)
        )
        normed_second = normed_second.astype(jnp.bfloat16)
        hidden = jnp.dot(
            normed_second, up_matrix, preferred_element_type=jnp.float32
        ) + up_shift.astype(jnp.float32)
        active, gelu_back = jax.vjp(partial(jax.nn.gelu, approximate=False), hidden)
        active = active.astype(jnp.bfloat16)
        branch_two = jnp.dot(
            active, down_matrix, preferred_element_type=jnp.float32
        ) + down_shift.astype(jnp.float32)
        outputs_list.append((middle + mlp_scale * branch_two).astype(jnp.bfloat16))
        upstream = cotangent[micro_step, 0, :, 0, :].astype(jnp.float32)
        scale2_grad = jnp.sum(upstream * branch_two, axis=0)
        branch_two_grad = (mlp_scale * upstream).astype(jnp.bfloat16)
        down_shift_grad = jnp.sum(branch_two_grad.astype(jnp.float32), axis=0)
        down_grad = inner_rows(active, branch_two_grad)
        active_grad = outer_cols(branch_two_grad, down_matrix)
        hidden_grad = gelu_back(active_grad)[0].astype(jnp.bfloat16)
        up_shift_grad = jnp.sum(hidden_grad.astype(jnp.float32), axis=0)
        up_grad = inner_rows(normed_second, hidden_grad)
        normed_second_grad = outer_cols(hidden_grad, up_matrix)
        middle_norm_grad, norm2_gain_grad, norm2_bias_grad = norm2_back(normed_second_grad)
        middle_grad = upstream + middle_norm_grad
        scale1_grad = jnp.sum(middle_grad * branch, axis=0)
        branch_grad = (attn_scale * middle_grad).astype(jnp.bfloat16)
        out_shift_grad = jnp.sum(branch_grad.astype(jnp.float32), axis=0)
        out_matrix_grad = inner_rows(attended, branch_grad)
        attended_grad = outer_cols(branch_grad, out_matrix).astype(jnp.bfloat16)
        padded_grad = jnp.concatenate(
            [attended_grad, jnp.zeros((1, model_width), jnp.bfloat16)], axis=0
        )
        outgoing_grad = padded_grad[send_rows].reshape(
            slot_count, capacity, HGROUPS, local_heads, head_width
        )
        outgoing_grad = jnp.transpose(outgoing_grad, (2, 0, 1, 3, 4)).reshape(
            seq_count, capacity * local_heads * head_width
        )
        arrived_grad = lax.all_to_all(outgoing_grad, "seq", split_axis=0, concat_axis=0, tiled=True)
        arrived_grad = jnp.transpose(
            arrived_grad.reshape(seq_count * capacity, local_heads, head_width), (1, 0, 2)
        )

        def backward_head(members):
            return attend_backward(
                members[0], members[1], members[2], members[3], members[4], segment, score_scale
            )

        query_grads, key_grads, value_grads = lax.map(
            backward_head, (per_head[0], per_head[1], per_head[2], arrived_grad, logsum)
        )
        stacked = jnp.stack([query_grads, key_grads, value_grads]).astype(jnp.bfloat16)
        stacked = jnp.transpose(stacked, (2, 0, 1, 3)).reshape(
            seq_count, capacity * 3 * local_heads * head_width
        )
        back_home = lax.all_to_all(stacked, "seq", split_axis=0, concat_axis=0, tiled=True)
        back_home = back_home.reshape(HGROUPS, slot_count, capacity, 3, local_heads, head_width)
        back_home = jnp.transpose(back_home, (1, 2, 3, 0, 4, 5)).reshape(
            slot_count * capacity, 3 * model_width
        )
        projected_grad = (
            jnp.zeros((tok_count + 1, 3 * model_width), jnp.bfloat16)
            .at[send_rows]
            .set(back_home)[:tok_count]
        )
        column_sums = jnp.sum(projected_grad.astype(jnp.float32), axis=0)
        qkv_grad = inner_rows(normed_first, projected_grad)
        normed_first_grad = outer_cols(projected_grad, qkv_matrix)
        input_norm_grad, norm1_gain_grad, norm1_bias_grad = norm1_back(normed_first_grad)
        grads_list.append((middle_grad + input_norm_grad).astype(jnp.bfloat16))
        micro_terms = (
            norm1_gain_grad,
            norm1_bias_grad,
            qkv_grad,
            column_sums[:model_width],
            column_sums[2 * model_width :],
            out_matrix_grad,
            out_shift_grad,
            scale1_grad,
            norm2_gain_grad,
            norm2_bias_grad,
            up_grad,
            up_shift_grad,
            down_grad,
            down_shift_grad,
            scale2_grad,
        )
        grad_sums = (
            micro_terms if grad_sums is None else jax.tree.map(jnp.add, grad_sums, micro_terms)
        )
    shards = (
        lax.psum_scatter(
            grad_sums[0].astype(jnp.bfloat16), "fsdp", scatter_dimension=0, tiled=True
        ).astype(jnp.float32),
        lax.psum_scatter(
            grad_sums[1].astype(jnp.bfloat16), "fsdp", scatter_dimension=0, tiled=True
        ).astype(jnp.float32),
        lax.psum_scatter(
            grad_sums[2].astype(jnp.bfloat16), "fsdp", scatter_dimension=0, tiled=True
        ).astype(jnp.float32),
        lax.psum_scatter(
            grad_sums[3].astype(jnp.bfloat16), "fsdp", scatter_dimension=0, tiled=True
        ).astype(jnp.float32),
        lax.psum_scatter(
            grad_sums[4].astype(jnp.bfloat16), "fsdp", scatter_dimension=0, tiled=True
        ).astype(jnp.float32),
        lax.psum_scatter(
            grad_sums[5].astype(jnp.bfloat16), "fsdp", scatter_dimension=0, tiled=True
        ).astype(jnp.float32),
        lax.psum_scatter(
            grad_sums[6].astype(jnp.bfloat16), "fsdp", scatter_dimension=0, tiled=True
        ).astype(jnp.float32),
        lax.psum_scatter(
            grad_sums[7].astype(jnp.bfloat16), "fsdp", scatter_dimension=0, tiled=True
        ).astype(jnp.float32),
        lax.psum_scatter(
            grad_sums[8].astype(jnp.bfloat16), "fsdp", scatter_dimension=0, tiled=True
        ).astype(jnp.float32),
        lax.psum_scatter(
            grad_sums[9].astype(jnp.bfloat16), "fsdp", scatter_dimension=0, tiled=True
        ).astype(jnp.float32),
        lax.psum_scatter(
            grad_sums[10].astype(jnp.bfloat16), "fsdp", scatter_dimension=0, tiled=True
        ).astype(jnp.float32),
        lax.psum_scatter(
            grad_sums[11].astype(jnp.bfloat16), "fsdp", scatter_dimension=0, tiled=True
        ).astype(jnp.float32),
        lax.psum_scatter(
            grad_sums[12].astype(jnp.bfloat16), "fsdp", scatter_dimension=0, tiled=True
        ).astype(jnp.float32),
        lax.psum_scatter(
            grad_sums[13].astype(jnp.bfloat16), "fsdp", scatter_dimension=0, tiled=True
        ).astype(jnp.float32),
        lax.psum_scatter(
            grad_sums[14].astype(jnp.bfloat16), "fsdp", scatter_dimension=0, tiled=True
        ).astype(jnp.float32),
    )
    totals = lax.psum(
        (
            shards[0],
            shards[1],
            shards[2],
            shards[3],
            shards[4],
            shards[5],
            shards[6],
            shards[7],
            shards[8],
            shards[9],
            shards[10],
            shards[11],
            shards[12],
            shards[13],
            shards[14],
        ),
        "seq",
    )
    output = jnp.stack(outputs_list)[:, None, :, None, :]
    input_grad = jnp.stack(grads_list)[:, None, :, None, :]
    return (
        output,
        input_grad,
        totals[0],
        totals[1],
        totals[2],
        totals[3],
        totals[4],
        totals[5],
        totals[6],
        totals[7],
        totals[8],
        totals[9],
        totals[10],
        totals[11],
        totals[12],
        totals[13],
        totals[14],
    )


def solution(mesh):
    return jax.shard_map(
        body,
        mesh=mesh,
        in_specs=(
            P(None, "fsdp", None, "seq", None),
            P(None, "fsdp", None, None),
            P("fsdp"),
            P("fsdp"),
            P("fsdp", None),
            P("fsdp"),
            P("fsdp"),
            P("fsdp", None),
            P("fsdp"),
            P("fsdp"),
            P("fsdp"),
            P("fsdp"),
            P("fsdp", None),
            P("fsdp"),
            P("fsdp", None),
            P("fsdp"),
            P("fsdp"),
            P(None, "fsdp", None, "seq", None),
        ),
        out_specs=(
            P(None, "fsdp", None, "seq", None),
            P(None, "fsdp", None, "seq", None),
            P("fsdp"),
            P("fsdp"),
            P("fsdp", None),
            P("fsdp"),
            P("fsdp"),
            P("fsdp", None),
            P("fsdp"),
            P("fsdp"),
            P("fsdp"),
            P("fsdp"),
            P("fsdp", None),
            P("fsdp"),
            P("fsdp", None),
            P("fsdp"),
            P("fsdp"),
        ),
        check_vma=False,
    )
```

profile of v0, /device:TPU:0, one launch (start us, length us, event | category | flops | bytes accessed | tf_op | source)
XLA Modules:
  0.0 805.8 jit_solution(17914054697233497106)
XLA Ops:
  21.2 18.2 %all-reduce.27 = (bf16[768]{0:T(1024)(128)(2,1)S(1)}, bf16[768]{0:T(1024)(128)(2,1)S(1)}, bf16[768]{0:T(1024)(128)(2,1)S(1)}, bf16[768]{0:T(1024)(128)(2,1)S(1)}...) all-reduce(bf16[768]{0:T(1024)(128)(2,1)S(1)} %dynamic-update-slice, ...), channel_id=1, replica_groups=mesh['fsdp'=4,'seq'=8] {'fsdp'}, use_global_device_ids=true, to_apply=%add.8 | all-reduce | flops 7680 | bytes 30720
  41.3 18.9 %all-gather.6.cloned.1.call-done = bf16[768,2304]{1,0:T(8,128)(2,1)} async-done(((bf16[192,2304]{1,0:T(8,128)(2,1)}), bf16[768,2304]{1,0:T(8,128)(2,1)}) %all-gather.6.cloned.1.call-update) | async-done | bytes 3538960 | tf_op jit(solution)/shard_map/all_gather | solution.py:113
  67.6 5.8 reshape.760
  73.4 6.4 copy.150
  79.9 6.8 all_to_all.64
  87.2 8.9 %reduce.22 = bf16[8,74304]{1,0:T(8,128)(2,1)} reduce(bf16[8,1,74304]{2,1,0:T(2,128)(2,1)S(1)} %all_to_all.64, bf16[]{:T(256)} %broadcast.1155), dimensions={1}, to_apply=%all_to_all.64.reduce_sub_computation | reduce | bytes 2377730 | tf_op jit(solution)/shard_map/all_to_all | solution.py:182
  99.7 5.0 all-to-all-start
  113.0 5.8 reshape.768
  118.8 6.4 copy.160
  125.2 6.6 all_to_all.66
  131.8 8.9 %reduce.20 = bf16[8,74304]{1,0:T(8,128)(2,1)} reduce(bf16[8,1,74304]{2,1,0:T(2,128)(2,1)S(1)} %all_to_all.66, bf16[]{:T(256)} %broadcast.1155), dimensions={1}, to_apply=%all_to_all.66.reduce_sub_computation | reduce | bytes 2377730 | tf_op jit(solution)/shard_map/all_to_all | solution.py:182
  144.3 5.1 all-to-all-start.2
  159.0 6.6 reshape.943
  165.5 8.2 %reduce.7 = bf16[8,74304]{1,0:T(8,128)(2,1)} reduce(bf16[8,1,74304]{2,1,0:T(2,128)(2,1)S(1)} %reshape.943, bf16[]{:T(256)} %constant.412), dimensions={1}, to_apply=%all_to_all.49.reduce_sub_computation | reduce | bytes 2377730 | tf_op jit(solution)/shard_map/all_to_all | solution.py:182
  179.2 6.6 reshape.951
  185.7 8.2 %reduce.10 = bf16[8,74304]{1,0:T(8,128)(2,1)} reduce(bf16[8,1,74304]{2,1,0:T(2,128)(2,1)S(1)} %reshape.951, bf16[]{:T(256)} %constant.412), dimensions={1}, to_apply=%all_to_all.53.reduce_sub_computation | reduce | bytes 2377730 | tf_op jit(solution)/shard_map/all_to_all | solution.py:182
  203.3 10.6 %while.53 = (s32[]{:T(128)}, bf16[3,1032,64]{1,2,0:T(8,128)(2,1)}, f32[3,1032]{1,0:T(4,128)S(1)}, s32[1032]{0:T(1024)S(1)}, bf16[3,1032,64]{2,1,0:T(8,128)(2,1)S...) while((s32[]{:T(128)}, bf16[3,1032,64]{1,2,0:T(8,128)(2,1)}, ...), condition=%wide.region_22.23_spmd, body=%wide.region_19.22_spmd.sunk | while | flops 282296384 | bytes 14291881 | solution.py:189
  220.3 4.8 reduce.21
  227.1 4.1 all-to-all-start.3
  231.2 6.6 reshape.761
  241.6 10.2 %while.52 = (s32[]{:T(128)}, bf16[3,1032,64]{1,2,0:T(8,128)(2,1)}, f32[3,1032]{1,0:T(4,128)S(1)}, s32[1032]{0:T(1024)S(1)}, bf16[3,1032,64]{2,1,0:T(8,128)(2,1)S...) while((s32[]{:T(128)}, bf16[3,1032,64]{1,2,0:T(8,128)(2,1)}, ...), condition=%wide.region_9.10_spmd, body=%wide.region_6.9_spmd.sunk | while | flops 282296384 | bytes 14291881 | solution.py:189
  258.2 4.8 reduce.23
  265.0 5.0 all-to-all-start.1
  271.3 8.1 %all-gather = bf16[4,1,768]{2,1,0:T(2,128)(2,1)S(1)} all-gather(bf16[1,1,768]{2,1,0:T(2,128)(2,1)S(1)} %reshape.876), channel_id=1, replica_groups=mesh['fsdp'=4,'seq'=8] {'fsdp'}, dimensions={0}, use_global_device_ids=true | all-gather | bytes 7680 | tf_op jit(solution)/shard_map/all_gather | solution.py:122
  308.6 11.6 %multiply_convert_fusion.3 = (bf16[256,3072]{1,0:T(8,128)(2,1)}, f32[256,3072]{1,0:T(8,128)}, f32[256,3072]{1,0:T(8,128)}) fusion(f32[3072]{0:T(1024)} %bitcast.435, bf16[768,3072]{1,0:T(8,128)(2,1)} %all-gather.10.cloned.1.call-done, f32[256,768]{1,0:T(8,128)S(1)} %get-tuple-element.577, f32[768]{0:T(1024)S(1)} %convert_element_type.286, ...), kind=kOutput, calls=%fused_computation.148 | convolution fusion | flops 1260847104 | bytes 13389824 | tf_op jit(solution)/shard_map/dot_general | solution.py:211
  320.2 7.0 convert_reduce_fusion.1
  329.9 8.1 %multiply_convert_fusion.2 = (bf16[256,3072]{1,0:T(8,128)(2,1)S(1)}, f32[256,3072]{1,0:T(8,128)S(1)}, f32[256,3072]{1,0:T(8,128)S(1)}) fusion(f32[3072]{0:T(1024)S(1)} %bitcast.436, bf16[768,3072]{1,0:T(8,128)(2,1)S(1)} %copy-done.104, f32[256,768]{1,0:T(8,128)S(1)} %get-tuple-element.611, f32[256]{0:T(256)S(1)} %copy-done.82, f32[256]{0:T(256)S(1)} %copy-done.63, ...), kind=kOutput, calls=%fused_computation.135 | convolution fusion | flops 1260847104 | bytes 13389824 | tf_op jit(solution)/shard_map/dot_general | solution.py:211
  372.2 5.1 all-to-all-start.6
  415.8 26.0 %while.55 = (s32[]{:T(128)}, bf16[3,1032,64]{1,2,0:T(8,128)(2,1)}, bf16[3,1032,64]{1,2,0:T(8,128)(2,1)}, bf16[3,1032,64]{1,2,0:T(8,128)(2,1)}, s32[1032]{0:T(102...) while((s32[]{:T(128)}, bf16[3,1032,64]{1,2,0:T(8,128)(2,1)}, ...), condition=%wide.region_38.39_spmd, body=%wide.region_36.38_spmd.sunk | while | flops 692396672 | bytes 45728288 | solution.py:256
  443.3 4.1 copy.187
  447.4 6.7 all_to_all.71
  454.1 9.2 %reduce.25 = bf16[8,74304]{1,0:T(8,128)(2,1)} reduce(bf16[8,1,74304]{2,1,0:T(2,128)(2,1)S(1)} %all_to_all.71, bf16[]{:T(256)} %broadcast.1155), dimensions={1}, to_apply=%all_to_all.71.reduce_sub_computation | reduce | bytes 2377730 | tf_op jit(solution)/shard_map/all_to_all | solution.py:263
  467.1 4.3 all-to-all-start.7
  472.2 22.7 %while.54 = (s32[]{:T(128)}, bf16[3,1032,64]{1,2,0:T(8,128)(2,1)S(1)}, bf16[3,1032,64]{1,2,0:T(8,128)(2,1)S(1)}, bf16[3,1032,64]{1,2,0:T(8,128)(2,1)}, s32[1032]...) while((s32[]{:T(128)}, ...), condition=%wide.region_30.31_spmd, body=%wide.region_28.30_spmd.sunk | while | flops 692396672 | bytes 39387568 | solution.py:256
  497.2 5.1 copy.176
  502.4 5.6 all_to_all.69
  508.0 8.9 %reduce.27 = bf16[8,74304]{1,0:T(8,128)(2,1)S(1)} reduce(bf16[8,1,74304]{2,1,0:T(2,128)(2,1)} %all_to_all.69, bf16[]{:T(256)} %broadcast.1155), dimensions={1}, to_apply=%all_to_all.69.reduce_sub_computation | reduce | bytes 2377730 | tf_op jit(solution)/shard_map/all_to_all | solution.py:263
  519.2 5.0 all-to-all-start.5
  524.2 6.7 reshape.957
  530.9 8.2 %reduce.15 = bf16[8,74304]{1,0:T(8,128)(2,1)} reduce(bf16[8,1,74304]{2,1,0:T(2,128)(2,1)S(1)} %reshape.957, bf16[]{:T(256)} %constant.412), dimensions={1}, to_apply=%all_to_all.63.reduce_sub_computation | reduce | bytes 2377730 | tf_op jit(solution)/shard_map/all_to_all | solution.py:263
  542.6 11.4 %all-to-all-done.5 = bf16[8,2,37152]{2,1,0:T(2,128)(2,1)} async-done(((bf16[8,2,37152]{2,1,0:T(2,128)(2,1)}), bf16[8,2,37152]{2,1,0:T(2,128)(2,1)}, u32[]{:S(2)}, u32[]{:S(2)}) %all-to-all-start.5) | async-done | bytes 1188896 | tf_op jit(solution)/shard_map/all_to_all | solution.py:263
  553.9 6.5 reshape.949
  560.4 8.2 %reduce.13 = bf16[8,74304]{1,0:T(8,128)(2,1)} reduce(bf16[8,1,74304]{2,1,0:T(2,128)(2,1)S(1)} %reshape.949, bf16[]{:T(256)} %constant.412), dimensions={1}, to_apply=%all_to_all.59.reduce_sub_computation | reduce | bytes 2377730 | tf_op jit(solution)/shard_map/all_to_all | solution.py:263
  580.8 5.4 reshape.778
  588.9 6.5 reshape.902
  616.8 16.1 %all-reduce.26 = (bf16[768]{0:T(1024)(128)(2,1)S(1)}, bf16[768]{0:T(1024)(128)(2,1)S(1)}, bf16[768]{0:T(1024)(128)(2,1)S(1)}, bf16[768]{0:T(1024)(128)(2,1)S(1)}...) all-reduce(bf16[768]{0:T(1024)(128)(2,1)S(1)} %add_convert_fusion.2, ...), channel_id=2, replica_groups=mesh['fsdp'=4,'seq'=8] {'fsdp'}, use_global_device_ids=true, to_apply=%region_44.45.clone | all-reduce | flops 10752 | bytes 43008
  637.3 15.9 %reduce-scatter.5.cloned.1.call-done = bf16[192,2304]{1,0:T(8,128)(2,1)} async-done(((bf16[768,2304]{1,0:T(8,128)(2,1)}), bf16[192,2304]{1,0:T(8,128)(2,1)}) %reduce-scatter.5.cloned.1.call-update) | async-done | bytes 884752 | tf_op jit(solution)/shard_map/reduce_scatter | solution.py:305
  653.2 145.4 %all-reduce.29 = (f32[192]{0:T(256)}, f32[192]{0:T(256)}, f32[192,2304]{1,0:T(8,128)}, f32[192]{0:T(256)}, f32[192]{0:T(256)}, /*index=5*/f32[192,768]{1,0:T(8,1...) all-reduce(f32[192]{0:T(256)S(1)} %dynamic-slice_convert_fusion.10,, ...), channel_id=1, replica_groups=mesh['fsdp'=4,'seq'=8] {'seq'}, use_global_device_ids=true, to_apply=%region_45.46 | all-reduce | flops 1772160 | bytes 10638336 | tf_op jit(solution)/shard_map/psum | solution.py:345
  (578 shorter events, 307.1 us)
Async XLA Ops:
  7.2 33.7 %copy-start = (bf16[2,1,256,1,768]{4,2,3,1,0:T(8,128)(2,1)S(1)}, bf16[2,1,256,1,768]{4,2,3,1,0:T(8,128)(2,1)}, u32[]{:S(2)}) copy-start(bf16[2,1,256,1,768]{4,2,3,1,0:T(8,128)(2,1)} %param.26) | copy-start | bytes 2359300
  7.2 53.0 %all-gather.6.cloned.1.call-start = ((), (), s32[]{:S(2)}) async-start(), calls=%async_computation.12 | async-start | bytes 4423680 | tf_op jit(solution)/shard_map/all_gather | solution.py:113
  7.9 294.0 %all-gather.8.cloned.1.call-start = ((), (), s32[]{:S(2)}) async-start(), calls=%async_computation.13 | async-start | bytes 1474560 | tf_op jit(solution)/shard_map/all_gather | solution.py:116
  8.7 299.9 %all-gather.10.cloned.1.call-start = ((), (), s32[]{:S(2)}) async-start(), calls=%async_computation.14 | async-start | bytes 5898240 | tf_op jit(solution)/shard_map/all_gather | solution.py:121
  39.4 65.6 %copy-start.47 = (f32[768]{0:T(1024)}, f32[768]{0:T(1024)S(1)}, u32[]{:S(2)}) copy-start(f32[768]{0:T(1024)S(1)} %convert_element_type.278) | copy-start | bytes 9220
  39.4 65.6 %copy-start.49 = (f32[768]{0:T(1024)}, f32[768]{0:T(1024)S(1)}, u32[]{:S(2)}) copy-start(f32[768]{0:T(1024)S(1)} %convert_element_type.279) | copy-start | bytes 9220
  39.5 259.7 %copy-start.84 = (s32[258]{0:T(512)}, s32[258]{0:T(512)S(1)}, u32[]{:S(2)}) copy-start(s32[258]{0:T(512)S(1)} %fusion.179) | copy-start | bytes 3100
  39.5 24.0 %copy-start.65 = (s32[1024]{0:T(1024)}, s32[1024]{0:T(1024)S(1)}, u32[]{:S(2)}) copy-start(s32[1024]{0:T(1024)S(1)} %pad_clamp_fusion.1) | copy-start | bytes 12292
  40.8 19.3 %copy-start.53 = (f32[256]{0:T(256)}, f32[256]{0:T(256)S(1)}, u32[]{:S(2)}) copy-start(f32[256]{0:T(256)S(1)} %get-tuple-element.636) | copy-start | bytes 3076
  40.8 64.2 %copy-start.57 = (f32[256]{0:T(256)}, f32[256]{0:T(256)S(1)}, u32[]{:S(2)}) copy-start(f32[256]{0:T(256)S(1)} %get-tuple-element.635) | copy-start | bytes 3076
  41.2 18.9 %copy-start.76 = (f32[256]{0:T(256)}, f32[256]{0:T(256)S(1)}, u32[]{:S(2)}) copy-start(f32[256]{0:T(256)S(1)} %get-tuple-element.456) | copy-start | bytes 3076
  41.2 63.7 %copy-start.74 = (f32[256]{0:T(256)}, f32[256]{0:T(256)S(1)}, u32[]{:S(2)}) copy-start(f32[256]{0:T(256)S(1)} %get-tuple-element.457) | copy-start | bytes 3076
  41.3 18.9 %copy-start.55 = (f32[256]{0:T(256)}, f32[256]{0:T(256)S(1)}, u32[]{:S(2)}) copy-start(f32[256]{0:T(256)S(1)} %fusion.181) | copy-start | bytes 3076
  99.7 44.6 %all-to-all-start = ((bf16[8,2,37152]{2,1,0:T(2,128)(2,1)}), bf16[8,2,37152]{2,1,0:T(2,128)(2,1)}, u32[]{:S(2)}, u32[]{:S(2)}) async-start(bf16[8,2,37152]{2,1,0:T(2,128)(2,1)} %reshape.942), calls=%async_computation | async-start | bytes 2383872 | tf_op jit(solution)/shard_map/all_to_all | solution.py:182
  104.9 192.5 %copy-start.85 = (s32[258]{0:T(512)}, s32[258]{0:T(512)S(1)}, u32[]{:S(2)}) copy-start(s32[258]{0:T(512)S(1)} %fusion.180) | copy-start | bytes 3100
  144.3 34.9 %all-to-all-start.2 = ((bf16[8,2,37152]{2,1,0:T(2,128)(2,1)}), bf16[8,2,37152]{2,1,0:T(2,128)(2,1)}, u32[]{:S(2)}, u32[]{:S(2)}) async-start(bf16[8,2,37152]{2,1,0:T(2,128)(2,1)} %reshape.950), calls=%async_computation.2 | async-start | bytes 2383872 | tf_op jit(solution)/shard_map/all_to_all | solution.py:182
  149.4 170.8 %all-gather.12.cloned.1.call-start = ((), (), s32[]{:S(2)}) async-start(), calls=%async_computation.15 | async-start | bytes 5898240 | tf_op jit(solution)/shard_map/all_gather | solution.py:123
  214.0 23.9 %copy-start.7 = (bf16[3,1032,64]{2,1,0:T(8,128)(2,1)}, bf16[3,1032,64]{2,1,0:T(8,128)(2,1)S(1)}, u32[]{:S(2)}) copy-start(bf16[3,1032,64]{2,1,0:T(8,128)(2,1)S(1)} %get-tuple-element.996) | copy-start | bytes 1188868
  214.0 23.9 %copy-start.9 = (bf16[3,1032,64]{2,1,0:T(8,128)(2,1)}, bf16[3,1032,64]{2,1,0:T(8,128)(2,1)S(1)}, u32[]{:S(2)}) copy-start(bf16[3,1032,64]{2,1,0:T(8,128)(2,1)S(1)} %get-tuple-element.997) | copy-start | bytes 1188868
  214.0 23.9 %copy-start.12 = (bf16[3,1032,64]{2,1,0:T(8,128)(2,1)}, bf16[3,1032,64]{2,1,0:T(8,128)(2,1)S(1)}, u32[]{:S(2)}) copy-start(bf16[3,1032,64]{2,1,0:T(8,128)(2,1)S(1)} %get-tuple-element.1001) | copy-start | bytes 1188868
  214.0 23.8 %copy-start.43 = (s32[1032]{0:T(1024)}, s32[1032]{0:T(1024)S(1)}, u32[]{:S(2)}) copy-start(s32[1032]{0:T(1024)S(1)} %get-tuple-element.1019) | copy-start | bytes 12388
  214.0 23.8 %copy-start.51 = (f32[3,1032]{1,0:T(4,128)}, f32[3,1032]{1,0:T(4,128)S(1)}, u32[]{:S(2)}) copy-start(f32[3,1032]{1,0:T(4,128)S(1)} %get-tuple-element.922) | copy-start | bytes 37156
  227.1 37.8 %all-to-all-start.3 = ((bf16[8,2,12384]{2,1,0:T(2,128)(2,1)}), bf16[8,2,12384]{2,1,0:T(2,128)(2,1)}, u32[]{:S(2)}, u32[]{:S(2)}) async-start(bf16[8,2,12384]{2,1,0:T(2,128)(2,1)} %reshape.952), calls=%async_computation.3 | async-start | bytes 794624 | tf_op jit(solution)/shard_map/all_to_all | solution.py:193
  251.8 31.9 %copy-start.3 = (bf16[3,1032,64]{2,1,0:T(8,128)(2,1)}, bf16[3,1032,64]{2,1,0:T(8,128)(2,1)S(1)}, u32[]{:S(2)}) copy-start(bf16[3,1032,64]{2,1,0:T(8,128)(2,1)S(1)} %get-tuple-element.994) | copy-start | bytes 1188868
  251.8 31.9 %copy-start.5 = (bf16[3,1032,64]{2,1,0:T(8,128)(2,1)}, bf16[3,1032,64]{2,1,0:T(8,128)(2,1)S(1)}, u32[]{:S(2)}) copy-start(bf16[3,1032,64]{2,1,0:T(8,128)(2,1)S(1)} %get-tuple-element.995) | copy-start | bytes 1188868
  251.8 31.9 %copy-start.11 = (bf16[3,1032,64]{2,1,0:T(8,128)(2,1)}, bf16[3,1032,64]{2,1,0:T(8,128)(2,1)S(1)}, u32[]{:S(2)}) copy-start(bf16[3,1032,64]{2,1,0:T(8,128)(2,1)S(1)} %get-tuple-element.1000) | copy-start | bytes 1188868
  251.8 31.9 %copy-start.41 = (s32[1032]{0:T(1024)}, s32[1032]{0:T(1024)S(1)}, u32[]{:S(2)}) copy-start(s32[1032]{0:T(1024)S(1)} %get-tuple-element.1018) | copy-start | bytes 12388
  251.8 31.9 %copy-start.52 = (f32[3,1032]{1,0:T(4,128)}, f32[3,1032]{1,0:T(4,128)S(1)}, u32[]{:S(2)}) copy-start(f32[3,1032]{1,0:T(4,128)S(1)} %get-tuple-element.955) | copy-start | bytes 37156
  251.8 18.2 %copy-start.103 = (bf16[768]{0:T(1024)(128)(2,1)S(1)}, bf16[768]{0:T(1024)(128)(2,1)}, u32[]{:S(2)}) copy-start(bf16[768]{0:T(1024)(128)(2,1)} %param.39) | copy-start | bytes 4612
  265.0 25.5 %all-to-all-start.1 = ((bf16[8,2,12384]{2,1,0:T(2,128)(2,1)}), bf16[8,2,12384]{2,1,0:T(2,128)(2,1)}, u32[]{:S(2)}, u32[]{:S(2)}) async-start(bf16[8,2,12384]{2,1,0:T(2,128)(2,1)} %reshape.944), calls=%async_computation.1 | async-start | bytes 794624 | tf_op jit(solution)/shard_map/all_to_all | solution.py:193
  270.0 340.4 %reduce-scatter.7.cloned.1.call-start = ((), (), s32[]{:S(2)}) async-start(), calls=%async_computation.17 | async-start | bytes 1474560 | tf_op jit(solution)/shard_map/reduce_scatter | solution.py:314
  352.6 284.8 %reduce-scatter.9.cloned.1.call-start = ((), (), s32[]{:S(2)}) async-start(), calls=%async_computation.18 | async-start | bytes 5898240 | tf_op jit(solution)/shard_map/reduce_scatter | solution.py:329
  364.0 13.3 %copy-start.35 = (bf16[256,768]{1,0:T(8,128)(2,1)S(1)}, bf16[256,768]{1,0:T(8,128)(2,1)}, u32[]{:S(2)}) copy-start(bf16[256,768]{1,0:T(8,128)(2,1)} %copy-done.34) | copy-start | bytes 1179652
  372.2 17.7 %all-to-all-start.6 = ((bf16[8,2,12384]{2,1,0:T(2,128)(2,1)}), bf16[8,2,12384]{2,1,0:T(2,128)(2,1)S(1)}, u32[]{:S(2)}, u32[]{:S(2)}) async-start(bf16[8,2,12384]{2,1,0:T(2,128)(2,1)} %reshape.954), calls=%async_computation.6 | async-start | bytes 794624 | tf_op jit(solution)/shard_map/all_to_all | solution.py:246
  380.5 12.9 %copy-start.22 = (bf16[2,1,256,1,768]{4,2,3,1,0:T(8,128)(2,1)S(1)}, bf16[2,1,256,1,768]{4,2,3,1,0:T(8,128)(2,1)}, u32[]{:S(2)}) copy-start(bf16[2,1,256,1,768]{4,2,3,1,0:T(8,128)(2,1)} %param.43) | copy-start | bytes 2359300
  389.9 16.0 %all-to-all-start.4 = ((bf16[8,2,12384]{2,1,0:T(2,128)(2,1)}), bf16[8,2,12384]{2,1,0:T(2,128)(2,1)S(1)}, u32[]{:S(2)}, u32[]{:S(2)}) async-start(bf16[8,2,12384]{2,1,0:T(2,128)(2,1)} %reshape.946), calls=%async_computation.4 | async-start | bytes 794624 | tf_op jit(solution)/shard_map/all_to_all | solution.py:246
  393.4 243.9 %reduce-scatter.11.cloned.1.call-start = ((), (), s32[]{:S(2)}) async-start(), calls=%async_computation.19 | async-start | bytes 5898240 | tf_op jit(solution)/shard_map/reduce_scatter | solution.py:335
  467.1 52.1 %all-to-all-start.7 = ((bf16[8,2,37152]{2,1,0:T(2,128)(2,1)}), bf16[8,2,37152]{2,1,0:T(2,128)(2,1)}, u32[]{:S(2)}, u32[]{:S(2)}) async-start(bf16[8,2,37152]{2,1,0:T(2,128)(2,1)} %reshape.956), calls=%async_computation.7 | async-start | bytes 2383872 | tf_op jit(solution)/shard_map/all_to_all | solution.py:263
  519.2 34.8 %all-to-all-start.5 = ((bf16[8,2,37152]{2,1,0:T(2,128)(2,1)}), bf16[8,2,37152]{2,1,0:T(2,128)(2,1)}, u32[]{:S(2)}, u32[]{:S(2)}) async-start(bf16[8,2,37152]{2,1,0:T(2,128)(2,1)} %reshape.948), calls=%async_computation.5 | async-start | bytes 2383872 | tf_op jit(solution)/shard_map/all_to_all | solution.py:263
  524.2 129.0 %reduce-scatter.5.cloned.1.call-start = ((), (), s32[]{:S(2)}) async-start(), calls=%async_computation.16 | async-start | bytes 4423680 | tf_op jit(solution)/shard_map/reduce_scatter | solution.py:305
  588.9 13.5 %copy-start.1 = (bf16[2,1,256,1,768]{4,2,3,1,0:T(8,128)(2,1)S(1)}, bf16[2,1,256,1,768]{4,2,3,1,0:T(8,128)(2,1)}, u32[]{:S(2)}) copy-start(bf16[2,1,256,1,768]{4,2,3,1,0:T(8,128)(2,1)} %param.26) | copy-start | bytes 2359300
  588.9 13.5 %copy-start.48 = (f32[768]{0:T(1024)S(1)}, f32[768]{0:T(1024)}, u32[]{:S(2)}) copy-start(f32[768]{0:T(1024)} %copy-done.47) | copy-start | bytes 9220
  588.9 13.5 %copy-start.50 = (f32[768]{0:T(1024)S(1)}, f32[768]{0:T(1024)}, u32[]{:S(2)}) copy-start(f32[768]{0:T(1024)} %copy-done.49) | copy-start | bytes 9220
  588.9 13.5 %copy-start.54 = (f32[256]{0:T(256)S(1)}, f32[256]{0:T(256)}, u32[]{:S(2)}) copy-start(f32[256]{0:T(256)} %copy-done.53) | copy-start | bytes 3076
  588.9 13.5 %copy-start.56 = (f32[256]{0:T(256)S(1)}, f32[256]{0:T(256)}, u32[]{:S(2)}) copy-start(f32[256]{0:T(256)} %copy-done.55) | copy-start | bytes 3076
  614.5 19.2 %copy-start.87 = (f32[256]{0:T(256)S(1)}, f32[256]{0:T(256)}, u32[]{:S(2)}) copy-start(f32[256]{0:T(256)} %copy-done.86) | copy-start | bytes 3076
  614.5 19.1 %copy-start.89 = (f32[256]{0:T(256)S(1)}, f32[256]{0:T(256)}, u32[]{:S(2)}) copy-start(f32[256]{0:T(256)} %copy-done.88) | copy-start | bytes 3076
  633.7 19.5 %copy-start.46 = (bf16[192,768]{1,0:T(8,128)(2,1)S(1)}, bf16[192,768]{1,0:T(8,128)(2,1)}, u32[]{:S(2)}) copy-start(bf16[192,768]{1,0:T(8,128)(2,1)} %reduce-scatter.7.cloned.1.call-done) | copy-start | bytes 884740
  (92 other events, 257.9 us)
Sparse Core Ops, SparseCore 0:
  9.9 50.2 all-gather.5
  62.0 27.7 all-gather.7
  91.6 57.0 all-gather.9
  151.7 57.6 all-gather.11
  352.7 28.9 reduce-scatter.6
  384.5 57.0 reduce-scatter.8
  444.6 57.0 reduce-scatter.10
  607.1 46.0 reduce-scatter.4
where the time goes:
time: 817 us; the launch traced here: 806 us
  local copies, waits for them, and re-layouts  249 us (30%)
  blocking collectives  188 us (23%)
  other arithmetic  129 us (16%)
  matrix products  125 us (15%)
  waiting for transfers between devices  55.6 us (7%)
  starting transfers between devices  37.3 us (5%)
  between operations  21 us (3%)
    psum x1, blocking collectives, body(): lax.psum((shards[0], shards[1], shards[2], shards[3], shards[4], shards[5...  145 us
    unnamed x243, local copies, waits for them, and re-layouts  79.7 us
    dot_general x26, matrix products, outer_cols(): lax.dot_general(left, right, (((1,), (1,)), ((), ())), preferred_element_...  45.9 us
    all_to_all x4, other arithmetic, body(): lax.all_to_all(stacked, 'seq', split_axis=0, concat_axis=0, tiled=True)  34.7 us
    all_to_all x4, other arithmetic, body(): lax.all_to_all(outgoing, 'seq', split_axis=0, concat_axis=0, tiled=True)  34.3 us
    unnamed x2, blocking collectives  34.3 us
    dot_general x20, matrix products, inner_rows(): lax.dot_general(left, right, (((0,), (0,)), ((), ())), preferred_element_...  30 us
    dot_general x2, matrix products, body(): jnp.dot(normed_second, up_matrix, preferred_element_type=jnp.float32)  19.7 us
  transfers between devices with their start and end apart: 16, of which 6 were waited for; matrix products, arithmetic and copies ran while one was open for 53% of the time, Pallas kernels for 0%

commit v1 on v0

v1 whole, which is shorter than its diff:
```python
from functools import partial
from math import pi, sqrt

import jax
import jax.numpy as jnp
from jax import lax
from jax.experimental import pallas as pl
from jax.experimental.pallas import tpu as pltpu
from jax.sharding import PartitionSpec as P

LONG = 1029
EPSILON = 1e-06
MASK_VALUE = -1e30
PAD_SEGMENT = 127
LANES = 128
HEAD_WIDTH = 64
MIB = 2**20
BOTH = ("fsdp", "seq")
F32 = jnp.float32
BF16 = jnp.bfloat16
VMEM = pl.BlockSpec()
SMEM = pl.BlockSpec(memory_space=pltpu.SMEM)
ANY = pl.BlockSpec(memory_space=pl.ANY)

LN1_GAIN, LN1_BIAS, QUERY_BIAS, VALUE_BIAS, OUT_BIAS = 0, 1, 2, 3, 4
SCALE_ATTN, LN2_GAIN, LN2_BIAS, DOWN_BIAS, SCALE_MLP, UP_ROW = 5, 6, 7, 8, 9, 10


def ceil_to(value, step):
    return (value + step - 1) // step * step


def move(value, flips):
    fsdp_count, seq_count = lax.axis_size("fsdp"), lax.axis_size("seq")
    pairs = []
    for f in range(fsdp_count):
        for s in range(seq_count):
            fsdp_flip, chip_flip, core_flip = flips[s % 2]
            there = (f ^ fsdp_flip) * seq_count + (s ^ (2 * chip_flip + core_flip))
            pairs.append((f * seq_count + s, there))
    return lax.ppermute(value, BOTH, pairs)


def to_core(value):
    return move(value, [(0, 0, 1)] * 2)


def to_chip(value, flip, other_flip=None):
    return move(value, [(0, flip, 0), (0, flip if other_flip is None else other_flip, 0)])


def to_fsdp(value, flips):
    return move(value, [(flip, 0, 0) for flip in flips])


def wide(value):
    return value.astype(F32)


def dot(left, right):
    return jnp.dot(left, right, preferred_element_type=F32)


def rows_of(left, right):
    return lax.dot_general(left, right, (((0,), (0,)), ((), ())), preferred_element_type=F32)


def cols_of(left, right):
    return lax.dot_general(left, right, (((1,), (1,)), ((), ())), preferred_element_type=F32)


def shape(dims, dtype=BF16):
    return jax.ShapeDtypeStruct(dims, dtype)


def call(kernel, operands, outs, scratch=(), after=(), limit=62, aliases=None):
    count = len(operands)

    def run(*refs):
        kernel(*refs[:count], *refs[count + len(after) :])

    return pl.pallas_call(
        run,
        in_specs=[spec for _, spec in operands] + [ANY] * len(after),
        out_specs=[ANY if aliases else VMEM] * len(outs),
        out_shape=list(outs),
        scratch_shapes=list(scratch),
        input_output_aliases=aliases or {},
        compiler_params=pltpu.CompilerParams(vmem_limit_bytes=limit * MIB),
    )(*[array for array, _ in operands], *after)


def hold(arrays, after):
    results = call(
        lambda *refs: None,
        [(item, ANY) for item in arrays],
        [shape(item.shape, item.dtype) for item in arrays],
        after=after,
        aliases={i: i for i in range(len(arrays))},
    )
    return list(results)


def cut_kernel(begin, source, out):
    out[...] = source[begin : begin + out.shape[0], :]


def cut_rows(value, begin, count, after=()):
    out = shape((count, value.shape[1]))
    return call(partial(cut_kernel, begin), [(value, VMEM)], [out], after=after)[0]


def add_kernel(*refs):
    total = wide(refs[0][...])
    for ref in refs[1:-1]:
        total = total + wide(ref[...])
    refs[-1][...] = total.astype(BF16)


def add(items, after=()):
    return call(add_kernel, [(item, VMEM) for item in items], [shape(items[0].shape)], after=after)[0]


def places_of(counts_ref, slots, images, chip, source, tok_count, seq_count):
    micro, slot = chip // slots, chip % slots
    total = jnp.int32(0)
    ends, sizes = [], []
    for j in range(slots):
        size = jnp.int32(0)
        for i in range(images):
            size = size + counts_ref[micro, 0, j, i]
            ends.append(total + size)
        sizes.append(size)
        total = total + size
    free = seq_count * tok_count - total
    start, room_end = jnp.int32(0), jnp.int32(0)
    picked = [jnp.int32(0)] * 4
    for j in range(slots):
        room = LONG - sizes[j]
        span = (
            start,
            start + sizes[j],
            total + jnp.minimum(room_end, free),
            total + jnp.minimum(room_end + room, free),
        )
        picked = [jnp.where(slot == j, a, b) for a, b in zip(span, picked)]
        start, room_end = start + sizes[j], room_end + room
    first, last, more, stop = [(a - source + seq_count - 1) // seq_count for a in picked]
    return micro, first, last - first, more, stop - more, total, ends


def local_rows_of(step, first, count, more, extra):
    local = jnp.where(step < count, first + step, more + step - count)
    return local, step < count + extra


def prepare_kernel(sizes, groups, small_count, counts_ref, values, *refs):
    slots, images, chips, capacity, tok_count, seq_count = sizes
    shards, refs = refs[: sum(groups)], refs[sum(groups) :]
    smalls, refs = refs[:small_count], refs[small_count:]
    parts, halves, rest = refs[:chips], refs[chips : chips + len(groups)], refs[chips + len(groups) :]
    seq_index = lax.axis_index("seq")
    chip, core = seq_index // 2, seq_index % 2
    for flip in range(chips):
        micro, first, count, more, extra, _, _ = places_of(
            counts_ref, slots, images, chip ^ flip, seq_index, tok_count, seq_count
        )
        step = lax.broadcasted_iota(jnp.int32, (capacity, tok_count), 0)
        held = lax.broadcasted_iota(jnp.int32, (capacity, tok_count), 1)
        local, valid = local_rows_of(step, first, count, more, extra)
        pick = jnp.where(valid & (local == held), 1.0, 0.0).astype(BF16)
        start = pl.multiple_of(micro * tok_count, tok_count)
        parts[flip][...] = dot(pick, values[pl.ds(start, tok_count), :]).astype(BF16)
    if smalls:
        first_half, inserted = rest
        half = (halves[0].shape[0] - EXTRA_ROWS) // 2
        inserted[...] = jnp.zeros_like(inserted)
        for i, small in enumerate(smalls):
            length = small.shape[0]
            inserted[i : i + 1, :length] = small[...].astype(F32).reshape(1, length)
        halves[0][half : half + EXTRA_ROWS, : inserted.shape[1]] = inserted[...].astype(BF16)
    at = 0
    for count, out in zip(groups, halves):
        half = shards[at].shape[0] // 2
        for i in range(2):
            start = pl.multiple_of((core ^ i) * half, 16)
            row = i * (out.shape[0] - half)
            col = 0
            for shard in shards[at : at + count]:
                out[row : row + half, col : col + shard.shape[1]] = shard[pl.ds(start, half), :]
                col += shard.shape[1]
        at += count
    if smalls:
        first_half[...] = halves[0][: first_half.shape[0], :]
    else:
        marks_kernel(sizes, counts_ref, *rest)


def collect_kernel(sizes, counts_ref, *refs):
    slots, images, chips, capacity, tok_count, seq_count = sizes
    parts, out = refs[:chips], refs[chips]
    seq_index = lax.axis_index("seq")
    micros = chips // slots
    sums = [None] * micros
    for flip in range(chips):
        micro, first, count, more, extra, _, _ = places_of(
            counts_ref, slots, images, seq_index // 2 ^ flip, seq_index, tok_count, seq_count
        )
        step = lax.broadcasted_iota(jnp.int32, (tok_count, capacity), 1)
        held = lax.broadcasted_iota(jnp.int32, (tok_count, capacity), 0)
        local, valid = local_rows_of(step, first, count, more, extra)
        pick = jnp.where(valid & (local == held), 1.0, 0.0).astype(BF16)
        found = dot(pick, parts[flip][...])
        for m in range(micros):
            term = jnp.where(micro == m, found, 0.0)
            sums[m] = term if sums[m] is None else sums[m] + term
    for m in range(micros):
        out[m * tok_count : (m + 1) * tok_count, :] = sums[m].astype(BF16)


def marks_kernel(sizes, counts_ref, q_marks, k_marks, live_ref):
    slots, images, chips, capacity, tok_count, seq_count = sizes
    rows = chips * capacity
    seq_index = lax.axis_index("seq")
    chip, core = seq_index // 2, seq_index % 2
    row = lax.broadcasted_iota(jnp.int32, (rows, LANES), 0)
    lane = lax.broadcasted_iota(jnp.int32, (rows, LANES), 1)
    for which in range(2):
        segment = jnp.full((rows, LANES), PAD_SEGMENT, jnp.int32)
        live = jnp.zeros((rows, LANES), jnp.int32)
        for flip in range(chips):
            source = 2 * (chip ^ flip) + (core ^ which)
            _, first, count, more, extra, total, ends = places_of(
                counts_ref, slots, images, chip, source, tok_count, seq_count
            )
            step = row - flip * capacity
            local, valid = local_rows_of(step, first, count, more, extra)
            valid = valid & (step >= 0) & (step < capacity)
            place = local * seq_count + source
            image = jnp.zeros((rows, LANES), jnp.int32)
            for end in ends:
                image = image + (end <= place).astype(jnp.int32)
            segment = jnp.where(valid, image, segment)
            live = jnp.where(valid & (place < total), 1, live)
        same = segment == lane
        k_marks[which * rows : (which + 1) * rows, :] = jnp.where(same, 0.0, MASK_VALUE).astype(
            BF16
        )
        if which == 0:
            q_marks[...] = jnp.where(same, 1.0, 0.0).astype(BF16)
            live_ref[...] = live.astype(F32)


def stage(out, own, pieces, first_col, extra, sems):
    rows, cols = own.shape
    half = rows // 2
    mine, core = lax.axis_index("fsdp"), lax.axis_index("seq") % 2
    copies = []

    def put(source, flip, at):
        start = pl.multiple_of((mine ^ flip) * rows + at, 16)
        copy = pltpu.make_async_copy(
            source, out.at[pl.ds(start, source.shape[0])], sems.at[len(copies)]
        )
        copy.start()
        copies.append(copy)

    here = slice(first_col, first_col + cols)
    put(own, 0, 0)
    for i in range(2):
        home = core ^ i
        near, far = pieces[i], pieces[2 + i]
        put(near.at[:half, here], 1 + home, home * half)
        put(near.at[half + extra :, here], 1 + home, (1 - home) * half)
        put(far.at[:half, here], 3, home * half)
    return copies


def wait_all(copies):
    for copy in copies:
        copy.wait()


STAGE_SEMS = pltpu.SemaphoreType.DMA((7,))
EXTRA_ROWS = 16


def norm_parts(values):
    center = values - jnp.mean(values, axis=-1, keepdims=True)
    rstd = lax.rsqrt(jnp.mean(center * center, axis=-1, keepdims=True) + EPSILON)
    return center * rstd, rstd


def norm_back(e, xhat, rstd):
    return rstd * (
        e
        - jnp.mean(e, axis=-1, keepdims=True)
        - xhat * jnp.mean(e * xhat, axis=-1, keepdims=True)
    )


def vector(ref, row):
    return ref[row : row + 1, :]


def project_kernel(chips, *refs):
    x_parts, sent, own, pieces = refs[:chips], refs[chips], refs[chips + 1], refs[chips + 2 : chips + 6]
    x_rows, normed, q, k, v, vec, up_shift, weight, vectors, sems, vector_sems = refs[chips + 6 :]
    copies = stage(weight, own, pieces, 0, EXTRA_ROWS, sems)
    capacity, width = x_parts[0].shape
    half = own.shape[0] // 2
    mine, core = lax.axis_index("fsdp"), lax.axis_index("seq") % 2
    vector_copies = []
    for i, (source, flip) in enumerate(
        ((sent, 0), (pieces[0], 1 + core), (pieces[1], 2 - core), (pieces[2], 3))
    ):
        copy = pltpu.make_async_copy(
            source.at[half : half + EXTRA_ROWS, :width], vectors.at[mine ^ flip], vector_sems.at[i]
        )
        copy.start()
        vector_copies.append(copy)
    wait_all(vector_copies)
    shard = width // 4
    for f in range(4):
        row = lax.broadcasted_iota(jnp.int32, (shard, width), 0)
        col = lax.broadcasted_iota(jnp.int32, (shard, width), 1)
        shift = jnp.where(col == row + f * shard, 1.0, 0.0).astype(BF16)
        placed = dot(vectors[f, :, :shard], shift)
        vec[...] = placed if f == 0 else vec[...] + placed
        up_shift[:, f * width : (f + 1) * width] = vectors[f, UP_ROW : UP_ROW + 1, :].astype(F32)
    for i, part in enumerate(x_parts):
        here = slice(i * capacity, (i + 1) * capacity)
        x_rows[here, :] = part[...]
        xhat, _ = norm_parts(part[...].astype(F32))
        normed[here, :] = (xhat * vector(vec, LN1_GAIN) + vector(vec, LN1_BIAS)).astype(BF16)
    wait_all(copies)
    q[...] = (dot(normed[...], weight[:, :width]) + vector(vec, QUERY_BIAS)).astype(BF16)
    k[...] = dot(normed[...], weight[:, width : 2 * width]).astype(BF16)
    v[...] = (dot(normed[...], weight[:, 2 * width :]) + vector(vec, VALUE_BIAS)).astype(BF16)


def half_lanes(dims, which):
    lane = lax.broadcasted_iota(jnp.int32, dims, len(dims) - 1)
    return (lane < HEAD_WIDTH) == (which == 0)


def attend_forward_kernel(
    tiles, q_ref, own_k, own_v, other_k, other_v, qa_ref, ka_ref, live_ref, o_ref, lse_ref
):
    pair = pl.program_id(0)
    rows = q_ref.shape[0]
    row_tile = rows // tiles
    keys = jnp.concatenate([own_k[...], other_k[...]], axis=0)
    keys = jnp.concatenate([keys, ka_ref[...]], axis=1)
    values = jnp.concatenate([own_v[...], other_v[...]], axis=0)
    lane = lax.broadcasted_iota(jnp.int32, (row_tile, LANES), 1)
    for start in range(0, rows, row_tile):
        here = pl.ds(start, row_tile)
        scaled = q_ref[here, :] * jnp.asarray(HEAD_WIDTH**-0.5, BF16)
        marks = qa_ref[here, :]
        halves, lses = [], []
        for which in range(2):
            own = jnp.where(half_lanes(scaled.shape, which), scaled, jnp.zeros_like(scaled))
            scores = cols_of(jnp.concatenate([own, marks], axis=1), keys)
            peak = jnp.max(scores, axis=1, keepdims=True)
            weights = jnp.exp(scores - peak)
            total = jnp.sum(weights, axis=1, keepdims=True)
            halves.append(dot(weights.astype(BF16), values) / total)
            lses.append(peak + jnp.log(total))
        mixed = jnp.where(lane < HEAD_WIDTH, halves[0], halves[1])
        o_ref[here, :] = (mixed * live_ref[here, :]).astype(BF16)
        kept = jnp.where(pair == 0, jnp.zeros((row_tile, LANES), F32), lse_ref[here, :])
        kept = jnp.where(lane == 2 * pair, lses[0], kept)
        lse_ref[here, :] = jnp.where(lane == 2 * pair + 1, lses[1], kept)


def attention_specs(rows, first):
    per_pair = pl.BlockSpec((rows, LANES), lambda i: (0, i + first))
    two = pl.BlockSpec((2, rows, LANES), lambda i: (0, 0, i + first))
    whole = lambda n: pl.BlockSpec((n, LANES), lambda i: (0, 0))
    return per_pair, two, whole(rows), whole(2 * rows)


def ignoring(kernel, start, count):
    return lambda *refs: kernel(*refs[:start], *refs[start + count :])


def attend_forward(first, pairs_here, q, own_k, own_v, other_k, other_v, q_marks, k_marks, live, after=()):
    rows = q.shape[0]
    per_pair, _, marks, all_marks = attention_specs(rows, first)
    out_pair = attention_specs(rows, 0)[0]
    return pl.pallas_call(
        ignoring(partial(attend_forward_kernel, 4), 8, len(after)),
        grid=(pairs_here,),
        in_specs=[per_pair] * 5 + [marks, all_marks, marks] + [ANY] * len(after),
        out_specs=[out_pair, marks],
        out_shape=[shape((rows, pairs_here * LANES)), shape((rows, LANES), F32)],
        compiler_params=pltpu.CompilerParams(vmem_limit_bytes=62 * MIB),
    )(q, own_k, own_v, other_k, other_v, q_marks, k_marks, live, *after)


def widen_kernel(count, tile, *refs):
    attended_parts, refs = refs[:count], refs[count:]
    x_rows, vec, up_shift, own_out, own_up = refs[:5]
    pieces = refs[5:9]
    attended, branch, middle, normed, active, slope, out_weight, up_weight, out_sems, up_sems = refs[9:]
    out_cols = own_out.shape[1]
    out_copies = stage(out_weight, own_out, pieces, 0, 0, out_sems)
    up_copies = stage(up_weight, own_up, pieces, out_cols, 0, up_sems)
    at = 0
    for part in attended_parts:
        attended[:, at : at + part.shape[1]] = part[...]
        at += part.shape[1]
    wait_all(out_copies)
    rows, width = attended.shape
    for start in range(0, rows, tile):
        here = slice(start, start + tile)
        found = dot(attended[here, :], out_weight[...]) + vector(vec, OUT_BIAS)
        branch[here, :] = found
        mid = x_rows[here, :].astype(F32) + vector(vec, SCALE_ATTN) * found
        middle[here, :] = mid
        xhat, _ = norm_parts(mid)
        normed[here, :] = (xhat * vector(vec, LN2_GAIN) + vector(vec, LN2_BIAS)).astype(BF16)
    wait_all(up_copies)

    def widen(block, _):
        cols = pl.ds(pl.multiple_of(block * width, width), width)
        for start in range(0, rows, tile):
            here = slice(start, start + tile)
            hidden = dot(normed[here, :], up_weight[:, cols]) + up_shift[:, cols]
            bell = jnp.exp(-0.5 * hidden * hidden) * (1 / sqrt(2 * pi))
            below = 0.5 + 0.5 * lax.erf(hidden * sqrt(0.5))
            active[here, cols] = (hidden * below).astype(BF16)
            slope[here, cols] = (below + hidden * bell).astype(BF16)
        return 0

    lax.fori_loop(0, up_weight.shape[1] // width, widen, 0)


def down_kernel(chips, tile, *refs):
    active, slope, middle, vec, own = refs[:5]
    pieces, cots, refs = refs[5:9], refs[9 : 9 + chips], refs[9 + chips :]
    outs, refs = refs[:chips], refs[chips:]
    hidden_grad, sums, up_shift_grad = refs[:3]
    terms = refs[3:7]
    cot_rows, down_in, weight, sems = refs[7:]
    copies = stage(weight, own, pieces, 0, 0, sems)
    rows, width = middle.shape
    capacity = cots[0].shape[0]
    bias_sum = None
    for i, part in enumerate(cots):
        here = slice(i * capacity, (i + 1) * capacity)
        cot_rows[here, :] = part[...]
        scaled = (part[...].astype(F32) * vector(vec, SCALE_MLP)).astype(BF16)
        down_in[here, :] = scaled
        term = jnp.sum(scaled.astype(F32), axis=0, keepdims=True)
        bias_sum = term if i == 0 else bias_sum + term
    emit_terms(active, down_in, None, terms, 0)
    wait_all(copies)
    scale_sum = None
    for i in range(chips):
        here = slice(i * capacity, (i + 1) * capacity)
        found = dot(active[here, :], weight[...]) + vector(vec, DOWN_BIAS)
        outs[i][...] = (middle[here, :] + vector(vec, SCALE_MLP) * found).astype(BF16)
        term = jnp.sum(cot_rows[here, :].astype(F32) * found, axis=0, keepdims=True)
        scale_sum = term if i == 0 else scale_sum + term
    sums[0:1, :] = scale_sum
    sums[1:2, :] = bias_sum

    def back(block, _):
        cols = pl.ds(pl.multiple_of(block * width, width), width)
        total = None
        for start in range(0, rows, tile):
            here = slice(start, start + tile)
            grad = cols_of(down_in[here, :], weight[cols, :])
            grad = (grad * slope[here, cols].astype(F32)).astype(BF16)
            hidden_grad[here, cols] = grad
            term = jnp.sum(grad.astype(F32), axis=0, keepdims=True)
            total = term if start == 0 else total + term
        up_shift_grad[:, cols] = total
        return 0

    lax.fori_loop(0, hidden_grad.shape[1] // width, back, 0)


def narrow_kernel(chips, tile, *refs):
    hidden_grad, middle, branch, vec, own_out, own_up = refs[:6]
    pieces, cots, refs = refs[6:10], refs[10 : 10 + chips], refs[10 + chips :]
    middle_grad, branch_grad, attended_grad, sums = refs[:4]
    cot_rows, out_weight, up_weight, out_sems, up_sems = refs[4:]
    out_cols = own_out.shape[1]
    up_copies = stage(up_weight, own_up, pieces, out_cols, 0, up_sems)
    out_copies = stage(out_weight, own_out, pieces, 0, 0, out_sems)
    capacity = cots[0].shape[0]
    for i, part in enumerate(cots):
        cot_rows[i * capacity : (i + 1) * capacity, :] = part[...]
    wait_all(up_copies)
    rows = middle.shape[0]
    totals = [None] * 4
    for start in range(0, rows, tile):
        here = slice(start, start + tile)
        grad = cols_of(hidden_grad[here, :], up_weight[...])
        xhat, rstd = norm_parts(middle[here, :])
        mid = cot_rows[here, :].astype(F32) + norm_back(grad * vector(vec, LN2_GAIN), xhat, rstd)
        middle_grad[here, :] = mid
        back = (mid * vector(vec, SCALE_ATTN)).astype(BF16)
        branch_grad[here, :] = back
        for i, term in enumerate((grad * xhat, grad, mid * branch[here, :], back.astype(F32))):
            term = jnp.sum(term, axis=0, keepdims=True)
            totals[i] = term if start == 0 else totals[i] + term
    for i, total in enumerate(totals):
        sums[i : i + 1, :] = total
    wait_all(out_copies)
    for start in range(0, rows, tile):
        here = slice(start, start + tile)
        attended_grad[here, :] = cols_of(branch_grad[here, :], out_weight[...]).astype(BF16)


def up_terms_kernel(hidden_grad, normed, branch_grad, attended, *refs):
    terms, (up_scratch, out_scratch) = refs[:4], refs[4:]
    emit_terms(normed, hidden_grad, up_scratch, terms, 0)
    emit_terms(attended, branch_grad, out_scratch, terms, hidden_grad.shape[1])


def attend_backward_kernel(
    tiles,
    skipped,
    q_ref,
    own_k,
    own_v,
    other_k,
    other_v,
    qa_ref,
    ka_ref,
    live_ref,
    o_ref,
    lse_ref,
    g_ref,
    dq_ref,
    own_grad_ref,
    other_grad_ref,
    dk_sum,
    dv_sum,
):
    pair = pl.program_id(0) + skipped
    rows = q_ref.shape[0]
    row_tile = rows // tiles
    key_rows = jnp.concatenate([own_k[...], other_k[...]], axis=0)
    keys = jnp.concatenate([key_rows, ka_ref[...]], axis=1)
    values = jnp.concatenate([own_v[...], other_v[...]], axis=0)
    lane = lax.broadcasted_iota(jnp.int32, (row_tile, LANES), 1)
    scale = HEAD_WIDTH**-0.5
    for start in range(0, rows, row_tile):
        here = pl.ds(start, row_tile)
        scaled = q_ref[here, :] * jnp.asarray(scale, BF16)
        marks = qa_ref[here, :]
        grads = (g_ref[here, :] * live_ref[here, :]).astype(BF16)
        both = grads.astype(F32) * o_ref[here, :].astype(F32)
        halves = []
        key_part = value_part = None
        for which in range(2):
            mine = half_lanes(scaled.shape, which)
            own = jnp.where(mine, scaled, jnp.zeros_like(scaled))
            own_grads = jnp.where(mine, grads, jnp.zeros_like(grads))
            row_dot = jnp.sum(jnp.where(mine, both, 0.0), axis=1, keepdims=True)
            lse = jnp.sum(
                jnp.where(lane == 2 * pair + which, lse_ref[here, :], 0.0), axis=1, keepdims=True
            )
            scores = cols_of(jnp.concatenate([own, marks], axis=1), keys)
            probs = jnp.exp(scores - lse)
            prob_grads = cols_of(own_grads, values)
            score_grads = (probs * (prob_grads - row_dot)).astype(BF16)
            halves.append(dot(score_grads, key_rows))
            value_term = rows_of(probs.astype(BF16), own_grads)
            key_term = rows_of(score_grads, own)
            value_part = value_term if which == 0 else value_part + value_term
            key_part = key_term if which == 0 else key_part + key_term
        mixed = jnp.where(lane < HEAD_WIDTH, halves[0], halves[1])
        dq_ref[here, :] = (mixed * scale).astype(BF16)
        if start == 0:
            dk_sum[...] = key_part
            dv_sum[...] = value_part
        else:
            dk_sum[...] += key_part
            dv_sum[...] += value_part
    own_grad_ref[0] = dk_sum[:rows, :].astype(BF16)
    own_grad_ref[1] = dv_sum[:rows, :].astype(BF16)
    other_grad_ref[0] = dk_sum[rows:, :].astype(BF16)
    other_grad_ref[1] = dv_sum[rows:, :].astype(BF16)


def attend_backward(
    first, pairs_here, skipped, q, own_k, own_v, other_k, other_v, q_marks, k_marks, live, attended, lse, grads, after=()
):
    rows = q.shape[0]
    per_pair, _, marks, all_marks = attention_specs(rows, first)
    out_pair, out_two = attention_specs(rows, 0)[:2]
    there = attention_specs(rows, skipped)[0]
    return pl.pallas_call(
        ignoring(partial(attend_backward_kernel, 4, skipped), 11, len(after)),
        grid=(pairs_here,),
        in_specs=[per_pair] * 5 + [marks, all_marks, marks, there, marks, per_pair]
        + [ANY] * len(after),
        out_specs=[out_pair, out_two, out_two],
        out_shape=[shape((rows, pairs_here * LANES))]
        + [shape((2, rows, pairs_here * LANES))] * 2,
        scratch_shapes=[pltpu.VMEM((2 * rows, LANES), F32)] * 2,
        compiler_params=pltpu.CompilerParams(vmem_limit_bytes=62 * MIB),
    )(q, own_k, own_v, other_k, other_v, q_marks, k_marks, live, attended, lse, grads, *after)


def emit_terms(left, right, scratch, terms, at):
    away, keep, keep_far, keep_own = terms
    mine, core = lax.axis_index("fsdp"), lax.axis_index("seq") % 2
    count, cols = left.shape[1] // 4, right.shape[1]
    half = count // 2
    here = slice(at, at + cols)
    if scratch is not None:
        scratch[...] = rows_of(left[...], right[...])

    def rows_at(flip, which):
        start = (mine ^ flip) * count + which * half
        if scratch is not None:
            value = scratch[pl.ds(pl.multiple_of(start, 16), half), :]
        else:
            value = rows_of(left[:, pl.ds(pl.multiple_of(start, LANES), half)], right[...])
        return value.astype(BF16)

    for i in range(2):
        home = core ^ i
        rows = [rows_at(1 + home, home), rows_at(1 + home, 1 - home), rows_at(3, home), rows_at(0, home)]
        if i == 0:
            keep[:half, here] = rows[0]
            keep[half:, here] = rows[1]
            keep_far[:, here] = rows[2]
            keep_own[:, here] = rows[3]
        else:
            for j, value in enumerate(rows):
                away[j * half : (j + 1) * half, here] = value


def term_shapes(rows, cols):
    return [shape((count, cols)) for count in (2 * rows, rows, rows // 2, rows // 2)]


def far_kernel(keep_far, other, out):
    half = out.shape[0]
    out[...] = (wide(keep_far[...]) + wide(other[2 * half : 3 * half, :])).astype(BF16)


def near_kernel(keep, other, far, out):
    half = far.shape[0]
    first = wide(keep[:half, :]) + wide(other[:half, :]) + wide(far[...])
    out[:half, :] = first.astype(BF16)
    second = wide(keep[half:, :]) + wide(other[half : 2 * half, :])
    out[half:, :] = second.astype(BF16)


def half_kernel(keep_own, other, near, both, out):
    half = out.shape[0]
    total = wide(keep_own[...]) + wide(other[3 * half :, :]) + wide(near[:half, :])
    out[...] = (total + wide(both[...])).astype(BF16)


class Reduction:
    def __init__(self, terms):
        away, self.keep, self.keep_far, self.keep_own = terms
        self.half = shape(self.keep_far.shape)
        self.other = to_core(away)

    def send_far(self, after=()):
        operands = [(self.keep_far, VMEM), (self.other, VMEM)]
        self.far_sent = call(far_kernel, operands, [self.half], after=after)[0]
        self.far = to_fsdp(self.far_sent, (2, 1))

    def send_near(self, after=()):
        operands = [(self.keep, VMEM), (self.other, VMEM), (self.far, VMEM)]
        self.near_sent = call(near_kernel, operands, [shape(self.keep.shape)], after=after)[0]
        self.near = to_fsdp(self.near_sent, (1, 2))

    def send_both(self, after=()):
        count = self.half.shape[0]
        self.both_sent = cut_rows(self.near, count, count, after)
        self.both = to_core(self.both_sent)

    def send_chips(self, after=()):
        flips = [1 << i for i in range((lax.axis_size("seq") // 2).bit_length() - 1)]
        self.orders = list(zip(flips, flips[::-1]))
        operands = [(item, VMEM) for item in (self.keep_own, self.other, self.near, self.both)]
        self.sent = call(half_kernel, operands, [self.half], after=after)[0]
        self.got = to_chip(self.sent, *self.orders[0])

    def send_chips_again(self, after=()):
        for order in self.orders[1:]:
            self.sent = add([self.sent, self.got], after)
            self.got = to_chip(self.sent, *order)

    def send_total(self, after=()):
        self.total = add([self.sent, self.got], after)
        self.other_total = to_core(self.total)

    def shards(self, widths, after=()):
        outs = [shape((2 * self.half.shape[0], cols), F32) for cols in widths]
        operands = [(self.total, VMEM), (self.other_total, VMEM)]
        return call(spread_kernel, operands, outs, after=after)


def spread_kernel(own_ref, other_ref, *outs):
    core = lax.axis_index("seq") % 2
    half = own_ref.shape[0]
    at = 0
    for out in outs:
        cols = out.shape[1]
        for i, source in enumerate((own_ref, other_ref)):
            start = pl.multiple_of((core ^ i) * half, 16)
            out[pl.ds(start, half), :] = source[:, at : at + cols].astype(F32)
        at += cols


def project_grad_kernel(count, *refs):
    q_grads, own_grads, other_grads = refs[:count], refs[count : 2 * count], refs[2 * count : 3 * count]
    normed, projected_grad, sums = refs[3 * count : 3 * count + 3]
    terms, scratch = refs[3 * count + 3 : 3 * count + 7], refs[3 * count + 7]
    width = normed.shape[1]
    at = 0
    for q_grad, own_grad, other_grad in zip(q_grads, own_grads, other_grads):
        here = slice(at, at + q_grad.shape[1])
        projected_grad[:, here] = q_grad[...]
        sums[0:1, here] = jnp.sum(q_grad[...].astype(F32), axis=0, keepdims=True)
        for i in range(2):
            both = (own_grad[i].astype(F32) + other_grad[i].astype(F32)).astype(BF16)
            first = (i + 1) * width + at
            projected_grad[:, first : first + q_grad.shape[1]] = both
        sums[1:2, here] = jnp.sum(both.astype(F32), axis=0, keepdims=True)
        at += q_grad.shape[1]
    emit_terms(normed, projected_grad, scratch, terms, 0)


def input_kernel(chips, *refs):
    projected_grad, x_rows, middle_grad, vec, own = refs[:5]
    pieces, rest = refs[5:9], refs[9:]
    outs, sums, weight, sems = rest[:chips], rest[chips], rest[chips + 1], rest[chips + 2]
    copies = stage(weight, own, pieces, 0, EXTRA_ROWS, sems)
    capacity = outs[0].shape[0]
    wait_all(copies)
    totals = [None] * 2
    for i in range(chips):
        here = slice(i * capacity, (i + 1) * capacity)
        grad = cols_of(projected_grad[here, :], weight[...])
        xhat, rstd = norm_parts(x_rows[here, :].astype(F32))
        back = norm_back(grad * vector(vec, LN1_GAIN), xhat, rstd)
        outs[i][...] = (middle_grad[here, :] + back).astype(BF16)
        for j, term in enumerate((grad * xhat, grad)):
            term = jnp.sum(term, axis=0, keepdims=True)
            totals[j] = term if i == 0 else totals[j] + term
    sums[0:1, :] = totals[0]
    sums[1:2, :] = totals[1]


def body(
    tokens,
    image_tokens,
    ln1_gain,
    ln1_bias,
    qkv_weight,
    query_bias,
    value_bias,
    out_weight,
    out_bias,
    scale_attn,
    ln2_gain,
    ln2_bias,
    up_weight,
    up_bias,
    down_weight,
    down_bias,
    scale_mlp,
    cotangent,
):
    seq_count = lax.axis_size("seq")
    fsdp_index = lax.axis_index("fsdp")
    chips = seq_count // 2
    micro_count, tok_count, width = tokens.shape[0], tokens.shape[2], tokens.shape[4]
    slots, images = image_tokens.shape[2:]
    assert chips == micro_count * slots and lax.axis_size("fsdp") == 4
    assert slots * images < PAD_SEGMENT
    capacity = ceil_to((LONG - 2) // seq_count + 2, 16)
    rows = chips * capacity
    tile = rows // 2
    hidden_width = up_weight.shape[1]
    sizes = (slots, images, chips, capacity, tok_count, seq_count)
    counts = image_tokens

    def prepare(values, groups, small=(), after=(), send=True):
        flat = values.reshape(micro_count * tok_count, width)
        shards = [shard for group in groups for shard in group]
        more = EXTRA_ROWS if small else 0
        outs = [
            shape((group[0].shape[0] + more, sum(shard.shape[1] for shard in group)))
            for group in groups
        ]
        if small:
            outs += [shape((outs[0].shape[0] // 2 + more // 2, outs[0].shape[1]))]
        else:
            outs += [shape((rows, LANES)), shape((2 * rows, LANES)), shape((rows, LANES), F32)]
        results = call(
            partial(prepare_kernel, sizes, [len(group) for group in groups], len(small)),
            [(counts, SMEM)] + [(item, VMEM) for item in [flat] + shards + list(small)],
            [shape((capacity, width))] * chips + outs,
            [pltpu.VMEM((EXTRA_ROWS, width), F32)] if small else [],
            after=after,
        )
        parts = list(results[:chips])
        if send:
            for flip in range(chips - 1, 0, -1):
                parts[flip] = to_chip(parts[flip], flip)
        return parts, *results[chips:]

    def send(parts):
        return [parts[0]] + [to_chip(parts[flip], flip) for flip in range(1, chips)]

    def collect(parts, after=()):
        return call(
            partial(collect_kernel, sizes),
            [(counts, SMEM)] + [(part, VMEM) for part in parts],
            [shape((micro_count * tok_count, width))],
            after=after,
        )[0]

    small = [
        ln1_gain,
        ln1_bias,
        query_bias,
        value_bias,
        out_bias,
        scale_attn,
        ln2_gain,
        ln2_bias,
        down_bias,
        scale_mlp,
    ]
    own_rows = ln1_gain.shape[0]
    x_parts, qkv_sent, qkv_first = prepare(tokens, [[qkv_weight]], small + [up_bias])
    near, far = to_fsdp(qkv_sent, (1, 2)), to_fsdp(qkv_first, (3, 3))
    cot_sent, up_sent, down_sent, q_marks, k_marks, live = prepare(
        cotangent, [[out_weight, up_weight], [down_weight]], after=[qkv_sent], send=False
    )
    near, far, up_sent = hold([near, far, up_sent], x_parts + [q_marks])
    qkv_pieces = [near, to_core(near), far, to_core(far)]
    up_near = to_fsdp(up_sent, (1, 2))

    x_rows, normed_first, q, own_k, own_v, vec, up_shift = call(
        partial(project_kernel, chips),
        [(part, VMEM) for part in x_parts]
        + [(item, ANY) for item in [qkv_sent, qkv_weight] + qkv_pieces],
        [shape((rows, width))] * 5
        + [shape((EXTRA_ROWS, width), F32), shape((1, hidden_width), F32)],
        [
            pltpu.VMEM((width, 3 * width), BF16),
            pltpu.VMEM((4, EXTRA_ROWS, width), BF16),
            STAGE_SEMS,
            pltpu.SemaphoreType.DMA((4,)),
        ],
    )
    attention = (q, own_k, own_v, to_core(own_k), to_core(own_v), q_marks, k_marks, live)
    step = width // LANES // 3
    attended_parts, lses = [], []

    def forward(i, after=()):
        part, lse = attend_forward(i * step, step, *attention, after=attended_parts[-1:] + list(after))
        attended_parts.append(part)
        lses.append(lse)

    forward(0)
    up_near, down_sent, *cot_sent = hold([up_near, down_sent] + cot_sent, attended_parts[-1:])
    cot_parts = send(cot_sent)
    up_first = cut_rows(up_near, 0, own_rows // 2)
    up_far = to_fsdp(up_first, (2, 1))
    down_near = to_fsdp(down_sent, (1, 2))
    forward(1, [up_first])
    up_far, *cot_parts = hold([up_far] + cot_parts, attended_parts[-1:])
    up_pieces = [up_near, to_core(up_near), up_far, to_core(up_far)]
    forward(2, [up_far])
    down_near = hold([down_near], attended_parts[-1:])[0]
    down_first = cut_rows(down_near, 0, down_weight.shape[0] // 2)
    down_far = to_fsdp(down_first, (2, 1))

    up_scratch = [
        pltpu.VMEM((width, width), BF16),
        pltpu.VMEM((width, hidden_width), BF16),
        STAGE_SEMS,
        STAGE_SEMS,
    ]
    attended, branch, middle, normed_second, active, slope = call(
        partial(widen_kernel, len(attended_parts), tile),
        [(item, VMEM) for item in attended_parts + [x_rows, vec, up_shift]]
        + [(item, ANY) for item in [out_weight, up_weight] + up_pieces],
        [
            shape((rows, width)),
            shape((rows, width), F32),
            shape((rows, width), F32),
            shape((rows, width)),
            shape((rows, hidden_width)),
            shape((rows, hidden_width)),
        ],
        up_scratch,
        after=[down_first],
    )
    down_far = hold([down_far], [attended])[0]
    down_pieces = [down_near, to_core(down_near), down_far, to_core(down_far)]
    results = call(
        partial(down_kernel, chips, tile),
        [(item, VMEM) for item in (active, slope, middle, vec)]
        + [(item, ANY) for item in [down_weight] + down_pieces]
        + [(part, VMEM) for part in cot_parts],
        [shape((capacity, width))] * chips
        + [
            shape((rows, hidden_width)),
            shape((2, width), F32),
            shape((1, hidden_width), F32),
        ]
        + term_shapes(down_weight.shape[0], width),
        [
            pltpu.VMEM((rows, width), BF16),
            pltpu.VMEM((rows, width), BF16),
            pltpu.VMEM((hidden_width, width), BF16),
            STAGE_SEMS,
        ],
    )
    out_sent, results = results[:chips], results[chips:]
    hidden_grad, down_sums, up_shift_grad, *down_terms = results
    down = Reduction(down_terms)
    out_parts = send(out_sent)

    middle_grad, branch_grad, attended_grad, narrow_sums = call(
        partial(narrow_kernel, chips, tile),
        [(item, VMEM) for item in (hidden_grad, middle, branch, vec)]
        + [(item, ANY) for item in [out_weight, up_weight] + up_pieces]
        + [(part, VMEM) for part in cot_parts],
        [
            shape((rows, width), F32),
            shape((rows, width)),
            shape((rows, width)),
            shape((4, width), F32),
        ],
        [pltpu.VMEM((rows, width), BF16)] + up_scratch,
    )
    down.send_far([middle_grad])
    up_terms = call(
        up_terms_kernel,
        [(item, VMEM) for item in (hidden_grad, normed_second, branch_grad, attended)],
        term_shapes(own_rows, hidden_width + width),
        [pltpu.VMEM((width, hidden_width), F32), pltpu.VMEM((width, width), F32)],
        after=[down.far_sent],
    )
    up = Reduction(up_terms)
    down.send_near([up_terms[0]])

    query_grads, own_grads, other_grads = [], [], []

    def backward(first, count, after):
        query_grad, own_grad, other_grad = attend_backward(
            first,
            count,
            first % step,
            *attention,
            attended_parts[first // step],
            lses[first // step],
            attended_grad,
            after=after + query_grads[-1:],
        )
        query_grads.append(query_grad)
        own_grads.append(own_grad)
        other_grads.append(to_core(other_grad))

    backward(0, 1, [down.near_sent])
    up.send_far(query_grads[-1:])
    out_parts = hold(out_parts, query_grads[-1:])
    backward(1, 1, [up.far_sent, out_parts[-1]])
    down.send_both(query_grads[-1:])
    backward(2, 1, [down.both_sent])
    down.send_chips(query_grads[-1:])
    up.send_near(query_grads[-1:])
    backward(3, 1, [down.sent, up.near_sent])
    backward(4, 1, [])
    down.send_chips_again(query_grads[-1:])
    up.send_both(query_grads[-1:])
    backward(5, 1, [down.sent, up.both_sent])
    up.send_chips(query_grads[-1:])

    projected_grad, qkv_sums, *qkv_terms = call(
        partial(project_grad_kernel, len(query_grads)),
        [(item, VMEM) for item in query_grads + own_grads + other_grads + [normed_first]],
        [shape((rows, 3 * width)), shape((2, width), F32)] + term_shapes(own_rows, 3 * width),
        [pltpu.VMEM((width, 3 * width), F32)],
        after=[up.sent],
    )
    qkv = Reduction(qkv_terms)
    down.send_total([projected_grad])
    qkv.send_far([down.total])
    *in_sent, input_sums = call(
        partial(input_kernel, chips),
        [(item, VMEM) for item in (projected_grad, x_rows, middle_grad, vec)]
        + [(item, ANY) for item in [qkv_weight] + qkv_pieces],
        [shape((capacity, width))] * chips + [shape((2, width), F32)],
        [pltpu.VMEM((width, 3 * width), BF16), STAGE_SEMS],
        after=[qkv.far_sent],
    )
    up.send_chips_again([input_sums])
    qkv.send_near([input_sums])
    in_parts = send(in_sent)
    output = collect(out_parts, [qkv.near_sent])
    (down_grad,) = down.shards([width], [output])
    qkv.send_both([down_grad])
    qkv.send_chips()
    up.send_total()
    up_grad, out_grad = up.shards([hidden_width, width], [qkv.sent])
    qkv.send_chips_again([up_grad])
    input_grad = collect(in_parts, [qkv.sent])
    qkv.send_total([input_grad])
    (qkv_grad,) = qkv.shards([3 * width])
    output, input_grad = output.reshape(tokens.shape), input_grad.reshape(tokens.shape)

    vector_grads = jnp.concatenate(
        [
            input_sums,
            qkv_sums,
            narrow_sums[3:4],
            narrow_sums[2:3],
            narrow_sums[0:2],
            down_sums[1:2],
            down_sums[0:1],
        ]
    )
    vector_grads = jnp.transpose(vector_grads.reshape(10, 4, -1), (1, 0, 2))
    vector_grads = jnp.concatenate([vector_grads, up_shift_grad.reshape(4, 4, -1)], 1)
    vector_grads = vector_grads + to_core(vector_grads)
    for flip in (1, 2):
        vector_grads = vector_grads + to_fsdp(vector_grads, (flip, flip))
    step = 1
    while step < chips:
        vector_grads = vector_grads + to_chip(vector_grads, step)
        step *= 2
    small_grads = lax.dynamic_index_in_dim(vector_grads, fsdp_index, 0, keepdims=False)

    return (
        output,
        input_grad,
        small_grads[LN1_GAIN],
        small_grads[LN1_BIAS],
        qkv_grad,
        small_grads[QUERY_BIAS],
        small_grads[VALUE_BIAS],
        out_grad,
        small_grads[OUT_BIAS],
        small_grads[SCALE_ATTN],
        small_grads[LN2_GAIN],
        small_grads[LN2_BIAS],
        up_grad,
        small_grads[10:].reshape(-1),
        down_grad,
        small_grads[DOWN_BIAS],
        small_grads[SCALE_MLP],
    )


def solution(mesh):
    vector, matrix = P("fsdp"), P("fsdp", None)
    places = P(None, "fsdp", None, "seq", None)
    return jax.shard_map(
        body,
        mesh=mesh,
        in_specs=(
            places,
            P(None, "fsdp", None, None),
            vector,
            vector,
            matrix,
            vector,
            vector,
            matrix,
            vector,
            vector,
            vector,
            vector,
            matrix,
            vector,
            matrix,
            vector,
            vector,
            places,
        ),
        out_specs=(
            places,
            places,
            vector,
            vector,
            matrix,
            vector,
            vector,
            matrix,
            vector,
            vector,
            vector,
            vector,
            matrix,
            vector,
            matrix,
            vector,
            vector,
        ),
        check_vma=False,
    )
```

time: 817 us -> 449 us (0.55)
  Pallas kernels: 0 us -> 239 us
  local copies, waits for them, and re-layouts: 249 us -> 22.8 us
  blocking collectives: 188 us -> 0 us
  other arithmetic: 129 us -> 0.8 us
  matrix products: 125 us -> 0 us
  waiting for transfers between devices: 55.6 us -> 126 us
  between operations: 21 us -> 1.35 us
  starting transfers between devices: 37.3 us -> 53.4 us
    pallas_call x0 -> x49, Pallas kernels: none -> 239 us  [the longest x40 158 us: call(): pl.pallas_call(run, in_specs=[spec for _, spec in operands] + [ANY] * len...]
    psum x1 -> x0, blocking collectives: 145 us -> none  [body(): lax.psum((shards[0], shards[1], shards[2], shards[3], shards[4], shards[5...]
    ppermute x0 -> x58, waiting for transfers between devices: none -> 126 us  [move(): return lax.ppermute(value, BOTH, pairs)]
    dot_general x66 -> x0, matrix products: 125 us -> none  [the longest x26 45.9 us: outer_cols(): lax.dot_general(left, right, (((1,), (1,)), ((), ())), preferred_element_...]
    all_to_all x16 -> x0, other arithmetic: 97.6 us -> none  [the longest x4 34.7 us: body(): lax.all_to_all(stacked, 'seq', split_axis=0, concat_axis=0, tiled=True)]
    unnamed x243 -> x92, local copies, waits for them, and re-layouts: 79.7 us -> 20.7 us
    ppermute x0 -> x58, starting transfers between devices: none -> 53.4 us  [move(): return lax.ppermute(value, BOTH, pairs)]
    reshape x20 -> x4, local copies, waits for them, and re-layouts: 53.8 us -> 0.85 us  [the longest x1 0.67 us: body(): small_grads[10:].reshape(-1)]
  transfers between devices with their start and end apart: 16 -> 58, of which waited for: 6 -> 23; matrix products, arithmetic and copies ran while one was open for 53% -> 1% of each run, Pallas kernels for 0% -> 41%
where the time goes in v1:
time: 449 us; the launch traced here: 443 us
  Pallas kernels  239 us (53%)
  waiting for transfers between devices  126 us (28%)
  starting transfers between devices  53.4 us (12%)
  local copies, waits for them, and re-layouts  22.8 us (5%)
    pallas_call x40, Pallas kernels, call(): pl.pallas_call(run, in_specs=[spec for _, spec in operands] + [ANY] * len...  158 us
    ppermute x58, waiting for transfers between devices, move(): return lax.ppermute(value, BOTH, pairs)  126 us
    ppermute x58, starting transfers between devices, move(): return lax.ppermute(value, BOTH, pairs)  53.4 us
    pallas_call x6, Pallas kernels, attend_backward(): pl.pallas_call(ignoring(partial(attend_backward_kernel, 4, skipped), 11,...  50.4 us
    pallas_call x3, Pallas kernels, attend_forward(): pl.pallas_call(ignoring(partial(attend_forward_kernel, 4), 8, len(after))...  30.9 us
    unnamed x92, local copies, waits for them, and re-layouts  20.7 us
  transfers between devices with their start and end apart: 58, of which 23 were waited for; matrix products, arithmetic and copies ran while one was open for 1% of the time, Pallas kernels for 41%

profile of v1, /device:TPU:0, one launch (start us, length us, event | category | flops | bytes accessed | tf_op | source)
XLA Modules:
  0.0 443.5 jit_solution(16643064093376071318)
XLA Ops:
  0.7 3.2 shard_map.305
  3.9 2.9 collective-permute-start.3
  9.9 2.6 collective-permute-start.1
  12.7 5.0 %shard_map.306 = (bf16[144,768]{1,0:T(8,128)(2,1)}, bf16[144,768]{1,0:T(8,128)(2,1)}, bf16[144,768]{1,0:T(8,128)(2,1)}, bf16[144,768]{1,0:T(8,128)(2,1)}, bf16[1...) custom-call(s32[2,1,2,3]{3,2,1,0:T(2,128)} %refs_0_.7, ...), custom_call_target="tpu_custom_call" | custom-call | tf_op jit(solution)/shard_map/pallas_call | solution.py:82
  18.7 10.2 %collective-permute-done.1.refs_5_.refs_2_ = bf16[144,768]{1,0:T(8,128)(2,1)S(1)} collective-permute-done((bf16[144,768]{1,0:T(8,128)(2,1)}, bf16[144,768]{1,0:T(8,128)(2,1)S(1)}, u32[]{:S(2)}, u32[]{:S(2)}) %collective-permute-start.1) | collective-permute-done | bytes 221216 | tf_op jit(solution)/shard_map/ppermute | solution.py:41
  37.9 7.3 %shard_map.308 = (bf16[576,768]{1,0:T(8,128)(2,1)}, bf16[576,768]{1,0:T(8,128)(2,1)}, bf16[576,768]{1,0:T(8,128)(2,1)}, bf16[576,768]{1,0:T(8,128)(2,1)}, bf16[5...) custom-call(bf16[144,768]{1,0:T(8,128)(2,1)} %get-tuple-element.119.refs_3_.refs_0_, ...), custom_call_target="tpu_custom_call" | custom-call | tf_op jit(solution)/shard_map/pallas_call | solution.py:82
  50.1 10.5 %shard_map.309 = (bf16[576,256]{1,0:T(8,128)(2,1)}, f32[576,128]{1,0:T(8,128)}) custom-call(bf16[576,768]{1,0:T(8,128)(2,1)} %get-tuple-element.129.refs_0_, bf16[576,768]{1,0:T(8,128)(2,1)} %get-tuple-element.130.refs_1_, bf16[576,768]{1,0:T(8,128)(2,1)} %get-tuple-element.131.refs_2_, bf16[576,768]{1,0:T(8,128)(2,1)} %copy-done, ...), custom_call_target="tpu_custom_call" | custom-call | tf_op jit(solution)/shard_map/pallas_call | solution.py:392
  66.5 2.6 collective-permute-start.12
  69.1 8.6 %collective-permute-done.11.refs_2_ = bf16[144,768]{1,0:T(8,128)(2,1)} collective-permute-done((bf16[144,768]{1,0:T(8,128)(2,1)}, bf16[144,768]{1,0:T(8,128)(2,1)}, u32[]{:S(2)}, u32[]{:S(2)}) %collective-permute-start.11) | collective-permute-done | bytes 221216 | tf_op jit(solution)/shard_map/ppermute | solution.py:41
  80.2 10.2 %shard_map.312 = (bf16[576,256]{1,0:T(8,128)(2,1)}, f32[576,128]{1,0:T(8,128)}) custom-call(bf16[576,768]{1,0:T(8,128)(2,1)} %get-tuple-element.129.refs_0_, bf16[576,768]{1,0:T(8,128)(2,1)} %get-tuple-element.130.refs_1_, bf16[576,768]{1,0:T(8,128)(2,1)} %get-tuple-element.131.refs_2_, bf16[576,768]{1,0:T(8,128)(2,1)} %copy-done, ...), custom_call_target="tpu_custom_call" | custom-call | tf_op jit(solution)/shard_map/pallas_call | solution.py:392
  91.4 10.2 %shard_map.314 = (bf16[576,256]{1,0:T(8,128)(2,1)}, f32[576,128]{1,0:T(8,128)}) custom-call(bf16[576,768]{1,0:T(8,128)(2,1)} %get-tuple-element.129.refs_0_, bf16[576,768]{1,0:T(8,128)(2,1)} %get-tuple-element.130.refs_1_, bf16[576,768]{1,0:T(8,128)(2,1)} %get-tuple-element.131.refs_2_, bf16[576,768]{1,0:T(8,128)(2,1)} %copy-done, ...), custom_call_target="tpu_custom_call" | custom-call | tf_op jit(solution)/shard_map/pallas_call | solution.py:392
  107.2 14.9 %shard_map.317 = (bf16[576,768]{1,0:T(8,128)(2,1)}, f32[576,768]{1,0:T(8,128)}, f32[576,768]{1,0:T(8,128)}, bf16[576,768]{1,0:T(8,128)(2,1)}, bf16[576,3072]{1,0:T(8,128)(2,1)}, /*index=5*/bf16[576,3072]{1,0:T(8,128)(2,1)}) custom-call(bf16[576,256]{1,0:T(8,128)(2,1)} %get-tuple-element.134.refs_6_.refs_8_.refs_0_, ...), custom_call_target="tpu_custom_call" | custom-call | tf_op jit(solution)/shard_map/pallas_call | solution.py:82
  125.3 18.8 %shard_map.319 = (bf16[144,768]{1,0:T(8,128)(2,1)}, bf16[144,768]{1,0:T(8,128)(2,1)}, bf16[144,768]{1,0:T(8,128)(2,1)}, bf16[144,768]{1,0:T(8,128)(2,1)}, bf16[5...) custom-call(bf16[576,3072]{1,0:T(8,128)(2,1)} %get-tuple-element.153, ...), custom_call_target="tpu_custom_call" | custom-call | tf_op jit(solution)/shard_map/pallas_call | solution.py:82
  144.6 11.9 %shard_map.320 = (f32[576,768]{1,0:T(8,128)}, bf16[576,768]{1,0:T(8,128)(2,1)}, bf16[576,768]{1,0:T(8,128)(2,1)}, f32[4,768]{1,0:T(4,128)}) custom-call(bf16[576,3072]{1,0:T(8,128)(2,1)} %get-tuple-element.166.refs_0_, f32[576,768]{1,0:T(8,128)} %get-tuple-element.155.refs_2_.refs_1_, f32[576,768]{1,0:T(8,128)} %get-tuple-element.167.refs_2_, ...), custom_call_target="tpu_custom_call" | custom-call | tf_op jit(solution)/shard_map/pallas_call | solution.py:82
  156.5 2.8 shard_map.321.refs_4_
  159.3 10.4 %shard_map.322 = (bf16[384,3840]{1,0:T(8,128)(2,1)}, bf16[192,3840]{1,0:T(8,128)(2,1)}, bf16[96,3840]{1,0:T(8,128)(2,1)}, bf16[96,3840]{1,0:T(8,128)(2,1)}) custom-call(bf16[576,3072]{1,0:T(8,128)(2,1)} %get-tuple-element.166.refs_0_, bf16[576,768]{1,0:T(8,128)(2,1)} %get-tuple-element.173.refs_1_, bf16[576,768]{1,0:T(8,128)(2,1)} %get-tuple-element.174.refs_2_, ...), custom_call_target="tpu_custom_call" | custom-call | tf_op jit(solution)/shard_map/pallas_call | solution.py:82
  170.6 9.1 %collective-permute-done.24.refs_2_ = bf16[384,768]{1,0:T(8,128)(2,1)S(1)} collective-permute-done((bf16[384,768]{1,0:T(8,128)(2,1)S(1)}, bf16[384,768]{1,0:T(8,128)(2,1)S(1)}, u32[]{:S(2)}, u32[]{:S(2)}) %collective-permute-start.24) | collective-permute-done | bytes 589856 | tf_op jit(solution)/shard_map/ppermute | solution.py:41
  180.5 3.5 shard_map.323.refs_11_
  184.7 8.5 %shard_map.324 = (bf16[576,128]{1,0:T(8,128)(2,1)}, bf16[2,576,128]{2,1,0:T(8,128)(2,1)}, bf16[2,576,128]{2,1,0:T(8,128)(2,1)}) custom-call(bf16[576,768]{1,0:T(8,128)(2,1)} %get-tuple-element.129.refs_0_, bf16[576,768]{1,0:T(8,128)(2,1)} %get-tuple-element.130.refs_1_, bf16[576,768]{1,0:T(8,128)(2,1)} %get-tuple-element.131.refs_2_, ...), custom_call_target="tpu_custom_call" | custom-call | tf_op jit(solution)/shard_map/pallas_call | solution.py:599
  193.2 3.1 shard_map.326.refs_11_
  202.1 6.0 %collective-permute-done.20.refs_1_ = bf16[144,768]{1,0:T(8,128)(2,1)S(1)} collective-permute-done((bf16[144,768]{1,0:T(8,128)(2,1)}, bf16[144,768]{1,0:T(8,128)(2,1)S(1)}, u32[]{:S(2)}, u32[]{:S(2)}) %collective-permute-start.20) | collective-permute-done | bytes 221216 | tf_op jit(solution)/shard_map/ppermute | solution.py:41
  208.1 8.2 %collective-permute-done.21.refs_2_ = bf16[144,768]{1,0:T(8,128)(2,1)S(1)} collective-permute-done((bf16[144,768]{1,0:T(8,128)(2,1)}, bf16[144,768]{1,0:T(8,128)(2,1)S(1)}, u32[]{:S(2)}, u32[]{:S(2)}) %collective-permute-start.21) | collective-permute-done | bytes 221216 | tf_op jit(solution)/shard_map/ppermute | solution.py:41
  217.1 8.3 %shard_map.327 = (bf16[576,128]{1,0:T(8,128)(2,1)}, bf16[2,576,128]{2,1,0:T(8,128)(2,1)}, bf16[2,576,128]{2,1,0:T(8,128)(2,1)}) custom-call(bf16[576,768]{1,0:T(8,128)(2,1)} %get-tuple-element.129.refs_0_, bf16[576,768]{1,0:T(8,128)(2,1)} %get-tuple-element.130.refs_1_, bf16[576,768]{1,0:T(8,128)(2,1)} %get-tuple-element.131.refs_2_, ...), custom_call_target="tpu_custom_call" | custom-call | tf_op jit(solution)/shard_map/pallas_call | solution.py:599
  228.5 8.7 %shard_map.329 = (bf16[576,128]{1,0:T(8,128)(2,1)}, bf16[2,576,128]{2,1,0:T(8,128)(2,1)}, bf16[2,576,128]{2,1,0:T(8,128)(2,1)}) custom-call(bf16[576,768]{1,0:T(8,128)(2,1)} %get-tuple-element.129.refs_0_, bf16[576,768]{1,0:T(8,128)(2,1)} %get-tuple-element.130.refs_1_, bf16[576,768]{1,0:T(8,128)(2,1)} %get-tuple-element.131.refs_2_, ...), custom_call_target="tpu_custom_call" | custom-call | tf_op jit(solution)/shard_map/pallas_call | solution.py:599
  237.3 4.0 shard_map.331.refs_12_
  244.3 3.4 shard_map.330.refs_11_.refs_0_
  247.7 8.3 %shard_map.332 = (bf16[576,128]{1,0:T(8,128)(2,1)}, bf16[2,576,128]{2,1,0:T(8,128)(2,1)}, bf16[2,576,128]{2,1,0:T(8,128)(2,1)}) custom-call(bf16[576,768]{1,0:T(8,128)(2,1)} %get-tuple-element.129.refs_0_, bf16[576,768]{1,0:T(8,128)(2,1)} %get-tuple-element.130.refs_1_, bf16[576,768]{1,0:T(8,128)(2,1)} %get-tuple-element.131.refs_2_, ...), custom_call_target="tpu_custom_call" | custom-call | tf_op jit(solution)/shard_map/pallas_call | solution.py:599
  256.0 8.4 %shard_map.333 = (bf16[576,128]{1,0:T(8,128)(2,1)}, bf16[2,576,128]{2,1,0:T(8,128)(2,1)}, bf16[2,576,128]{2,1,0:T(8,128)(2,1)}) custom-call(bf16[576,768]{1,0:T(8,128)(2,1)} %get-tuple-element.129.refs_0_, bf16[576,768]{1,0:T(8,128)(2,1)} %get-tuple-element.130.refs_1_, bf16[576,768]{1,0:T(8,128)(2,1)} %get-tuple-element.131.refs_2_, ...), custom_call_target="tpu_custom_call" | custom-call | tf_op jit(solution)/shard_map/pallas_call | solution.py:599
  267.9 3.3 collective-permute-start.29
  272.2 13.5 %collective-permute-done.29.refs_1_ = bf16[384,768]{1,0:T(8,128)(2,1)S(1)} collective-permute-done((bf16[384,768]{1,0:T(8,128)(2,1)}, bf16[384,768]{1,0:T(8,128)(2,1)S(1)}, u32[]{:S(2)}, u32[]{:S(2)}) %collective-permute-start.29) | collective-permute-done | bytes 589856 | tf_op jit(solution)/shard_map/ppermute | solution.py:41
  288.6 8.3 %shard_map.336 = (bf16[576,128]{1,0:T(8,128)(2,1)}, bf16[2,576,128]{2,1,0:T(8,128)(2,1)}, bf16[2,576,128]{2,1,0:T(8,128)(2,1)}) custom-call(bf16[576,768]{1,0:T(8,128)(2,1)} %get-tuple-element.129.refs_0_, bf16[576,768]{1,0:T(8,128)(2,1)} %get-tuple-element.130.refs_1_, bf16[576,768]{1,0:T(8,128)(2,1)} %get-tuple-element.131.refs_2_, ...), custom_call_target="tpu_custom_call" | custom-call | tf_op jit(solution)/shard_map/pallas_call | solution.py:599
  297.9 3.9 shard_map.337.refs_19_.refs_0_
  302.7 8.1 %shard_map.338 = (bf16[576,2304]{1,0:T(8,128)(2,1)}, f32[2,768]{1,0:T(2,128)}, bf16[384,2304]{1,0:T(8,128)(2,1)}, bf16[192,2304]{1,0:T(8,128)(2,1)}, bf16[96,2304]{1,0:T(8,128)(2,1)}, /*index=5*/bf16[96,2304]{1,0:T(8,128)(2,1)}) custom-call(bf16[576,128]{1,0:T(8,128)(2,1)} %get-tuple-element.176.refs_4_.refs_2_.refs_13_.refs_0_, ...), custom_call_target="tpu_custom_call" | custom-call | tf_op jit(solution)/shard_map/pallas_call | solution.py:82
  313.5 13.9 %collective-permute-done.39.refs_1_ = bf16[384,768]{1,0:T(8,128)(2,1)} collective-permute-done((bf16[384,768]{1,0:T(8,128)(2,1)}, bf16[384,768]{1,0:T(8,128)(2,1)}, u32[]{:S(2)}, u32[]{:S(2)}) %collective-permute-start.39) | collective-permute-done | bytes 589856 | tf_op jit(solution)/shard_map/ppermute | solution.py:41
  336.6 10.5 %shard_map.341 = (bf16[144,768]{1,0:T(8,128)(2,1)}, bf16[144,768]{1,0:T(8,128)(2,1)}, bf16[144,768]{1,0:T(8,128)(2,1)}, bf16[144,768]{1,0:T(8,128)(2,1)}, f32[2,768]{1,0:T(2,128)}) custom-call(bf16[576,2304]{1,0:T(8,128)(2,1)} %get-tuple-element.208.refs_2_.refs_0_, bf16[576,768]{1,0:T(8,128)(2,1)} %get-tuple-element.149.refs_3_.refs_1_, ...), custom_call_target="tpu_custom_call" | custom-call | tf_op jit(solution)/shard_map/pallas_call | solution.py:82
  347.9 3.1 shard_map.342.refs_5_
  356.7 2.9 shard_map.343.refs_2_
  359.6 2.8 shard_map.344.refs_1_
  367.1 9.4 %collective-permute-done.49.refs_1_ = bf16[96,3840]{1,0:T(8,128)(2,1)} collective-permute-done((bf16[96,3840]{1,0:T(8,128)(2,1)}, bf16[96,3840]{1,0:T(8,128)(2,1)}, u32[]{:S(2)}, u32[]{:S(2)}) %collective-permute-start.49) | collective-permute-done | bytes 737312 | tf_op jit(solution)/shard_map/ppermute | solution.py:41
  381.0 3.0 shard_map.346.refs_2_.refs_0_
  385.1 3.1 shard_map.349
  388.2 8.6 %collective-permute-done.47.refs_1_ = bf16[96,2304]{1,0:T(8,128)(2,1)S(1)} collective-permute-done((bf16[96,2304]{1,0:T(8,128)(2,1)}, bf16[96,2304]{1,0:T(8,128)(2,1)S(1)}, u32[]{:S(2)}, u32[]{:S(2)}) %collective-permute-start.47) | collective-permute-done | bytes 442400 | tf_op jit(solution)/shard_map/ppermute | solution.py:41
  406.2 3.1 collective-permute-done.52
  410.2 3.4 collective-permute-done.53
  414.5 11.1 %collective-permute-done.54 = f32[4,14,192]{2,0,1:T(4,128)S(1)} collective-permute-done((f32[4,14,192]{2,0,1:T(4,128)S(1)}, f32[4,14,192]{2,0,1:T(4,128)S(1)}, u32[]{:S(2)}, u32[]{:S(2)}) %collective-permute-start.54) | collective-permute-done | bytes 43040 | tf_op jit(solution)/shard_map/ppermute | solution.py:41
  425.5 3.1 collective-permute-start.55
  428.6 2.9 collective-permute-done.42.refs_3_
  432.3 2.9 shard_map.351.refs_2_
  (227 shorter events, 109.7 us)
Async XLA Ops:
  3.9 27.5 %collective-permute-start.3 = (bf16[208,2304]{1,0:T(8,128)(2,1)}, bf16[208,2304]{1,0:T(8,128)(2,1)S(1)}, u32[]{:S(2)}, u32[]{:S(2)}) collective-permute-start(bf16[208,2304]{1,0:T(8,128)(2,1)} %get-tuple-element.123.refs_5_.refs_4_), channel_id=1, source_target_pairs={{0,8},{1,17},{2,10},{3,19},{4,12},{5,21},{6,14},{7,23},{8,0},{9,25... | collective-permute-start | bytes 2875400 | tf_op jit(solution)/shard_map/ppermute | solution.py:41
  6.8 24.6 %collective-permute-start.4 = (bf16[112,2304]{1,0:T(8,128)(2,1)}, bf16[112,2304]{1,0:T(8,128)(2,1)S(1)}, u32[]{:S(2)}, u32[]{:S(2)}) collective-permute-start(bf16[112,2304]{1,0:T(8,128)(2,1)} %get-tuple-element.124), channel_id=1, source_target_pairs={{0,24},{1,25},{2,26},{3,27},{4,28},{5,29},{6,30},{7,31},{8,16},{9,... | collective-permute-start | bytes 1548296 | tf_op jit(solution)/shard_map/ppermute | solution.py:41
  8.3 10.3 %collective-permute-start = (bf16[144,768]{1,0:T(8,128)(2,1)}, bf16[144,768]{1,0:T(8,128)(2,1)S(1)}, u32[]{:S(2)}, u32[]{:S(2)}) collective-permute-start(bf16[144,768]{1,0:T(8,128)(2,1)} %get-tuple-element.120), channel_id=1, source_target_pairs={{0,2},{1,3},{2,0},{3,1},{4,6},{5,7},{6,4},{7,5},{8,10},{9,11},{10,... | collective-permute-start | bytes 663560 | tf_op jit(solution)/shard_map/ppermute | solution.py:41
  9.9 19.0 %collective-permute-start.1 = (bf16[144,768]{1,0:T(8,128)(2,1)}, bf16[144,768]{1,0:T(8,128)(2,1)S(1)}, u32[]{:S(2)}, u32[]{:S(2)}) collective-permute-start(bf16[144,768]{1,0:T(8,128)(2,1)} %get-tuple-element.121), channel_id=1, source_target_pairs={{0,4},{1,5},{2,6},{3,7},{4,0},{5,1},{6,2},{7,3},{8,12},{9,13},{10,... | collective-permute-start | bytes 663560 | tf_op jit(solution)/shard_map/ppermute | solution.py:41
  12.5 16.4 %collective-permute-start.2 = (bf16[144,768]{1,0:T(8,128)(2,1)}, bf16[144,768]{1,0:T(8,128)(2,1)}, u32[]{:S(2)}, u32[]{:S(2)}) collective-permute-start(bf16[144,768]{1,0:T(8,128)(2,1)} %get-tuple-element.122), channel_id=1, source_target_pairs={{0,6},{1,7},{2,4},{3,5},{4,2},{5,3},{6,0},{7,1},{8,14},{9,15},{10,... | collective-permute-start | bytes 663560 | tf_op jit(solution)/shard_map/ppermute | solution.py:41
  32.6 28.1 %collective-permute-start.9 = (bf16[192,3840]{1,0:T(8,128)(2,1)}, bf16[192,3840]{1,0:T(8,128)(2,1)}, u32[]{:S(2)}, u32[]{:S(2)}) collective-permute-start(bf16[192,3840]{1,0:T(8,128)(2,1)} %get-tuple-element.135), channel_id=1, source_target_pairs={{0,8},{1,17},{2,10},{3,19},{4,12},{5,21},{6,14},{7,23},{8,0},{9,25... | collective-permute-start | bytes 4423688 | tf_op jit(solution)/shard_map/ppermute | solution.py:41
  60.7 40.9 %collective-permute-start.16 = (bf16[768,768]{1,0:T(8,128)(2,1)}, bf16[768,768]{1,0:T(8,128)(2,1)S(1)}, u32[]{:S(2)}, u32[]{:S(2)}) collective-permute-start(bf16[768,768]{1,0:T(8,128)(2,1)} %get-tuple-element.152), channel_id=1, source_target_pairs={{0,8},{1,17},{2,10},{3,19},{4,12},{5,21},{6,14},{7,23},{8,0},{9,25... | collective-permute-start | bytes 3538952 | tf_op jit(solution)/shard_map/ppermute | solution.py:41
  64.4 26.1 %collective-permute-start.10 = (bf16[96,3840]{1,0:T(8,128)(2,1)}, bf16[96,3840]{1,0:T(8,128)(2,1)S(1)}, u32[]{:S(2)}, u32[]{:S(2)}) collective-permute-start(bf16[96,3840]{1,0:T(8,128)(2,1)} %shard_map.311.refs_9_), channel_id=1, source_target_pairs={{0,16},{1,9},{2,18},{3,11},{4,20},{5,13},{6,22},{7,15},{8,24},{9,1... | collective-permute-start | bytes 2211848 | tf_op jit(solution)/shard_map/ppermute | solution.py:41
  64.9 41.4 %collective-permute-start.14 = (bf16[192,3840]{1,0:T(8,128)(2,1)}, bf16[192,3840]{1,0:T(8,128)(2,1)}, u32[]{:S(2)}, u32[]{:S(2)}) collective-permute-start(bf16[192,3840]{1,0:T(8,128)(2,1)} %get-tuple-element.141.refs_0_.refs_8_.refs_6_), channel_id=1, source_target_pairs={{0,1},{1,0},{2,3},{3,2},{4,5},{5,4},{6,7},{7,6},{8,9},{9,8},{10,11... | collective-permute-start | bytes 4423688 | tf_op jit(solution)/shard_map/ppermute | solution.py:41
  64.9 12.8 %collective-permute-start.11 = (bf16[144,768]{1,0:T(8,128)(2,1)}, bf16[144,768]{1,0:T(8,128)(2,1)}, u32[]{:S(2)}, u32[]{:S(2)}) collective-permute-start(bf16[144,768]{1,0:T(8,128)(2,1)} %get-tuple-element.144), channel_id=1, source_target_pairs={{0,2},{1,3},{2,0},{3,1},{4,6},{5,7},{6,4},{7,5},{8,10},{9,11},{10,... | collective-permute-start | bytes 663560 | tf_op jit(solution)/shard_map/ppermute | solution.py:41
  66.5 24.0 %collective-permute-start.12 = (bf16[144,768]{1,0:T(8,128)(2,1)}, bf16[144,768]{1,0:T(8,128)(2,1)}, u32[]{:S(2)}, u32[]{:S(2)}) collective-permute-start(bf16[144,768]{1,0:T(8,128)(2,1)} %get-tuple-element.145), channel_id=1, source_target_pairs={{0,4},{1,5},{2,6},{3,7},{4,0},{5,1},{6,2},{7,3},{8,12},{9,13},{10,... | collective-permute-start | bytes 663560 | tf_op jit(solution)/shard_map/ppermute | solution.py:41
  77.7 12.8 %collective-permute-start.13 = (bf16[144,768]{1,0:T(8,128)(2,1)}, bf16[144,768]{1,0:T(8,128)(2,1)}, u32[]{:S(2)}, u32[]{:S(2)}) collective-permute-start(bf16[144,768]{1,0:T(8,128)(2,1)} %get-tuple-element.146), channel_id=1, source_target_pairs={{0,6},{1,7},{2,4},{3,5},{4,2},{5,3},{6,0},{7,1},{8,14},{9,15},{10,... | collective-permute-start | bytes 663560 | tf_op jit(solution)/shard_map/ppermute | solution.py:41
  91.4 15.0 %collective-permute-start.15 = (bf16[96,3840]{1,0:T(8,128)(2,1)}, bf16[96,3840]{1,0:T(8,128)(2,1)S(1)}, u32[]{:S(2)}, u32[]{:S(2)}) collective-permute-start(bf16[96,3840]{1,0:T(8,128)(2,1)} %get-tuple-element.147.refs_9_.refs_10_.refs_8_), channel_id=1, source_target_pairs={{0,1},{1,0},{2,3},{3,2},{4,5},{5,4},{6,7},{7,6},{8,9},{9,8},{10,11... | collective-permute-start | bytes 2211848 | tf_op jit(solution)/shard_map/ppermute | solution.py:41
  104.8 17.3 %collective-permute-start.18 = (bf16[384,768]{1,0:T(8,128)(2,1)}, bf16[384,768]{1,0:T(8,128)(2,1)}, u32[]{:S(2)}, u32[]{:S(2)}) collective-permute-start(bf16[384,768]{1,0:T(8,128)(2,1)} %shard_map.316.refs_12_), channel_id=1, source_target_pairs={{0,16},{1,9},{2,18},{3,11},{4,20},{5,13},{6,22},{7,15},{8,24},{9,1... | collective-permute-start | bytes 1769480 | tf_op jit(solution)/shard_map/ppermute | solution.py:41
  106.3 18.2 %collective-permute-start.17 = (bf16[768,768]{1,0:T(8,128)(2,1)S(1)}, bf16[768,768]{1,0:T(8,128)(2,1)}, u32[]{:S(2)}, u32[]{:S(2)}) collective-permute-start(bf16[768,768]{1,0:T(8,128)(2,1)S(1)} %copy-done.5), channel_id=1, source_target_pairs={{0,1},{1,0},{2,3},{3,2},{4,5},{5,4},{6,7},{7,6},{8,9},{9,8},{10,11... | collective-permute-start | bytes 3538952 | tf_op jit(solution)/shard_map/ppermute | solution.py:41
  144.1 12.4 %collective-permute-start.23 = (bf16[1536,768]{1,0:T(8,128)(2,1)}, bf16[1536,768]{1,0:T(8,128)(2,1)}, u32[]{:S(2)}, u32[]{:S(2)}) collective-permute-start(bf16[1536,768]{1,0:T(8,128)(2,1)} %get-tuple-element.170), channel_id=1, source_target_pairs={{0,1},{1,0},{2,3},{3,2},{4,5},{5,4},{6,7},{7,6},{8,9},{9,8},{10,11... | collective-permute-start | bytes 7077896 | tf_op jit(solution)/shard_map/ppermute | solution.py:41
  169.7 23.5 %collective-permute-start.25 = (bf16[384,3840]{1,0:T(8,128)(2,1)}, bf16[384,3840]{1,0:T(8,128)(2,1)}, u32[]{:S(2)}, u32[]{:S(2)}) collective-permute-start(bf16[384,3840]{1,0:T(8,128)(2,1)} %get-tuple-element.175.refs_3_), channel_id=1, source_target_pairs={{0,1},{1,0},{2,3},{3,2},{4,5},{5,4},{6,7},{7,6},{8,9},{9,8},{10,11... | collective-permute-start | bytes 8847368 | tf_op jit(solution)/shard_map/ppermute | solution.py:41
  169.8 9.9 %collective-permute-start.24 = (bf16[384,768]{1,0:T(8,128)(2,1)S(1)}, bf16[384,768]{1,0:T(8,128)(2,1)S(1)}, u32[]{:S(2)}, u32[]{:S(2)}) collective-permute-start(bf16[384,768]{1,0:T(8,128)(2,1)S(1)} %copy-done.14), channel_id=1, source_target_pairs={{0,16},{1,9},{2,18},{3,11},{4,20},{5,13},{6,22},{7,15},{8,24},{9,1... | collective-permute-start | bytes 1769480 | tf_op jit(solution)/shard_map/ppermute | solution.py:41
  184.0 41.4 %collective-permute-start.26 = (bf16[768,768]{1,0:T(8,128)(2,1)}, bf16[768,768]{1,0:T(8,128)(2,1)S(1)}, u32[]{:S(2)}, u32[]{:S(2)}) collective-permute-start(bf16[768,768]{1,0:T(8,128)(2,1)} %shard_map.323.refs_11_), channel_id=1, source_target_pairs={{0,8},{1,17},{2,10},{3,19},{4,12},{5,21},{6,14},{7,23},{8,0},{9,25... | collective-permute-start | bytes 3538952 | tf_op jit(solution)/shard_map/ppermute | solution.py:41
  196.3 40.9 %collective-permute-start.28 = (bf16[96,3840]{1,0:T(8,128)(2,1)}, bf16[96,3840]{1,0:T(8,128)(2,1)}, u32[]{:S(2)}, u32[]{:S(2)}) collective-permute-start(bf16[96,3840]{1,0:T(8,128)(2,1)} %shard_map.326.refs_11_), channel_id=1, source_target_pairs={{0,16},{1,9},{2,18},{3,11},{4,20},{5,13},{6,22},{7,15},{8,24},{9,1... | collective-permute-start | bytes 2211848 | tf_op jit(solution)/shard_map/ppermute | solution.py:41
  197.7 10.4 %collective-permute-start.20 = (bf16[144,768]{1,0:T(8,128)(2,1)}, bf16[144,768]{1,0:T(8,128)(2,1)S(1)}, u32[]{:S(2)}, u32[]{:S(2)}) collective-permute-start(bf16[144,768]{1,0:T(8,128)(2,1)} %get-tuple-element.162), channel_id=1, source_target_pairs={{0,2},{1,3},{2,0},{3,1},{4,6},{5,7},{6,4},{7,5},{8,10},{9,11},{10,... | collective-permute-start | bytes 663560 | tf_op jit(solution)/shard_map/ppermute | solution.py:41
  197.7 18.6 %collective-permute-start.21 = (bf16[144,768]{1,0:T(8,128)(2,1)}, bf16[144,768]{1,0:T(8,128)(2,1)S(1)}, u32[]{:S(2)}, u32[]{:S(2)}) collective-permute-start(bf16[144,768]{1,0:T(8,128)(2,1)} %get-tuple-element.163), channel_id=1, source_target_pairs={{0,4},{1,5},{2,6},{3,7},{4,0},{5,1},{6,2},{7,3},{8,12},{9,13},{10,... | collective-permute-start | bytes 663560 | tf_op jit(solution)/shard_map/ppermute | solution.py:41
  199.6 16.8 %collective-permute-start.22 = (bf16[144,768]{1,0:T(8,128)(2,1)}, bf16[144,768]{1,0:T(8,128)(2,1)S(1)}, u32[]{:S(2)}, u32[]{:S(2)}) collective-permute-start(bf16[144,768]{1,0:T(8,128)(2,1)} %get-tuple-element.164), channel_id=1, source_target_pairs={{0,6},{1,7},{2,4},{3,5},{4,2},{5,3},{6,0},{7,1},{8,14},{9,15},{10,... | collective-permute-start | bytes 663560 | tf_op jit(solution)/shard_map/ppermute | solution.py:41
  241.2 23.2 %collective-permute-start.30 = (bf16[192,3840]{1,0:T(8,128)(2,1)}, bf16[192,3840]{1,0:T(8,128)(2,1)S(1)}, u32[]{:S(2)}, u32[]{:S(2)}) collective-permute-start(bf16[192,3840]{1,0:T(8,128)(2,1)} %shard_map.331.refs_12_), channel_id=1, source_target_pairs={{0,8},{1,17},{2,10},{3,19},{4,12},{5,21},{6,14},{7,23},{8,0},{9,25... | collective-permute-start | bytes 4423688 | tf_op jit(solution)/shard_map/ppermute | solution.py:41
  267.8 29.2 %collective-permute-start.37 = (bf16[96,3840]{1,0:T(8,128)(2,1)}, bf16[96,3840]{1,0:T(8,128)(2,1)S(1)}, u32[]{:S(2)}, u32[]{:S(2)}) collective-permute-start(bf16[96,3840]{1,0:T(8,128)(2,1)} %shard_map.335.refs_12_), channel_id=1, source_target_pairs={{0,1},{1,0},{2,3},{3,2},{4,5},{5,4},{6,7},{7,6},{8,9},{9,8},{10,11... | collective-permute-start | bytes 2211848 | tf_op jit(solution)/shard_map/ppermute | solution.py:41
  267.9 17.7 %collective-permute-start.29 = (bf16[384,768]{1,0:T(8,128)(2,1)}, bf16[384,768]{1,0:T(8,128)(2,1)S(1)}, u32[]{:S(2)}, u32[]{:S(2)}) collective-permute-start(bf16[384,768]{1,0:T(8,128)(2,1)} %shard_map.330.refs_11_.refs_0_), channel_id=1, source_target_pairs={{0,2},{1,5},{2,0},{3,7},{4,6},{5,1},{6,4},{7,3},{8,10},{9,13},{10,... | collective-permute-start | bytes 1769480 | tf_op jit(solution)/shard_map/ppermute | solution.py:41
  271.2 25.7 %collective-permute-start.31 = (bf16[2,576,128]{2,1,0:T(8,128)(2,1)}, bf16[2,576,128]{2,1,0:T(8,128)(2,1)S(1)}, u32[]{:S(2)}, u32[]{:S(2)}) collective-permute-start(bf16[2,576,128]{2,1,0:T(8,128)(2,1)} %get-tuple-element.197), channel_id=1, source_target_pairs={{0,1},{1,0},{2,3},{3,2},{4,5},{5,4},{6,7},{7,6},{8,9},{9,8},{10,11... | collective-permute-start | bytes 884744 | tf_op jit(solution)/shard_map/ppermute | solution.py:41
  271.6 30.1 %collective-permute-start.33 = (bf16[2,576,128]{2,1,0:T(8,128)(2,1)}, bf16[2,576,128]{2,1,0:T(8,128)(2,1)S(1)}, u32[]{:S(2)}, u32[]{:S(2)}) collective-permute-start(bf16[2,576,128]{2,1,0:T(8,128)(2,1)} %get-tuple-element.199), channel_id=1, source_target_pairs={{0,1},{1,0},{2,3},{3,2},{4,5},{5,4},{6,7},{7,6},{8,9},{9,8},{10,11... | collective-permute-start | bytes 884744 | tf_op jit(solution)/shard_map/ppermute | solution.py:41
  271.7 30.0 %collective-permute-start.32 = (bf16[2,576,128]{2,1,0:T(8,128)(2,1)}, bf16[2,576,128]{2,1,0:T(8,128)(2,1)}, u32[]{:S(2)}, u32[]{:S(2)}) collective-permute-start(bf16[2,576,128]{2,1,0:T(8,128)(2,1)} %get-tuple-element.198), channel_id=1, source_target_pairs={{0,1},{1,0},{2,3},{3,2},{4,5},{5,4},{6,7},{7,6},{8,9},{9,8},{10,11... | collective-permute-start | bytes 884744 | tf_op jit(solution)/shard_map/ppermute | solution.py:41
  285.6 16.1 %collective-permute-start.35 = (bf16[2,576,128]{2,1,0:T(8,128)(2,1)}, bf16[2,576,128]{2,1,0:T(8,128)(2,1)}, u32[]{:S(2)}, u32[]{:S(2)}) collective-permute-start(bf16[2,576,128]{2,1,0:T(8,128)(2,1)} %get-tuple-element.201), channel_id=1, source_target_pairs={{0,1},{1,0},{2,3},{3,2},{4,5},{5,4},{6,7},{7,6},{8,9},{9,8},{10,11... | collective-permute-start | bytes 884744 | tf_op jit(solution)/shard_map/ppermute | solution.py:41
  296.9 4.9 %collective-permute-start.34 = (bf16[2,576,128]{2,1,0:T(8,128)(2,1)}, bf16[2,576,128]{2,1,0:T(8,128)(2,1)S(1)}, u32[]{:S(2)}, u32[]{:S(2)}) collective-permute-start(bf16[2,576,128]{2,1,0:T(8,128)(2,1)} %get-tuple-element.200), channel_id=1, source_target_pairs={{0,1},{1,0},{2,3},{3,2},{4,5},{5,4},{6,7},{7,6},{8,9},{9,8},{10,11... | collective-permute-start | bytes 884744 | tf_op jit(solution)/shard_map/ppermute | solution.py:41
  297.0 4.8 %collective-permute-start.36 = (bf16[2,576,128]{2,1,0:T(8,128)(2,1)}, bf16[2,576,128]{2,1,0:T(8,128)(2,1)S(1)}, u32[]{:S(2)}, u32[]{:S(2)}) collective-permute-start(bf16[2,576,128]{2,1,0:T(8,128)(2,1)} %get-tuple-element.202), channel_id=1, source_target_pairs={{0,1},{1,0},{2,3},{3,2},{4,5},{5,4},{6,7},{7,6},{8,9},{9,8},{10,11... | collective-permute-start | bytes 884744 | tf_op jit(solution)/shard_map/ppermute | solution.py:41
  310.7 18.9 %collective-permute-start.38 = (bf16[384,2304]{1,0:T(8,128)(2,1)}, bf16[384,2304]{1,0:T(8,128)(2,1)S(1)}, u32[]{:S(2)}, u32[]{:S(2)}) collective-permute-start(bf16[384,2304]{1,0:T(8,128)(2,1)} %get-tuple-element.206), channel_id=1, source_target_pairs={{0,1},{1,0},{2,3},{3,2},{4,5},{5,4},{6,7},{7,6},{8,9},{9,8},{10,11... | collective-permute-start | bytes 5308424 | tf_op jit(solution)/shard_map/ppermute | solution.py:41
  311.2 16.2 %collective-permute-start.39 = (bf16[384,768]{1,0:T(8,128)(2,1)}, bf16[384,768]{1,0:T(8,128)(2,1)}, u32[]{:S(2)}, u32[]{:S(2)}) collective-permute-start(bf16[384,768]{1,0:T(8,128)(2,1)} %shard_map.334.refs_11_.refs_0_), channel_id=1, source_target_pairs={{0,4},{1,3},{2,6},{3,1},{4,0},{5,7},{6,2},{7,5},{8,12},{9,11},{10,... | collective-permute-start | bytes 1769480 | tf_op jit(solution)/shard_map/ppermute | solution.py:41
  333.3 13.8 %collective-permute-start.40 = (bf16[96,2304]{1,0:T(8,128)(2,1)}, bf16[96,2304]{1,0:T(8,128)(2,1)S(1)}, u32[]{:S(2)}, u32[]{:S(2)}) collective-permute-start(bf16[96,2304]{1,0:T(8,128)(2,1)} %shard_map.340.refs_9_), channel_id=1, source_target_pairs={{0,16},{1,9},{2,18},{3,11},{4,20},{5,13},{6,22},{7,15},{8,24},{9,1... | collective-permute-start | bytes 1327112 | tf_op jit(solution)/shard_map/ppermute | solution.py:41
  334.8 19.3 %collective-permute-start.48 = (bf16[96,3840]{1,0:T(8,128)(2,1)}, bf16[96,3840]{1,0:T(8,128)(2,1)}, u32[]{:S(2)}, u32[]{:S(2)}) collective-permute-start(bf16[96,3840]{1,0:T(8,128)(2,1)} %shard_map.337.refs_19_.refs_0_), channel_id=1, source_target_pairs={{0,2},{1,5},{2,0},{3,7},{4,6},{5,1},{6,4},{7,3},{8,10},{9,13},{10,... | collective-permute-start | bytes 2211848 | tf_op jit(solution)/shard_map/ppermute | solution.py:41
  351.0 13.3 %collective-permute-start.44 = (bf16[192,2304]{1,0:T(8,128)(2,1)}, bf16[192,2304]{1,0:T(8,128)(2,1)S(1)}, u32[]{:S(2)}, u32[]{:S(2)}) collective-permute-start(bf16[192,2304]{1,0:T(8,128)(2,1)} %shard_map.342.refs_5_), channel_id=1, source_target_pairs={{0,8},{1,17},{2,10},{3,19},{4,12},{5,21},{6,14},{7,23},{8,0},{9,25... | collective-permute-start | bytes 2654216 | tf_op jit(solution)/shard_map/ppermute | solution.py:41
  351.7 7.8 %collective-permute-start.45 = (bf16[384,768]{1,0:T(8,128)(2,1)S(1)}, bf16[384,768]{1,0:T(8,128)(2,1)}, u32[]{:S(2)}, u32[]{:S(2)}) collective-permute-start(bf16[384,768]{1,0:T(8,128)(2,1)S(1)} %copy-done.8), channel_id=1, source_target_pairs={{0,1},{1,0},{2,3},{3,2},{4,5},{5,4},{6,7},{7,6},{8,9},{9,8},{10,11... | collective-permute-start | bytes 1769480 | tf_op jit(solution)/shard_map/ppermute | solution.py:41
  356.4 20.1 %collective-permute-start.49 = (bf16[96,3840]{1,0:T(8,128)(2,1)}, bf16[96,3840]{1,0:T(8,128)(2,1)}, u32[]{:S(2)}, u32[]{:S(2)}) collective-permute-start(bf16[96,3840]{1,0:T(8,128)(2,1)} %shard_map.347.refs_0_), channel_id=1, source_target_pairs={{0,4},{1,3},{2,6},{3,1},{4,0},{5,7},{6,2},{7,5},{8,12},{9,11},{10,... | collective-permute-start | bytes 2211848 | tf_op jit(solution)/shard_map/ppermute | solution.py:41
  367.1 13.1 %collective-permute-start.46 = (bf16[96,2304]{1,0:T(8,128)(2,1)}, bf16[96,2304]{1,0:T(8,128)(2,1)S(1)}, u32[]{:S(2)}, u32[]{:S(2)}) collective-permute-start(bf16[96,2304]{1,0:T(8,128)(2,1)} %shard_map.345), channel_id=1, source_target_pairs={{0,1},{1,0},{2,3},{3,2},{4,5},{5,4},{6,7},{7,6},{8,9},{9,8},{10,11... | collective-permute-start | bytes 1327112 | tf_op jit(solution)/shard_map/ppermute | solution.py:41
  378.9 5.3 %collective-permute-start.50 = (bf16[96,3840]{1,0:T(8,128)(2,1)}, bf16[96,3840]{1,0:T(8,128)(2,1)S(1)}, u32[]{:S(2)}, u32[]{:S(2)}) collective-permute-start(bf16[96,3840]{1,0:T(8,128)(2,1)} %shard_map.348.refs_0_), channel_id=1, source_target_pairs={{0,1},{1,0},{2,3},{3,2},{4,5},{5,4},{6,7},{7,6},{8,9},{9,8},{10,11... | collective-permute-start | bytes 2211848 | tf_op jit(solution)/shard_map/ppermute | solution.py:41
  384.0 12.8 %collective-permute-start.47 = (bf16[96,2304]{1,0:T(8,128)(2,1)}, bf16[96,2304]{1,0:T(8,128)(2,1)S(1)}, u32[]{:S(2)}, u32[]{:S(2)}) collective-permute-start(bf16[96,2304]{1,0:T(8,128)(2,1)} %shard_map.346.refs_2_.refs_0_), channel_id=1, source_target_pairs={{0,2},{1,5},{2,0},{3,7},{4,6},{5,1},{6,4},{7,3},{8,10},{9,13},{10,... | collective-permute-start | bytes 1327112 | tf_op jit(solution)/shard_map/ppermute | solution.py:41
  399.7 35.6 %collective-permute-start.56 = (bf16[96,2304]{1,0:T(8,128)(2,1)}, bf16[96,2304]{1,0:T(8,128)(2,1)S(1)}, u32[]{:S(2)}, u32[]{:S(2)}) collective-permute-start(bf16[96,2304]{1,0:T(8,128)(2,1)} %shard_map.350.refs_5_.refs_0_), channel_id=1, source_target_pairs={{0,4},{1,3},{2,6},{3,1},{4,0},{5,7},{6,2},{7,5},{8,12},{9,11},{10,... | collective-permute-start | bytes 1327112 | tf_op jit(solution)/shard_map/ppermute | solution.py:41
  400.6 28.0 %collective-permute-start.41 = (bf16[144,768]{1,0:T(8,128)(2,1)S(1)}, bf16[144,768]{1,0:T(8,128)(2,1)S(1)}, u32[]{:S(2)}, u32[]{:S(2)}) collective-permute-start(bf16[144,768]{1,0:T(8,128)(2,1)S(1)} %copy-done.45), channel_id=1, source_target_pairs={{0,2},{1,3},{2,0},{3,1},{4,6},{5,7},{6,4},{7,5},{8,10},{9,11},{10,... | collective-permute-start | bytes 663560 | tf_op jit(solution)/shard_map/ppermute | solution.py:41
  402.4 29.2 %collective-permute-start.42 = (bf16[144,768]{1,0:T(8,128)(2,1)S(1)}, bf16[144,768]{1,0:T(8,128)(2,1)S(1)}, u32[]{:S(2)}, u32[]{:S(2)}) collective-permute-start(bf16[144,768]{1,0:T(8,128)(2,1)S(1)} %copy-done.44), channel_id=1, source_target_pairs={{0,4},{1,5},{2,6},{3,7},{4,0},{5,1},{6,2},{7,3},{8,12},{9,13},{10,... | collective-permute-start | bytes 663560 | tf_op jit(solution)/shard_map/ppermute | solution.py:41
  403.0 28.5 %collective-permute-start.43 = (bf16[144,768]{1,0:T(8,128)(2,1)S(1)}, bf16[144,768]{1,0:T(8,128)(2,1)S(1)}, u32[]{:S(2)}, u32[]{:S(2)}) collective-permute-start(bf16[144,768]{1,0:T(8,128)(2,1)S(1)} %copy-done.43), channel_id=1, source_target_pairs={{0,6},{1,7},{2,4},{3,5},{4,2},{5,3},{6,0},{7,1},{8,14},{9,15},{10,... | collective-permute-start | bytes 663560 | tf_op jit(solution)/shard_map/ppermute | solution.py:41
  413.6 11.9 %collective-permute-start.54 = (f32[4,14,192]{2,0,1:T(4,128)S(1)}, f32[4,14,192]{2,0,1:T(4,128)S(1)}, u32[]{:S(2)}, u32[]{:S(2)}) collective-permute-start(f32[4,14,192]{2,0,1:T(4,128)S(1)} %add.21), channel_id=1, source_target_pairs={{0,2},{1,3},{2,0},{3,1},{4,6},{5,7},{6,4},{7,5},{8,10},{9,11},{10,... | collective-permute-start | bytes 129032 | tf_op jit(solution)/shard_map/ppermute | solution.py:41
  425.5 12.5 %collective-permute-start.55 = (f32[4,14,192]{2,0,1:T(4,128)S(1)}, f32[4,14,192]{2,0,1:T(4,128)S(1)}, u32[]{:S(2)}, u32[]{:S(2)}) collective-permute-start(f32[4,14,192]{2,0,1:T(4,128)S(1)} %add.22), channel_id=1, source_target_pairs={{0,4},{1,5},{2,6},{3,7},{4,0},{5,1},{6,2},{7,3},{8,12},{9,13},{10,... | collective-permute-start | bytes 129032 | tf_op jit(solution)/shard_map/ppermute | solution.py:41
  (56 other events, 153.9 us)

commit v2 on v1

--- a/solution.py
+++ b/solution.py
@@ -73,7 +73,7 @@
     return jax.ShapeDtypeStruct(dims, dtype)
 
 
-def call(kernel, operands, outs, scratch=(), after=(), limit=62, aliases=None):
+def call(kernel, operands, outs, scratch=(), after=(), limit=16, aliases=None):
     count = len(operands)
 
     def run(*refs):
@@ -101,24 +101,14 @@
     return list(results)
 
 
-def cut_kernel(begin, source, out):
-    out[...] = source[begin : begin + out.shape[0], :]
-
-
-def cut_rows(value, begin, count, after=()):
-    out = shape((count, value.shape[1]))
-    return call(partial(cut_kernel, begin), [(value, VMEM)], [out], after=after)[0]
-
-
-def add_kernel(*refs):
-    total = wide(refs[0][...])
-    for ref in refs[1:-1]:
-        total = total + wide(ref[...])
-    refs[-1][...] = total.astype(BF16)
-
-
-def add(items, after=()):
-    return call(add_kernel, [(item, VMEM) for item in items], [shape(items[0].shape)], after=after)[0]
+def flips_of(label, chips):
+    bits = chips.bit_length() - 1
+    return sum(((label >> i) & 1) << (bits - 1 - i) for i in range(bits)), label
+
+
+def flip_of(label, core, chips):
+    first, second = flips_of(label, chips)
+    return label if first == second else jnp.where(core == 0, first, second)
 
 
 def places_of(counts_ref, slots, images, chip, source, tok_count, seq_count):
@@ -161,7 +151,8 @@
     parts, halves, rest = refs[:chips], refs[chips : chips + len(groups)], refs[chips + len(groups) :]
     seq_index = lax.axis_index("seq")
     chip, core = seq_index // 2, seq_index % 2
-    for flip in range(chips):
+    for label in range(chips):
+        flip = flip_of(label, core, chips)
         micro, first, count, more, extra, _, _ = places_of(
             counts_ref, slots, images, chip ^ flip, seq_index, tok_count, seq_count
         )
@@ -170,7 +161,7 @@
         local, valid = local_rows_of(step, first, count, more, extra)
         pick = jnp.where(valid & (local == held), 1.0, 0.0).astype(BF16)
         start = pl.multiple_of(micro * tok_count, tok_count)
-        parts[flip][...] = dot(pick, values[pl.ds(start, tok_count), :]).astype(BF16)
+        parts[label][...] = dot(pick, values[pl.ds(start, tok_count), :]).astype(BF16)
     if smalls:
         first_half, inserted = rest
         half = (halves[0].shape[0] - EXTRA_ROWS) // 2
@@ -202,7 +193,8 @@
     seq_index = lax.axis_index("seq")
     micros = chips // slots
     sums = [None] * micros
-    for flip in range(chips):
+    for label in range(chips):
+        flip = flip_of(label, seq_index % 2, chips)
         micro, first, count, more, extra, _, _ = places_of(
             counts_ref, slots, images, seq_index // 2 ^ flip, seq_index, tok_count, seq_count
         )
@@ -210,7 +202,7 @@
         held = lax.broadcasted_iota(jnp.int32, (tok_count, capacity), 0)
         local, valid = local_rows_of(step, first, count, more, extra)
         pick = jnp.where(valid & (local == held), 1.0, 0.0).astype(BF16)
-        found = dot(pick, parts[flip][...])
+        found = dot(pick, parts[label][...])
         for m in range(micros):
             term = jnp.where(micro == m, found, 0.0)
             sums[m] = term if sums[m] is None else sums[m] + term
@@ -228,12 +220,13 @@
     for which in range(2):
         segment = jnp.full((rows, LANES), PAD_SEGMENT, jnp.int32)
         live = jnp.zeros((rows, LANES), jnp.int32)
-        for flip in range(chips):
+        for label in range(chips):
+            flip = flip_of(label, core ^ which, chips)
             source = 2 * (chip ^ flip) + (core ^ which)
             _, first, count, more, extra, total, ends = places_of(
                 counts_ref, slots, images, chip, source, tok_count, seq_count
             )
-            step = row - flip * capacity
+            step = row - label * capacity
             local, valid = local_rows_of(step, first, count, more, extra)
             valid = valid & (step >= 0) & (step < capacity)
             place = local * seq_count + source
@@ -395,7 +388,7 @@
         in_specs=[per_pair] * 5 + [marks, all_marks, marks] + [ANY] * len(after),
         out_specs=[out_pair, marks],
         out_shape=[shape((rows, pairs_here * LANES)), shape((rows, LANES), F32)],
-        compiler_params=pltpu.CompilerParams(vmem_limit_bytes=62 * MIB),
+        compiler_params=pltpu.CompilerParams(vmem_limit_bytes=16 * MIB),
     )(q, own_k, own_v, other_k, other_v, q_marks, k_marks, live, *after)
 
 
@@ -437,15 +430,10 @@
     lax.fori_loop(0, up_weight.shape[1] // width, widen, 0)
 
 
-def down_kernel(chips, tile, *refs):
-    active, slope, middle, vec, own = refs[:5]
-    pieces, cots, refs = refs[5:9], refs[9 : 9 + chips], refs[9 + chips :]
-    outs, refs = refs[:chips], refs[chips:]
-    hidden_grad, sums, up_shift_grad = refs[:3]
-    terms = refs[3:7]
-    cot_rows, down_in, weight, sems = refs[7:]
-    copies = stage(weight, own, pieces, 0, 0, sems)
-    rows, width = middle.shape
+def down_terms_kernel(chips, *refs):
+    active, vec, cots = refs[0], refs[1], refs[2 : 2 + chips]
+    cot_rows, down_in, sums = refs[2 + chips : 5 + chips]
+    terms = refs[5 + chips :]
     capacity = cots[0].shape[0]
     bias_sum = None
     for i, part in enumerate(cots):
@@ -455,7 +443,18 @@
         down_in[here, :] = scaled
         term = jnp.sum(scaled.astype(F32), axis=0, keepdims=True)
         bias_sum = term if i == 0 else bias_sum + term
+    sums[...] = bias_sum
     emit_terms(active, down_in, None, terms, 0)
+
+
+def down_kernel(chips, tile, *refs):
+    active, slope, middle, cot_rows, down_in, vec, own = refs[:7]
+    pieces, refs = refs[7:11], refs[11:]
+    outs, refs = refs[:chips], refs[chips:]
+    hidden_grad, sums, up_shift_grad, weight, sems = refs
+    copies = stage(weight, own, pieces, 0, 0, sems)
+    rows, width = middle.shape
+    capacity = outs[0].shape[0]
     wait_all(copies)
     scale_sum = None
     for i in range(chips):
@@ -464,8 +463,7 @@
         outs[i][...] = (middle[here, :] + vector(vec, SCALE_MLP) * found).astype(BF16)
         term = jnp.sum(cot_rows[here, :].astype(F32) * found, axis=0, keepdims=True)
         scale_sum = term if i == 0 else scale_sum + term
-    sums[0:1, :] = scale_sum
-    sums[1:2, :] = bias_sum
+    sums[...] = scale_sum
 
     def back(block, _):
         cols = pl.ds(pl.multiple_of(block * width, width), width)
@@ -483,17 +481,14 @@
     lax.fori_loop(0, hidden_grad.shape[1] // width, back, 0)
 
 
-def narrow_kernel(chips, tile, *refs):
+def narrow_kernel(tile, *refs):
     hidden_grad, middle, branch, vec, own_out, own_up = refs[:6]
-    pieces, cots, refs = refs[6:10], refs[10 : 10 + chips], refs[10 + chips :]
+    pieces, cot_rows, refs = refs[6:10], refs[10], refs[11:]
     middle_grad, branch_grad, attended_grad, sums = refs[:4]
-    cot_rows, out_weight, up_weight, out_sems, up_sems = refs[4:]
+    out_weight, up_weight, out_sems, up_sems = refs[4:]
     out_cols = own_out.shape[1]
     up_copies = stage(up_weight, own_up, pieces, out_cols, 0, up_sems)
     out_copies = stage(out_weight, own_out, pieces, 0, 0, out_sems)
-    capacity = cots[0].shape[0]
-    for i, part in enumerate(cots):
-        cot_rows[i * capacity : (i + 1) * capacity, :] = part[...]
     wait_all(up_copies)
     rows = middle.shape[0]
     totals = [None] * 4
@@ -605,7 +600,7 @@
         out_shape=[shape((rows, pairs_here * LANES))]
         + [shape((2, rows, pairs_here * LANES))] * 2,
         scratch_shapes=[pltpu.VMEM((2 * rows, LANES), F32)] * 2,
-        compiler_params=pltpu.CompilerParams(vmem_limit_bytes=62 * MIB),
+        compiler_params=pltpu.CompilerParams(vmem_limit_bytes=16 * MIB),
     )(q, own_k, own_v, other_k, other_v, q_marks, k_marks, live, attended, lse, grads, *after)
 
 
@@ -643,64 +638,51 @@
     return [shape((count, cols)) for count in (2 * rows, rows, rows // 2, rows // 2)]
 
 
-def far_kernel(keep_far, other, out):
-    half = out.shape[0]
-    out[...] = (wide(keep_far[...]) + wide(other[2 * half : 3 * half, :])).astype(BF16)
-
-
-def near_kernel(keep, other, far, out):
-    half = far.shape[0]
-    first = wide(keep[:half, :]) + wide(other[:half, :]) + wide(far[...])
-    out[:half, :] = first.astype(BF16)
-    second = wide(keep[half:, :]) + wide(other[half : 2 * half, :])
-    out[half:, :] = second.astype(BF16)
-
-
-def half_kernel(keep_own, other, near, both, out):
-    half = out.shape[0]
-    total = wide(keep_own[...]) + wide(other[3 * half :, :]) + wide(near[:half, :])
-    out[...] = (total + wide(both[...])).astype(BF16)
-
-
 class Reduction:
     def __init__(self, terms):
-        away, self.keep, self.keep_far, self.keep_own = terms
-        self.half = shape(self.keep_far.shape)
-        self.other = to_core(away)
-
-    def send_far(self, after=()):
-        operands = [(self.keep_far, VMEM), (self.other, VMEM)]
-        self.far_sent = call(far_kernel, operands, [self.half], after=after)[0]
-        self.far = to_fsdp(self.far_sent, (2, 1))
-
-    def send_near(self, after=()):
-        operands = [(self.keep, VMEM), (self.other, VMEM), (self.far, VMEM)]
-        self.near_sent = call(near_kernel, operands, [shape(self.keep.shape)], after=after)[0]
-        self.near = to_fsdp(self.near_sent, (1, 2))
-
-    def send_both(self, after=()):
-        count = self.half.shape[0]
-        self.both_sent = cut_rows(self.near, count, count, after)
-        self.both = to_core(self.both_sent)
-
-    def send_chips(self, after=()):
+        self.away, self.keep, self.keep_far, self.keep_own = terms
+        self.count = self.keep_far.shape[0]
+
+    def send_other(self):
+        self.other = to_core(self.away)
+        return [self.other]
+
+    def send_far(self):
+        part = self.other[2 * self.count : 3 * self.count]
+        self.far = to_fsdp((wide(self.keep_far) + wide(part)).astype(BF16), (2, 1))
+        return [self.far]
+
+    def send_near(self):
+        first = wide(self.keep[: self.count]) + wide(self.other[: self.count]) + wide(self.far)
+        second = wide(self.keep[self.count :]) + wide(self.other[self.count : 2 * self.count])
+        self.near = to_fsdp(jnp.concatenate([first, second], 0).astype(BF16), (1, 2))
+        return [self.near]
+
+    def send_both(self):
+        self.both = to_core(self.near[self.count :])
+        return [self.both]
+
+    def send_chips(self):
         flips = [1 << i for i in range((lax.axis_size("seq") // 2).bit_length() - 1)]
         self.orders = list(zip(flips, flips[::-1]))
-        operands = [(item, VMEM) for item in (self.keep_own, self.other, self.near, self.both)]
-        self.sent = call(half_kernel, operands, [self.half], after=after)[0]
+        total = wide(self.keep_own) + wide(self.other[3 * self.count :])
+        self.sent = (total + wide(self.near[: self.count]) + wide(self.both)).astype(BF16)
         self.got = to_chip(self.sent, *self.orders[0])
-
-    def send_chips_again(self, after=()):
+        return [self.got]
+
+    def send_chips_again(self):
         for order in self.orders[1:]:
-            self.sent = add([self.sent, self.got], after)
+            self.sent = (wide(self.sent) + wide(self.got)).astype(BF16)
             self.got = to_chip(self.sent, *order)
-
-    def send_total(self, after=()):
-        self.total = add([self.sent, self.got], after)
+        return [self.got]
+
+    def send_total(self):
+        self.total = (wide(self.sent) + wide(self.got)).astype(BF16)
         self.other_total = to_core(self.total)
+        return [self.other_total]
 
     def shards(self, widths, after=()):
-        outs = [shape((2 * self.half.shape[0], cols), F32) for cols in widths]
+        outs = [shape((2 * self.count, cols), F32) for cols in widths]
         operands = [(self.total, VMEM), (self.other_total, VMEM)]
         return call(spread_kernel, operands, outs, after=after)
 
@@ -737,11 +719,12 @@
 
 
 def input_kernel(chips, *refs):
-    projected_grad, x_rows, middle_grad, vec, own = refs[:5]
-    pieces, rest = refs[5:9], refs[9:]
+    projected_grad, x_rows, middle_grad, vec = refs[:4]
+    qkv_sums, narrow_sums, down_shift_grad, scale_grad, up_shift_grad, own = refs[4:10]
+    pieces, rest = refs[10:14], refs[14:]
     outs, sums, weight, sems = rest[:chips], rest[chips], rest[chips + 1], rest[chips + 2]
     copies = stage(weight, own, pieces, 0, EXTRA_ROWS, sems)
-    capacity = outs[0].shape[0]
+    capacity, width = outs[0].shape
     wait_all(copies)
     totals = [None] * 2
     for i in range(chips):
@@ -753,8 +736,22 @@
         for j, term in enumerate((grad * xhat, grad)):
             term = jnp.sum(term, axis=0, keepdims=True)
             totals[j] = term if i == 0 else totals[j] + term
-    sums[0:1, :] = totals[0]
-    sums[1:2, :] = totals[1]
+    sums[...] = jnp.zeros_like(sums)
+    for row, value in (
+        (LN1_GAIN, totals[0]),
+        (LN1_BIAS, totals[1]),
+        (QUERY_BIAS, qkv_sums[0:1, :]),
+        (VALUE_BIAS, qkv_sums[1:2, :]),
+        (OUT_BIAS, narrow_sums[3:4, :]),
+        (SCALE_ATTN, narrow_sums[2:3, :]),
+        (LN2_GAIN, narrow_sums[0:1, :]),
+        (LN2_BIAS, narrow_sums[1:2, :]),
+        (DOWN_BIAS, down_shift_grad[...]),
+        (SCALE_MLP, scale_grad[...]),
+    ):
+        sums[row : row + 1, :] = value
+    for f in range(4):
+        sums[UP_ROW + f : UP_ROW + f + 1, :] = up_shift_grad[:, f * width : (f + 1) * width]
 
 
 def body(
@@ -809,15 +806,30 @@
             [shape((capacity, width))] * chips + outs,
             [pltpu.VMEM((EXTRA_ROWS, width), F32)] if small else [],
             after=after,
+            limit=60 if small else 16,
         )
         parts = list(results[:chips])
         if send:
-            for flip in range(chips - 1, 0, -1):
-                parts[flip] = to_chip(parts[flip], flip)
+            for label in range(chips - 1, 0, -1):
+                parts[label] = to_chip(parts[label], *flips_of(label, chips))
         return parts, *results[chips:]
 
-    def send(parts):
-        return [parts[0]] + [to_chip(parts[flip], flip) for flip in range(1, chips)]
+    def cross(parts, bit):
+        labels = [label for label in range(chips) if label & bit]
+        return to_chip(jnp.concatenate([parts[label] for label in labels]), *flips_of(bit, chips))
+
+    def crossed(parts, moved, bit):
+        parts = list(parts)
+        for i, label in enumerate(label for label in range(chips) if label & bit):
+            parts[label] = moved[i * capacity : (i + 1) * capacity]
+        return parts
+
+    def cross_rest(parts):
+        bit = 2
+        while 2 * bit < chips:
+            parts = crossed(parts, cross(parts, bit), bit)
+            bit *= 2
+        return parts, cross(parts, bit), bit
 
     def collect(parts, after=()):
         return call(
@@ -862,28 +874,30 @@
             pltpu.SemaphoreType.DMA((4,)),
         ],
     )
+    down_sent, *cot_sent = hold([down_sent] + cot_sent, [q])
+    down_near = to_fsdp(down_sent, (1, 2))
+    cot_moved = cross(cot_sent, 1)
     attention = (q, own_k, own_v, to_core(own_k), to_core(own_v), q_marks, k_marks, live)
     step = width // LANES // 3
     attended_parts, lses = [], []
 
-    def forward(i, after=()):
-        part, lse = attend_forward(i * step, step, *attention, after=attended_parts[-1:] + list(after))
+    def forward(i):
+        part, lse = attend_forward(i * step, step, *attention, after=attended_parts[-1:])
         attended_parts.append(part)
         lses.append(lse)
-
-    forward(0)
-    up_near, down_sent, *cot_sent = hold([up_near, down_sent] + cot_sent, attended_parts[-1:])
-    cot_parts = send(cot_sent)
-    up_first = cut_rows(up_near, 0, own_rows // 2)
-    up_far = to_fsdp(up_first, (2, 1))
-    down_near = to_fsdp(down_sent, (1, 2))
-    forward(1, [up_first])
-    up_far, *cot_parts = hold([up_far] + cot_parts, attended_parts[-1:])
+        return part
+
+    up_near, cot_moved = hold([up_near, cot_moved], [forward(0)])
+    cot_parts = crossed(cot_sent, cot_moved, 1)
+    up_far = to_fsdp(up_near[: own_rows // 2], (2, 1))
+    cot_parts, cot_moved, last_bit = cross_rest(cot_parts)
+    up_far, down_near, cot_moved = hold([up_far, down_near, cot_moved], [forward(1)])
+    cot_parts = crossed(cot_parts, cot_moved, last_bit)
     up_pieces = [up_near, to_core(up_near), up_far, to_core(up_far)]
-    forward(2, [up_far])
-    down_near = hold([down_near], attended_parts[-1:])[0]
-    down_first = cut_rows(down_near, 0, down_weight.shape[0] // 2)
-    down_far = to_fsdp(down_first, (2, 1))
+    down_far = to_fsdp(down_near[: down_weight.shape[0] // 2], (2, 1))
+    up_pieces = hold(up_pieces, [forward(2)])
+    (down_near,) = hold([down_near], up_pieces)
+    down_other = to_core(down_near)
 
     up_scratch = [
         pltpu.VMEM((width, width), BF16),
@@ -904,145 +918,163 @@
             shape((rows, hidden_width)),
         ],
         up_scratch,
-        after=[down_first],
-    )
-    down_far = hold([down_far], [attended])[0]
-    down_pieces = [down_near, to_core(down_near), down_far, to_core(down_far)]
+    )
+    down_far, down_other = hold([down_far, down_other], [attended])
+    far_other = to_core(down_far)
+    cot_rows, down_in, down_shift_grad, *down_terms = call(
+        partial(down_terms_kernel, chips),
+        [(item, VMEM) for item in [active, vec] + cot_parts],
+        [shape((rows, width)), shape((rows, width)), shape((1, width), F32)]
+        + term_shapes(down_weight.shape[0], width),
+        after=[down_far],
+    )
+    down = Reduction(down_terms)
+    down_pieces = [down_near, down_other, down_far, far_other]
+    down.away, *down_pieces = hold([down.away] + down_pieces, [down_in])
+    waits = down.send_other()
     results = call(
         partial(down_kernel, chips, tile),
-        [(item, VMEM) for item in (active, slope, middle, vec)]
-        + [(item, ANY) for item in [down_weight] + down_pieces]
-        + [(part, VMEM) for part in cot_parts],
+        [(item, VMEM) for item in (active, slope, middle, cot_rows, down_in, vec)]
+        + [(item, ANY) for item in [down_weight] + down_pieces],
         [shape((capacity, width))] * chips
         + [
             shape((rows, hidden_width)),
-            shape((2, width), F32),
+            shape((1, width), F32),
             shape((1, hidden_width), F32),
-        ]
-        + term_shapes(down_weight.shape[0], width),
-        [
-            pltpu.VMEM((rows, width), BF16),
-            pltpu.VMEM((rows, width), BF16),
-            pltpu.VMEM((hidden_width, width), BF16),
-            STAGE_SEMS,
         ],
-    )
-    out_sent, results = results[:chips], results[chips:]
-    hidden_grad, down_sums, up_shift_grad, *down_terms = results
-    down = Reduction(down_terms)
-    out_parts = send(out_sent)
+        [pltpu.VMEM((hidden_width, width), BF16), STAGE_SEMS],
+    )
+    out_sent, (hidden_grad, scale_grad, up_shift_grad) = list(results[:chips]), results[chips:]
+    (down.other,) = hold(waits, [hidden_grad])
+    waits = down.send_far()
 
     middle_grad, branch_grad, attended_grad, narrow_sums = call(
-        partial(narrow_kernel, chips, tile),
+        partial(narrow_kernel, tile),
         [(item, VMEM) for item in (hidden_grad, middle, branch, vec)]
         + [(item, ANY) for item in [out_weight, up_weight] + up_pieces]
-        + [(part, VMEM) for part in cot_parts],
+        + [(cot_rows, VMEM)],
         [
             shape((rows, width), F32),
             shape((rows, width)),
             shape((rows, width)),
             shape((4, width), F32),
         ],
-        [pltpu.VMEM((rows, width), BF16)] + up_scratch,
-    )
-    down.send_far([middle_grad])
+        up_scratch,
+    )
+    down.far, *out_sent = hold(waits + out_sent, [middle_grad])
+    waits = down.send_near()
+    out_moved = cross(out_sent, 1)
     up_terms = call(
         up_terms_kernel,
         [(item, VMEM) for item in (hidden_grad, normed_second, branch_grad, attended)],
         term_shapes(own_rows, hidden_width + width),
         [pltpu.VMEM((width, hidden_width), F32), pltpu.VMEM((width, width), F32)],
-        after=[down.far_sent],
     )
     up = Reduction(up_terms)
-    down.send_near([up_terms[0]])
 
     query_grads, own_grads, other_grads = [], [], []
 
-    def backward(first, count, after):
+    def backward(first, after=()):
         query_grad, own_grad, other_grad = attend_backward(
             first,
-            count,
+            1,
             first % step,
             *attention,
             attended_parts[first // step],
             lses[first // step],
             attended_grad,
-            after=after + query_grads[-1:],
+            after=query_grads[-1:] + list(after),
         )
         query_grads.append(query_grad)
         own_grads.append(own_grad)
-        other_grads.append(to_core(other_grad))
-
-    backward(0, 1, [down.near_sent])
-    up.send_far(query_grads[-1:])
-    out_parts = hold(out_parts, query_grads[-1:])
-    backward(1, 1, [up.far_sent, out_parts[-1]])
-    down.send_both(query_grads[-1:])
-    backward(2, 1, [down.both_sent])
-    down.send_chips(query_grads[-1:])
-    up.send_near(query_grads[-1:])
-    backward(3, 1, [down.sent, up.near_sent])
-    backward(4, 1, [])
-    down.send_chips_again(query_grads[-1:])
-    up.send_both(query_grads[-1:])
-    backward(5, 1, [down.sent, up.both_sent])
-    up.send_chips(query_grads[-1:])
+        other_grads.append(other_grad)
+        return query_grad
+
+    def hold_grads(arrays):
+        first, count = sent_grads[0], len(arrays)
+        items = hold(list(arrays) + other_grads[first:], query_grads[-1:])
+        other_grads[first:] = items[count:]
+        sent_grads[0] = len(other_grads)
+        return items[:count], [to_core(item) for item in other_grads[first:]]
+
+    sent_grads = [0]
+    core_grads = []
+
+    backward(0, up_terms[:1])
+    (down.near, up.away, out_moved), moved = hold_grads(waits + [up.away, out_moved])
+    out_parts = crossed(out_sent, out_moved, 1)
+    waits = down.send_both() + up.send_other() + moved
+    out_parts, out_moved, _ = cross_rest(out_parts)
+    backward(1)
+    (down.both, up.other, *core_grads), fresh = hold_grads(waits)
+    waits = down.send_chips() + up.send_far() + [out_moved] + fresh
+    backward(2)
+    backward(3)
+    (down.got, up.far, out_moved, *more), fresh = hold_grads(waits)
+    out_parts = crossed(out_parts, out_moved, last_bit)
+    core_grads += more
+    waits = up.send_near() + down.send_chips_again() + fresh
+    backward(4)
+    backward(5)
+    (up.near, down.got, *more), fresh = hold_grads(waits)
+    core_grads += more
+    (up.both, *more) = hold(up.send_both() + fresh, [])
+    core_grads += more
+    got = up.send_chips()
+    waits = down.send_total()
 
     projected_grad, qkv_sums, *qkv_terms = call(
         partial(project_grad_kernel, len(query_grads)),
-        [(item, VMEM) for item in query_grads + own_grads + other_grads + [normed_first]],
+        [(item, VMEM) for item in query_grads + own_grads + core_grads + [normed_first]],
         [shape((rows, 3 * width)), shape((2, width), F32)] + term_shapes(own_rows, 3 * width),
         [pltpu.VMEM((width, 3 * width), F32)],
-        after=[up.sent],
-    )
+    )
+    output = collect(out_parts, [projected_grad])
+    (down.other_total,) = hold(waits, [output])
+    (down_grad,) = down.shards([width])
     qkv = Reduction(qkv_terms)
-    down.send_total([projected_grad])
-    qkv.send_far([down.total])
-    *in_sent, input_sums = call(
+    (qkv.away,) = hold([qkv.away], [projected_grad])
+    (qkv.other,) = hold(qkv.send_other(), [])
+    waits = qkv.send_far()
+    *in_sent, sums = call(
         partial(input_kernel, chips),
         [(item, VMEM) for item in (projected_grad, x_rows, middle_grad, vec)]
+        + [(item, VMEM) for item in (qkv_sums, narrow_sums, down_shift_grad, scale_grad, up_shift_grad)]
         + [(item, ANY) for item in [qkv_weight] + qkv_pieces],
-        [shape((capacity, width))] * chips + [shape((2, width), F32)],
+        [shape((capacity, width))] * chips + [shape((EXTRA_ROWS, width), F32)],
         [pltpu.VMEM((width, 3 * width), BF16), STAGE_SEMS],
-        after=[qkv.far_sent],
-    )
-    up.send_chips_again([input_sums])
-    qkv.send_near([input_sums])
-    in_parts = send(in_sent)
-    output = collect(out_parts, [qkv.near_sent])
-    (down_grad,) = down.shards([width], [output])
-    qkv.send_both([down_grad])
-    qkv.send_chips()
+    )
+    qkv.far, up.got, sums, *in_sent = hold(waits + got + [sums] + in_sent, [down_grad])
+    waits = qkv.send_near()
+    got = up.send_chips_again()
+    in_moved = cross(in_sent, 1)
+    other_sums = to_core(sums)
+    qkv.near, sums, other_sums, in_moved = hold(waits + [sums, other_sums, in_moved], [])
+    sums = sums + other_sums
+    other_sums = to_fsdp(sums, (1, 1))
+    in_parts, in_moved, _ = cross_rest(crossed(in_sent, in_moved, 1))
+    (qkv.both,) = hold(qkv.send_both(), [])
+    waits = qkv.send_chips()
+    qkv.got, up.got, sums, other_sums = hold(waits + got + [sums, other_sums], [])
+    sums = sums + other_sums
+    other_sums = to_fsdp(sums, (2, 2))
+    waits = qkv.send_chips_again()
+    (in_moved,) = hold([in_moved], [])
+    input_grad = collect(crossed(in_parts, in_moved, last_bit))
     up.send_total()
-    up_grad, out_grad = up.shards([hidden_width, width], [qkv.sent])
-    qkv.send_chips_again([up_grad])
-    input_grad = collect(in_parts, [qkv.sent])
-    qkv.send_total([input_grad])
+    up_grad, out_grad = up.shards([hidden_width, width])
+    qkv.got, sums, other_sums = hold(waits + [sums, other_sums], [input_grad, up_grad])
+    sums = sums + other_sums
+    flip = 1
+    while flip < chips:
+        sums = sums + to_chip(sums, flip)
+        flip *= 2
+    qkv.send_total()
     (qkv_grad,) = qkv.shards([3 * width])
     output, input_grad = output.reshape(tokens.shape), input_grad.reshape(tokens.shape)
 
-    vector_grads = jnp.concatenate(
-        [
-            input_sums,
-            qkv_sums,
-            narrow_sums[3:4],
-            narrow_sums[2:3],
-            narrow_sums[0:2],
-            down_sums[1:2],
-            down_sums[0:1],
-        ]
-    )
-    vector_grads = jnp.transpose(vector_grads.reshape(10, 4, -1), (1, 0, 2))
-    vector_grads = jnp.concatenate([vector_grads, up_shift_grad.reshape(4, 4, -1)], 1)
-    vector_grads = vector_grads + to_core(vector_grads)
-    for flip in (1, 2):
-        vector_grads = vector_grads + to_fsdp(vector_grads, (flip, flip))
-    step = 1
-    while step < chips:
-        vector_grads = vector_grads + to_chip(vector_grads, step)
-        step *= 2
-    small_grads = lax.dynamic_index_in_dim(vector_grads, fsdp_index, 0, keepdims=False)
-
+    small_grads = lax.dynamic_slice_in_dim(sums[:UP_ROW], fsdp_index * own_rows, own_rows, 1)
+    up_shift_total = lax.dynamic_index_in_dim(sums, UP_ROW + fsdp_index, 0, keepdims=False)
     return (
         output,
         input_grad,
@@ -1057,7 +1089,7 @@
         small_grads[LN2_GAIN],
         small_grads[LN2_BIAS],
         up_grad,
-        small_grads[10:].reshape(-1),
+        up_shift_total,
         down_grad,
         small_grads[DOWN_BIAS],
         small_grads[SCALE_MLP],

time: 449 us -> 294 us (0.65)
  Pallas kernels: 239 us -> 125 us
  waiting for transfers between devices: 126 us -> 102 us
  local copies, waits for them, and re-layouts: 22.8 us -> 9.39 us
  starting transfers between devices: 53.4 us -> 48.8 us
    pallas_call x40 -> x39, Pallas kernels: 158 us -> 62 us  [call(): pl.pallas_call(run, in_specs=[spec for _, spec in operands] + [ANY] * len...]
    ppermute x58 -> x55, waiting for transfers between devices: 126 us -> 102 us  [move(): return lax.ppermute(value, BOTH, pairs)]
    unnamed x92 -> x48, local copies, waits for them, and re-layouts: 20.7 us -> 7.72 us
    pallas_call x6, Pallas kernels: 50.4 us -> 37.5 us  [attend_backward(): pl.pallas_call(ignoring(partial(attend_backward_kernel, 4, skipped), 11,...]
    pallas_call x3, Pallas kernels: 30.9 us -> 25.5 us  [attend_forward(): pl.pallas_call(ignoring(partial(attend_forward_kernel, 4), 8, len(after))...]
    ppermute x58 -> x55, starting transfers between devices: 53.4 us -> 48.8 us  [move(): return lax.ppermute(value, BOTH, pairs)]
  transfers between devices with their start and end apart: 58 -> 55, of which waited for: 23 -> 23; matrix products, arithmetic and copies ran while one was open for 1% -> 1% of each run, Pallas kernels for 41% -> 40%
where the time goes in v2:
time: 294 us; the launch traced here: 291 us
  Pallas kernels  125 us (43%)
  waiting for transfers between devices  102 us (35%)
  starting transfers between devices  48.8 us (17%)
  local copies, waits for them, and re-layouts  9.39 us (3%)
  other arithmetic  3.9 us (1%)
    ppermute x55, waiting for transfers between devices, move(): return lax.ppermute(value, BOTH, pairs)  102 us
    pallas_call x39, Pallas kernels, call(): pl.pallas_call(run, in_specs=[spec for _, spec in operands] + [ANY] * len...  62 us
    ppermute x55, starting transfers between devices, move(): return lax.ppermute(value, BOTH, pairs)  48.8 us
    pallas_call x6, Pallas kernels, attend_backward(): pl.pallas_call(ignoring(partial(attend_backward_kernel, 4, skipped), 11,...  37.5 us
    pallas_call x3, Pallas kernels, attend_forward(): pl.pallas_call(ignoring(partial(attend_forward_kernel, 4), 8, len(after))...  25.5 us
    unnamed x48, local copies, waits for them, and re-layouts  7.72 us
  transfers between devices with their start and end apart: 55, of which 23 were waited for; matrix products, arithmetic and copies ran while one was open for 1% of the time, Pallas kernels for 40%

profile of v2, /device:TPU:0, one launch (start us, length us, event | category | flops | bytes accessed | tf_op | source)
XLA Modules:
  0.0 290.8 jit_solution(785070441378449777)
XLA Ops:
  0.7 3.3 %shard_map.305 = (bf16[144,768]{1,0:T(8,128)(2,1)}, bf16[144,768]{1,0:T(8,128)(2,1)}, bf16[144,768]{1,0:T(8,128)(2,1)}, bf16[144,768]{1,0:T(8,128)(2,1)}, bf16[2...) custom-call(s32[2,1,2,3]{3,2,1,0:T(2,128)} %refs_0_.7, bf16[512,768]{1,0:T(8,128)(2,1)} %bitcast.22, ...), custom_call_target="tpu_custom_call" | custom-call | tf_op jit(solution)/shard_map/pallas_call | solution.py:82
  4.0 2.9 %collective-permute-start.3 = (bf16[208,2304]{1,0:T(8,128)(2,1)}, bf16[208,2304]{1,0:T(8,128)(2,1)S(1)}, u32[]{:S(2)}, u32[]{:S(2)}) collective-permute-start(bf16[208,2304]{1,0:T(8,128)(2,1)} %get-tuple-element.178.refs_5_.refs_4_), channel_id=1, source_target_pairs={{0,8},{1,17},{2,10},{3,19},{4,12},{5,21},{6,14},{7,23},{8,0},{9,25... | collective-permute-start | bytes 2875400 | tf_op jit(solution)/shard_map/ppermute | solution.py:41
  8.5 2.6 collective-permute-start
  16.5 1.8 shard_map.306
  18.3 9.0 %collective-permute-done.refs_4_.refs_1_ = bf16[144,768]{1,0:T(8,128)(2,1)S(1)} collective-permute-done((bf16[144,768]{1,0:T(8,128)(2,1)}, bf16[144,768]{1,0:T(8,128)(2,1)S(1)}, u32[]{:S(2)}, u32[]{:S(2)}) %collective-permute-start) | collective-permute-done | bytes 221216 | tf_op jit(solution)/shard_map/ppermute | solution.py:41
  27.3 4.2 %collective-permute-done.4.refs_1_ = bf16[112,2304]{1,0:T(8,128)(2,1)S(1)} collective-permute-done((bf16[112,2304]{1,0:T(8,128)(2,1)}, bf16[112,2304]{1,0:T(8,128)(2,1)S(1)}, u32[]{:S(2)}, u32[]{:S(2)}) %collective-permute-start.4) | collective-permute-done | bytes 516128 | tf_op jit(solution)/shard_map/ppermute | solution.py:41
  33.2 1.9 collective-permute-done.6.refs_9_.refs_13_
  35.1 5.3 %shard_map.308 = (bf16[576,768]{1,0:T(8,128)(2,1)S(1)}, bf16[576,768]{1,0:T(8,128)(2,1)S(1)}, bf16[576,768]{1,0:T(8,128)(2,1)S(1)}, bf16[576,768]{1,0:T(8,128)(2...) custom-call(bf16[144,768]{1,0:T(8,128)(2,1)S(1)} %copy-done.20, ...), custom_call_target="tpu_custom_call" | custom-call | tf_op jit(solution)/shard_map/pallas_call | solution.py:82
  41.4 2.7 collective-permute-start.10
  45.3 8.3 %shard_map.309 = (bf16[576,256]{1,0:T(8,128)(2,1)S(1)}, f32[576,128]{1,0:T(8,128)S(1)}) custom-call(bf16[576,768]{1,0:T(8,128)(2,1)S(1)} %get-tuple-element.184.refs_0_.refs_5_, bf16[576,768]{1,0:T(8,128)(2,1)S(1)} %get-tuple-element.185.refs_1_, bf16[576,768]{1,0:T(8,128)(2,1)S(1)} %get-tuple-element.186.refs_2_, ...), custom_call_target="tpu_custom_call" | custom-call | tf_op jit(solution)/shard_map/pallas_call | solution.py:385
  55.3 1.8 collective-permute-start.14
  57.1 8.3 %shard_map.310 = (bf16[576,256]{1,0:T(8,128)(2,1)S(1)}, f32[576,128]{1,0:T(8,128)S(1)}) custom-call(bf16[576,768]{1,0:T(8,128)(2,1)S(1)} %get-tuple-element.184.refs_0_.refs_5_, bf16[576,768]{1,0:T(8,128)(2,1)S(1)} %get-tuple-element.185.refs_1_, bf16[576,768]{1,0:T(8,128)(2,1)S(1)} %get-tuple-element.186.refs_2_, ...), custom_call_target="tpu_custom_call" | custom-call | tf_op jit(solution)/shard_map/pallas_call | solution.py:385
  65.5 4.2 %collective-permute-done.13.refs_1_ = bf16[768,768]{1,0:T(8,128)(2,1)S(1)} collective-permute-done((bf16[768,768]{1,0:T(8,128)(2,1)S(1)}, bf16[768,768]{1,0:T(8,128)(2,1)S(1)}, u32[]{:S(2)}, u32[]{:S(2)}) %collective-permute-start.13) | collective-permute-done | bytes 1179680 | tf_op jit(solution)/shard_map/ppermute | solution.py:41
  71.4 8.9 %shard_map.311 = (bf16[576,256]{1,0:T(8,128)(2,1)S(1)}, f32[576,128]{1,0:T(8,128)S(1)}) custom-call(bf16[576,768]{1,0:T(8,128)(2,1)S(1)} %get-tuple-element.184.refs_0_.refs_5_, bf16[576,768]{1,0:T(8,128)(2,1)S(1)} %get-tuple-element.185.refs_1_, bf16[576,768]{1,0:T(8,128)(2,1)S(1)} %get-tuple-element.186.refs_2_, ...), custom_call_target="tpu_custom_call" | custom-call | tf_op jit(solution)/shard_map/pallas_call | solution.py:385
  81.4 8.2 %shard_map.316 = (bf16[576,768]{1,0:T(8,128)(2,1)S(1)}, f32[576,768]{1,0:T(8,128)S(1)}, f32[576,768]{1,0:T(8,128)S(1)}, bf16[576,768]{1,0:T(8,128)(2,1)S(1)}, bf...) custom-call(bf16[576,256]{1,0:T(8,128)(2,1)S(1)} %get-tuple-element.189.refs_8_.refs_2_.refs_0_, ...), custom_call_target="tpu_custom_call" | custom-call | tf_op jit(solution)/shard_map/pallas_call | solution.py:82
  90.8 4.0 %shard_map.319 = (bf16[576,768]{1,0:T(8,128)(2,1)S(1)}, bf16[576,768]{1,0:T(8,128)(2,1)S(1)}, f32[1,768]{1,0:T(1,128)S(1)}, bf16[1536,768]{1,0:T(8,128)(2,1)S(1)...) custom-call(bf16[576,3072]{1,0:T(8,128)(2,1)S(1)} %get-tuple-element.212.refs_0_, ...), custom_call_target="tpu_custom_call" | custom-call | tf_op jit(solution)/shard_map/pallas_call | solution.py:82
  96.0 8.1 %shard_map.321 = (bf16[144,768]{1,0:T(8,128)(2,1)S(1)}, bf16[144,768]{1,0:T(8,128)(2,1)S(1)}, bf16[144,768]{1,0:T(8,128)(2,1)S(1)}, bf16[144,768]{1,0:T(8,128)(2...) custom-call(bf16[576,3072]{1,0:T(8,128)(2,1)S(1)} %get-tuple-element.212.refs_0_, ...), custom_call_target="tpu_custom_call" | custom-call | tf_op jit(solution)/shard_map/pallas_call | solution.py:82
  105.7 6.0 %shard_map.323 = (f32[576,768]{1,0:T(8,128)S(1)}, bf16[576,768]{1,0:T(8,128)(2,1)S(1)}, bf16[576,768]{1,0:T(8,128)(2,1)S(1)}, f32[4,768]{1,0:T(4,128)S(1)}) custom-call(bf16[576,3072]{1,0:T(8,128)(2,1)S(1)} %get-tuple-element.230.refs_1_.refs_0_, f32[576,768]{1,0:T(8,128)S(1)} %get-tuple-element.224.refs_2_.refs_1_, ...), custom_call_target="tpu_custom_call" | custom-call | tf_op jit(solution)/shard_map/pallas_call | solution.py:82
  111.7 2.6 collective-permute-done.20.refs_0_
  116.4 2.6 collective-permute-start.22
  119.0 5.4 %shard_map.325 = (bf16[384,3840]{1,0:T(8,128)(2,1)S(1)}, bf16[192,3840]{1,0:T(8,128)(2,1)S(1)}, bf16[96,3840]{1,0:T(8,128)(2,1)S(1)}, bf16[96,3840]{1,0:T(8,128)(2,1)S(1)}) custom-call(bf16[576,3072]{1,0:T(8,128)(2,1)S(1)} %get-tuple-element.230.refs_1_.refs_0_, bf16[576,768]{1,0:T(8,128)(2,1)S(1)} %copy-done.17, ...), custom_call_target="tpu_custom_call" | custom-call | tf_op jit(solution)/shard_map/pallas_call | solution.py:82
  124.4 6.3 %shard_map.326 = (bf16[576,128]{1,0:T(8,128)(2,1)S(1)}, bf16[2,576,128]{2,1,0:T(8,128)(2,1)S(1)}, bf16[2,576,128]{2,1,0:T(8,128)(2,1)S(1)}) custom-call(bf16[576,768]{1,0:T(8,128)(2,1)S(1)} %get-tuple-element.184.refs_0_.refs_5_, bf16[576,768]{1,0:T(8,128)(2,1)S(1)} %get-tuple-element.185.refs_1_, bf16[576,768]{1,0:T(8,128)(2,1)S(1)} %get-tuple-element.186.refs_2_, ...), custom_call_target="tpu_custom_call" | custom-call | tf_op jit(solution)/shard_map/pallas_call | solution.py:594
  131.8 6.1 %shard_map.328 = (bf16[576,128]{1,0:T(8,128)(2,1)S(1)}, bf16[2,576,128]{2,1,0:T(8,128)(2,1)S(1)}, bf16[2,576,128]{2,1,0:T(8,128)(2,1)S(1)}) custom-call(bf16[576,768]{1,0:T(8,128)(2,1)S(1)} %get-tuple-element.184.refs_0_.refs_5_, bf16[576,768]{1,0:T(8,128)(2,1)S(1)} %get-tuple-element.185.refs_1_, bf16[576,768]{1,0:T(8,128)(2,1)S(1)} %get-tuple-element.186.refs_2_, ...), custom_call_target="tpu_custom_call" | custom-call | tf_op jit(solution)/shard_map/pallas_call | solution.py:594
  142.7 6.5 %shard_map.330 = (bf16[576,128]{1,0:T(8,128)(2,1)S(1)}, bf16[2,576,128]{2,1,0:T(8,128)(2,1)S(1)}, bf16[2,576,128]{2,1,0:T(8,128)(2,1)S(1)}) custom-call(bf16[576,768]{1,0:T(8,128)(2,1)S(1)} %get-tuple-element.184.refs_0_.refs_5_, bf16[576,768]{1,0:T(8,128)(2,1)S(1)} %get-tuple-element.185.refs_1_, bf16[576,768]{1,0:T(8,128)(2,1)S(1)} %get-tuple-element.186.refs_2_, ...), custom_call_target="tpu_custom_call" | custom-call | tf_op jit(solution)/shard_map/pallas_call | solution.py:594
  149.2 6.1 %shard_map.331 = (bf16[576,128]{1,0:T(8,128)(2,1)S(1)}, bf16[2,576,128]{2,1,0:T(8,128)(2,1)S(1)}, bf16[2,576,128]{2,1,0:T(8,128)(2,1)S(1)}) custom-call(bf16[576,768]{1,0:T(8,128)(2,1)S(1)} %get-tuple-element.184.refs_0_.refs_5_, bf16[576,768]{1,0:T(8,128)(2,1)S(1)} %get-tuple-element.185.refs_1_, bf16[576,768]{1,0:T(8,128)(2,1)S(1)} %get-tuple-element.186.refs_2_, ...), custom_call_target="tpu_custom_call" | custom-call | tf_op jit(solution)/shard_map/pallas_call | solution.py:594
  155.3 10.2 %collective-permute-done.28.refs_2_ = bf16[288,768]{1,0:T(8,128)(2,1)S(1)} collective-permute-done((bf16[288,768]{1,0:T(8,128)(2,1)S(1)}, bf16[288,768]{1,0:T(8,128)(2,1)S(1)}, u32[]{:S(2)}, u32[]{:S(2)}) %collective-permute-start.28) | collective-permute-done | bytes 442400 | tf_op jit(solution)/shard_map/ppermute | solution.py:41
  166.5 3.0 %collective-permute-start.31 = (bf16[384,768]{1,0:T(8,128)(2,1)S(1)}, bf16[384,768]{1,0:T(8,128)(2,1)S(1)}, u32[]{:S(2)}, u32[]{:S(2)}) collective-permute-start(bf16[384,768]{1,0:T(8,128)(2,1)S(1)} %add_convert_fusion.7), channel_id=1, source_target_pairs={{0,4},{1,3},{2,6},{3,1},{4,0},{5,7},{6,2},{7,5},{8,12},{9,11},{10,... | collective-permute-start | bytes 1769480 | tf_op jit(solution)/shard_map/ppermute | solution.py:41
  170.0 6.3 %shard_map.333 = (bf16[576,128]{1,0:T(8,128)(2,1)S(1)}, bf16[2,576,128]{2,1,0:T(8,128)(2,1)S(1)}, bf16[2,576,128]{2,1,0:T(8,128)(2,1)S(1)}) custom-call(bf16[576,768]{1,0:T(8,128)(2,1)S(1)} %get-tuple-element.184.refs_0_.refs_5_, bf16[576,768]{1,0:T(8,128)(2,1)S(1)} %get-tuple-element.185.refs_1_, bf16[576,768]{1,0:T(8,128)(2,1)S(1)} %get-tuple-element.186.refs_2_, ...), custom_call_target="tpu_custom_call" | custom-call | tf_op jit(solution)/shard_map/pallas_call | solution.py:594
  176.3 6.1 %shard_map.334 = (bf16[576,128]{1,0:T(8,128)(2,1)S(1)}, bf16[2,576,128]{2,1,0:T(8,128)(2,1)S(1)}, bf16[2,576,128]{2,1,0:T(8,128)(2,1)S(1)}) custom-call(bf16[576,768]{1,0:T(8,128)(2,1)S(1)} %get-tuple-element.184.refs_0_.refs_5_, bf16[576,768]{1,0:T(8,128)(2,1)S(1)} %get-tuple-element.185.refs_1_, bf16[576,768]{1,0:T(8,128)(2,1)S(1)} %get-tuple-element.186.refs_2_, ...), custom_call_target="tpu_custom_call" | custom-call | tf_op jit(solution)/shard_map/pallas_call | solution.py:594
  182.5 3.1 %collective-permute-done.30.refs_0_ = bf16[192,3840]{1,0:T(8,128)(2,1)S(1)} collective-permute-done((bf16[192,3840]{1,0:T(8,128)(2,1)S(1)}, bf16[192,3840]{1,0:T(8,128)(2,1)S(1)}, u32[]{:S(2)}, u32[]{:S(2)}) %collective-permute-start.30) | collective-permute-done | bytes 1474592 | tf_op jit(solution)/shard_map/ppermute | solution.py:41
  186.3 2.0 collective-permute-done.35.refs_1_
  188.7 3.7 %shard_map.337 = (bf16[576,2304]{1,0:T(8,128)(2,1)S(1)}, f32[2,768]{1,0:T(2,128)S(1)}, bf16[384,2304]{1,0:T(8,128)(2,1)S(1)}, bf16[192,2304]{1,0:T(8,128)(2,1)S(...) custom-call(bf16[576,128]{1,0:T(8,128)(2,1)S(1)} %get-tuple-element.248.refs_4_.refs_11_.refs_0_, ...), custom_call_target="tpu_custom_call" | custom-call | tf_op jit(solution)/shard_map/pallas_call | solution.py:82
  197.0 2.2 shard_map.338.refs_1_
  202.0 7.1 %shard_map.341 = (bf16[144,768]{1,0:T(8,128)(2,1)S(1)}, bf16[144,768]{1,0:T(8,128)(2,1)S(1)}, bf16[144,768]{1,0:T(8,128)(2,1)S(1)}, bf16[144,768]{1,0:T(8,128)(2,1)S(1)}, f32[16,768]{1,0:T(8,128)S(1)}) custom-call(bf16[576,2304]{1,0:T(8,128)(2,1)S(1)} %get-tuple-element.293.refs_5_.refs_1_.refs_0_, bf16[576,768]{1,0:T(8,128)(2,1)S(1)} %copy-done.8, ...), custom_call_target="tpu_custom_call" | custom-call | tf_op jit(solution)/shard_map/pallas_call | solution.py:82
  209.1 4.0 %collective-permute-done.39.refs_1_ = bf16[96,3840]{1,0:T(8,128)(2,1)S(1)} collective-permute-done((bf16[96,3840]{1,0:T(8,128)(2,1)S(1)}, bf16[96,3840]{1,0:T(8,128)(2,1)S(1)}, u32[]{:S(2)}, u32[]{:S(2)}) %collective-permute-start.39) | collective-permute-done | bytes 737312 | tf_op jit(solution)/shard_map/ppermute | solution.py:41
  214.0 2.7 collective-permute-start.43
  217.9 10.2 %collective-permute-done.43.refs_3_ = bf16[288,768]{1,0:T(8,128)(2,1)S(1)} collective-permute-done((bf16[288,768]{1,0:T(8,128)(2,1)S(1)}, bf16[288,768]{1,0:T(8,128)(2,1)S(1)}, u32[]{:S(2)}, u32[]{:S(2)}) %collective-permute-start.43) | collective-permute-done | bytes 442400 | tf_op jit(solution)/shard_map/ppermute | solution.py:41
  230.2 3.1 %collective-permute-start.46 = (bf16[96,2304]{1,0:T(8,128)(2,1)S(1)}, bf16[96,2304]{1,0:T(8,128)(2,1)S(1)}, u32[]{:S(2)}, u32[]{:S(2)}) collective-permute-start(bf16[96,2304]{1,0:T(8,128)(2,1)S(1)} %add_convert_fusion.14), channel_id=1, source_target_pairs={{0,2},{1,5},{2,0},{3,7},{4,6},{5,1},{6,4},{7,3},{8,10},{9,13},{10,... | collective-permute-start | bytes 1327112 | tf_op jit(solution)/shard_map/ppermute | solution.py:41
  233.9 27.4 %collective-permute-done.47.refs_1_ = bf16[96,3840]{1,0:T(8,128)(2,1)S(1)} collective-permute-done((bf16[96,3840]{1,0:T(8,128)(2,1)S(1)}, bf16[96,3840]{1,0:T(8,128)(2,1)S(1)}, u32[]{:S(2)}, u32[]{:S(2)}) %collective-permute-start.47) | collective-permute-done | bytes 737312 | tf_op jit(solution)/shard_map/ppermute | solution.py:41
  261.8 4.1 %collective-permute-done.44.refs_0_ = bf16[288,768]{1,0:T(8,128)(2,1)S(1)} collective-permute-done((bf16[288,768]{1,0:T(8,128)(2,1)S(1)}, bf16[288,768]{1,0:T(8,128)(2,1)S(1)}, u32[]{:S(2)}, u32[]{:S(2)}) %collective-permute-start.44) | collective-permute-done | bytes 442400 | tf_op jit(solution)/shard_map/ppermute | solution.py:41
  266.4 2.2 shard_map.347.refs_3_
  268.7 1.8 shard_map.350
  270.4 5.7 %collective-permute-done.49.refs_0_ = bf16[96,2304]{1,0:T(8,128)(2,1)S(1)} collective-permute-done((bf16[96,2304]{1,0:T(8,128)(2,1)S(1)}, bf16[96,2304]{1,0:T(8,128)(2,1)S(1)}, u32[]{:S(2)}, u32[]{:S(2)}) %collective-permute-start.49) | collective-permute-done | bytes 442400 | tf_op jit(solution)/shard_map/ppermute | solution.py:41
  276.2 1.7 copy-done.15
  278.0 2.4 collective-permute-start.52
  280.5 2.3 collective-permute-done.52
  282.8 1.8 collective-permute-start.53
  284.6 3.3 %collective-permute-done.53 = f32[16,768]{1,0:T(8,128)S(1)} collective-permute-done((f32[16,768]{1,0:T(8,128)S(1)}, f32[16,768]{1,0:T(8,128)S(1)}, u32[]{:S(2)}, u32[]{:S(2)}) %collective-permute-start.53) | collective-permute-done | bytes 49184 | tf_op jit(solution)/shard_map/ppermute | solution.py:41
  (200 shorter events, 45.7 us)
Async XLA Ops:
  4.0 27.5 %collective-permute-start.3 = (bf16[208,2304]{1,0:T(8,128)(2,1)}, bf16[208,2304]{1,0:T(8,128)(2,1)S(1)}, u32[]{:S(2)}, u32[]{:S(2)}) collective-permute-start(bf16[208,2304]{1,0:T(8,128)(2,1)} %get-tuple-element.178.refs_5_.refs_4_), channel_id=1, source_target_pairs={{0,8},{1,17},{2,10},{3,19},{4,12},{5,21},{6,14},{7,23},{8,0},{9,25... | collective-permute-start | bytes 2875400 | tf_op jit(solution)/shard_map/ppermute | solution.py:41
  7.0 24.6 %collective-permute-start.4 = (bf16[112,2304]{1,0:T(8,128)(2,1)}, bf16[112,2304]{1,0:T(8,128)(2,1)S(1)}, u32[]{:S(2)}, u32[]{:S(2)}) collective-permute-start(bf16[112,2304]{1,0:T(8,128)(2,1)} %get-tuple-element.179), channel_id=1, source_target_pairs={{0,24},{1,25},{2,26},{3,27},{4,28},{5,29},{6,30},{7,31},{8,16},{9,... | collective-permute-start | bytes 1548296 | tf_op jit(solution)/shard_map/ppermute | solution.py:41
  8.5 18.9 %collective-permute-start = (bf16[144,768]{1,0:T(8,128)(2,1)}, bf16[144,768]{1,0:T(8,128)(2,1)S(1)}, u32[]{:S(2)}, u32[]{:S(2)}) collective-permute-start(bf16[144,768]{1,0:T(8,128)(2,1)} %get-tuple-element.175), channel_id=1, source_target_pairs={{0,4},{1,3},{2,6},{3,1},{4,0},{5,7},{6,2},{7,5},{8,12},{9,11},{10,... | collective-permute-start | bytes 663560 | tf_op jit(solution)/shard_map/ppermute | solution.py:41
  11.1 16.3 %collective-permute-start.1 = (bf16[144,768]{1,0:T(8,128)(2,1)}, bf16[144,768]{1,0:T(8,128)(2,1)S(1)}, u32[]{:S(2)}, u32[]{:S(2)}) collective-permute-start(bf16[144,768]{1,0:T(8,128)(2,1)} %get-tuple-element.176), channel_id=1, source_target_pairs={{0,2},{1,5},{2,0},{3,7},{4,6},{5,1},{6,4},{7,3},{8,10},{9,13},{10,... | collective-permute-start | bytes 663560 | tf_op jit(solution)/shard_map/ppermute | solution.py:41
  12.6 14.7 %collective-permute-start.2 = (bf16[144,768]{1,0:T(8,128)(2,1)}, bf16[144,768]{1,0:T(8,128)(2,1)S(1)}, u32[]{:S(2)}, u32[]{:S(2)}) collective-permute-start(bf16[144,768]{1,0:T(8,128)(2,1)} %get-tuple-element.177), channel_id=1, source_target_pairs={{0,6},{1,7},{2,4},{3,5},{4,2},{5,3},{6,0},{7,1},{8,14},{9,15},{10,... | collective-permute-start | bytes 663560 | tf_op jit(solution)/shard_map/ppermute | solution.py:41
  31.7 22.9 %collective-permute-start.9 = (bf16[192,3840]{1,0:T(8,128)(2,1)S(1)}, bf16[192,3840]{1,0:T(8,128)(2,1)S(1)}, u32[]{:S(2)}, u32[]{:S(2)}) collective-permute-start(bf16[192,3840]{1,0:T(8,128)(2,1)S(1)} %get-tuple-element.195), channel_id=1, source_target_pairs={{0,8},{1,17},{2,10},{3,19},{4,12},{5,21},{6,14},{7,23},{8,0},{9,25... | collective-permute-start | bytes 4423688 | tf_op jit(solution)/shard_map/ppermute | solution.py:41
  40.5 4.9 %collective-permute-start.7 = (bf16[576,768]{1,0:T(8,128)(2,1)S(1)}, bf16[576,768]{1,0:T(8,128)(2,1)S(1)}, u32[]{:S(2)}, u32[]{:S(2)}) collective-permute-start(bf16[576,768]{1,0:T(8,128)(2,1)S(1)} %get-tuple-element.185.refs_1_), channel_id=1, source_target_pairs={{0,1},{1,0},{2,3},{3,2},{4,5},{5,4},{6,7},{7,6},{8,9},{9,8},{10,11... | collective-permute-start | bytes 2654216 | tf_op jit(solution)/shard_map/ppermute | solution.py:41
  40.7 4.7 %collective-permute-start.8 = (bf16[576,768]{1,0:T(8,128)(2,1)S(1)}, bf16[576,768]{1,0:T(8,128)(2,1)S(1)}, u32[]{:S(2)}, u32[]{:S(2)}) collective-permute-start(bf16[576,768]{1,0:T(8,128)(2,1)S(1)} %get-tuple-element.186.refs_2_), channel_id=1, source_target_pairs={{0,1},{1,0},{2,3},{3,2},{4,5},{5,4},{6,7},{7,6},{8,9},{9,8},{10,11... | collective-permute-start | bytes 2654216 | tf_op jit(solution)/shard_map/ppermute | solution.py:41
  41.4 13.1 %collective-permute-start.10 = (bf16[288,768]{1,0:T(8,128)(2,1)S(1)}, bf16[288,768]{1,0:T(8,128)(2,1)S(1)}, u32[]{:S(2)}, u32[]{:S(2)}) collective-permute-start(bf16[288,768]{1,0:T(8,128)(2,1)S(1)} %pad_maximum_fusion.3), channel_id=1, source_target_pairs={{0,4},{1,3},{2,6},{3,1},{4,0},{5,7},{6,2},{7,5},{8,12},{9,11},{10,... | collective-permute-start | bytes 1327112 | tf_op jit(solution)/shard_map/ppermute | solution.py:41
  44.0 25.6 %collective-permute-start.13 = (bf16[768,768]{1,0:T(8,128)(2,1)S(1)}, bf16[768,768]{1,0:T(8,128)(2,1)S(1)}, u32[]{:S(2)}, u32[]{:S(2)}) collective-permute-start(bf16[768,768]{1,0:T(8,128)(2,1)S(1)} %get-tuple-element.204), channel_id=1, source_target_pairs={{0,8},{1,17},{2,10},{3,19},{4,12},{5,21},{6,14},{7,23},{8,0},{9,25... | collective-permute-start | bytes 3538952 | tf_op jit(solution)/shard_map/ppermute | solution.py:41
  54.6 25.8 %collective-permute-start.11 = (bf16[192,3840]{1,0:T(8,128)(2,1)S(1)}, bf16[192,3840]{1,0:T(8,128)(2,1)S(1)}, u32[]{:S(2)}, u32[]{:S(2)}) collective-permute-start(bf16[192,3840]{1,0:T(8,128)(2,1)S(1)} %get-tuple-element.203.refs_0_), channel_id=1, source_target_pairs={{0,1},{1,0},{2,3},{3,2},{4,5},{5,4},{6,7},{7,6},{8,9},{9,8},{10,11... | collective-permute-start | bytes 4423688 | tf_op jit(solution)/shard_map/ppermute | solution.py:41
  54.7 16.4 %collective-permute-start.12 = (bf16[96,3840]{1,0:T(8,128)(2,1)S(1)}, bf16[96,3840]{1,0:T(8,128)(2,1)S(1)}, u32[]{:S(2)}, u32[]{:S(2)}) collective-permute-start(bf16[96,3840]{1,0:T(8,128)(2,1)S(1)} %slice.147), channel_id=1, source_target_pairs={{0,16},{1,9},{2,18},{3,11},{4,20},{5,13},{6,22},{7,15},{8,24},{9,1... | collective-permute-start | bytes 2211848 | tf_op jit(solution)/shard_map/ppermute | solution.py:41
  55.3 14.3 %collective-permute-start.14 = (bf16[288,768]{1,0:T(8,128)(2,1)S(1)}, bf16[288,768]{1,0:T(8,128)(2,1)S(1)}, u32[]{:S(2)}, u32[]{:S(2)}) collective-permute-start(bf16[288,768]{1,0:T(8,128)(2,1)S(1)} %pad_maximum_fusion.4), channel_id=1, source_target_pairs={{0,2},{1,5},{2,0},{3,7},{4,6},{5,1},{6,4},{7,3},{8,10},{9,13},{10,... | collective-permute-start | bytes 1327112 | tf_op jit(solution)/shard_map/ppermute | solution.py:41
  71.1 9.3 %collective-permute-start.15 = (bf16[96,3840]{1,0:T(8,128)(2,1)S(1)}, bf16[96,3840]{1,0:T(8,128)(2,1)S(1)}, u32[]{:S(2)}, u32[]{:S(2)}) collective-permute-start(bf16[96,3840]{1,0:T(8,128)(2,1)S(1)} %get-tuple-element.207.refs_2_), channel_id=1, source_target_pairs={{0,1},{1,0},{2,3},{3,2},{4,5},{5,4},{6,7},{7,6},{8,9},{9,8},{10,11... | collective-permute-start | bytes 2211848 | tf_op jit(solution)/shard_map/ppermute | solution.py:41
  80.4 10.1 %collective-permute-start.17 = (bf16[768,768]{1,0:T(8,128)(2,1)S(1)}, bf16[768,768]{1,0:T(8,128)(2,1)S(1)}, u32[]{:S(2)}, u32[]{:S(2)}) collective-permute-start(bf16[768,768]{1,0:T(8,128)(2,1)S(1)} %shard_map.317.refs_1_), channel_id=1, source_target_pairs={{0,1},{1,0},{2,3},{3,2},{4,5},{5,4},{6,7},{7,6},{8,9},{9,8},{10,11... | collective-permute-start | bytes 3538952 | tf_op jit(solution)/shard_map/ppermute | solution.py:41
  80.7 9.9 %collective-permute-start.16 = (bf16[384,768]{1,0:T(8,128)(2,1)S(1)}, bf16[384,768]{1,0:T(8,128)(2,1)S(1)}, u32[]{:S(2)}, u32[]{:S(2)}) collective-permute-start(bf16[384,768]{1,0:T(8,128)(2,1)S(1)} %slice.152), channel_id=1, source_target_pairs={{0,16},{1,9},{2,18},{3,11},{4,20},{5,13},{6,22},{7,15},{8,24},{9,1... | collective-permute-start | bytes 1769480 | tf_op jit(solution)/shard_map/ppermute | solution.py:41
  90.5 4.2 %collective-permute-start.18 = (bf16[384,768]{1,0:T(8,128)(2,1)S(1)}, bf16[384,768]{1,0:T(8,128)(2,1)S(1)}, u32[]{:S(2)}, u32[]{:S(2)}) collective-permute-start(bf16[384,768]{1,0:T(8,128)(2,1)S(1)} %get-tuple-element.217.refs_6_.refs_3_), channel_id=1, source_target_pairs={{0,1},{1,0},{2,3},{3,2},{4,5},{5,4},{6,7},{7,6},{8,9},{9,8},{10,11... | collective-permute-start | bytes 1769480 | tf_op jit(solution)/shard_map/ppermute | solution.py:41
  94.8 9.4 %collective-permute-start.19 = (bf16[1536,768]{1,0:T(8,128)(2,1)S(1)}, bf16[1536,768]{1,0:T(8,128)(2,1)S(1)}, u32[]{:S(2)}, u32[]{:S(2)}) collective-permute-start(bf16[1536,768]{1,0:T(8,128)(2,1)S(1)} %get-tuple-element.222), channel_id=1, source_target_pairs={{0,1},{1,0},{2,3},{3,2},{4,5},{5,4},{6,7},{7,6},{8,9},{9,8},{10,11... | collective-permute-start | bytes 7077896 | tf_op jit(solution)/shard_map/ppermute | solution.py:41
  104.3 9.9 %collective-permute-start.20 = (bf16[384,768]{1,0:T(8,128)(2,1)S(1)}, bf16[384,768]{1,0:T(8,128)(2,1)S(1)}, u32[]{:S(2)}, u32[]{:S(2)}) collective-permute-start(bf16[384,768]{1,0:T(8,128)(2,1)S(1)} %add_convert_fusion.11), channel_id=1, source_target_pairs={{0,16},{1,9},{2,18},{3,11},{4,20},{5,13},{6,22},{7,15},{8,24},{9,1... | collective-permute-start | bytes 1769480 | tf_op jit(solution)/shard_map/ppermute | solution.py:41
  114.8 16.3 %collective-permute-start.21 = (bf16[768,768]{1,0:T(8,128)(2,1)S(1)}, bf16[768,768]{1,0:T(8,128)(2,1)S(1)}, u32[]{:S(2)}, u32[]{:S(2)}) collective-permute-start(bf16[768,768]{1,0:T(8,128)(2,1)S(1)} %pad_maximum_fusion.1), channel_id=1, source_target_pairs={{0,8},{1,17},{2,10},{3,19},{4,12},{5,21},{6,14},{7,23},{8,0},{9,25... | collective-permute-start | bytes 3538952 | tf_op jit(solution)/shard_map/ppermute | solution.py:41
  116.4 14.4 %collective-permute-start.22 = (bf16[288,768]{1,0:T(8,128)(2,1)S(1)}, bf16[288,768]{1,0:T(8,128)(2,1)S(1)}, u32[]{:S(2)}, u32[]{:S(2)}) collective-permute-start(bf16[288,768]{1,0:T(8,128)(2,1)S(1)} %pad_maximum_fusion.5), channel_id=1, source_target_pairs={{0,4},{1,3},{2,6},{3,1},{4,0},{5,7},{6,2},{7,5},{8,12},{9,11},{10,... | collective-permute-start | bytes 1327112 | tf_op jit(solution)/shard_map/ppermute | solution.py:41
  131.1 6.8 %collective-permute-start.24 = (bf16[384,3840]{1,0:T(8,128)(2,1)S(1)}, bf16[384,3840]{1,0:T(8,128)(2,1)S(1)}, u32[]{:S(2)}, u32[]{:S(2)}) collective-permute-start(bf16[384,3840]{1,0:T(8,128)(2,1)S(1)} %get-tuple-element.252), channel_id=1, source_target_pairs={{0,1},{1,0},{2,3},{3,2},{4,5},{5,4},{6,7},{7,6},{8,9},{9,8},{10,11... | collective-permute-start | bytes 8847368 | tf_op jit(solution)/shard_map/ppermute | solution.py:41
  131.1 6.8 %collective-permute-start.23 = (bf16[384,768]{1,0:T(8,128)(2,1)S(1)}, bf16[384,768]{1,0:T(8,128)(2,1)S(1)}, u32[]{:S(2)}, u32[]{:S(2)}) collective-permute-start(bf16[384,768]{1,0:T(8,128)(2,1)S(1)} %slice.161), channel_id=1, source_target_pairs={{0,1},{1,0},{2,3},{3,2},{4,5},{5,4},{6,7},{7,6},{8,9},{9,8},{10,11... | collective-permute-start | bytes 1769480 | tf_op jit(solution)/shard_map/ppermute | solution.py:41
  131.7 6.2 %collective-permute-start.25 = (bf16[2,576,128]{2,1,0:T(8,128)(2,1)S(1)}, bf16[2,576,128]{2,1,0:T(8,128)(2,1)S(1)}, u32[]{:S(2)}, u32[]{:S(2)}) collective-permute-start(bf16[2,576,128]{2,1,0:T(8,128)(2,1)S(1)} %get-tuple-element.253), channel_id=1, source_target_pairs={{0,1},{1,0},{2,3},{3,2},{4,5},{5,4},{6,7},{7,6},{8,9},{9,8},{10,11... | collective-permute-start | bytes 884744 | tf_op jit(solution)/shard_map/ppermute | solution.py:41
  138.1 27.4 %collective-permute-start.27 = (bf16[96,3840]{1,0:T(8,128)(2,1)S(1)}, bf16[96,3840]{1,0:T(8,128)(2,1)S(1)}, u32[]{:S(2)}, u32[]{:S(2)}) collective-permute-start(bf16[96,3840]{1,0:T(8,128)(2,1)S(1)} %add_convert_fusion.5), channel_id=1, source_target_pairs={{0,16},{1,9},{2,18},{3,11},{4,20},{5,13},{6,22},{7,15},{8,24},{9,1... | collective-permute-start | bytes 2211848 | tf_op jit(solution)/shard_map/ppermute | solution.py:41
  139.8 25.7 %collective-permute-start.26 = (bf16[384,768]{1,0:T(8,128)(2,1)S(1)}, bf16[384,768]{1,0:T(8,128)(2,1)S(1)}, u32[]{:S(2)}, u32[]{:S(2)}) collective-permute-start(bf16[384,768]{1,0:T(8,128)(2,1)S(1)} %add_convert_fusion.8), channel_id=1, source_target_pairs={{0,2},{1,5},{2,0},{3,7},{4,6},{5,1},{6,4},{7,3},{8,10},{9,13},{10,... | collective-permute-start | bytes 1769480 | tf_op jit(solution)/shard_map/ppermute | solution.py:41
  141.5 24.0 %collective-permute-start.28 = (bf16[288,768]{1,0:T(8,128)(2,1)S(1)}, bf16[288,768]{1,0:T(8,128)(2,1)S(1)}, u32[]{:S(2)}, u32[]{:S(2)}) collective-permute-start(bf16[288,768]{1,0:T(8,128)(2,1)S(1)} %pad_maximum_fusion.6), channel_id=1, source_target_pairs={{0,2},{1,5},{2,0},{3,7},{4,6},{5,1},{6,4},{7,3},{8,10},{9,13},{10,... | collective-permute-start | bytes 1327112 | tf_op jit(solution)/shard_map/ppermute | solution.py:41
  142.0 23.5 %collective-permute-start.29 = (bf16[2,576,128]{2,1,0:T(8,128)(2,1)S(1)}, bf16[2,576,128]{2,1,0:T(8,128)(2,1)S(1)}, u32[]{:S(2)}, u32[]{:S(2)}) collective-permute-start(bf16[2,576,128]{2,1,0:T(8,128)(2,1)S(1)} %get-tuple-element.260), channel_id=1, source_target_pairs={{0,1},{1,0},{2,3},{3,2},{4,5},{5,4},{6,7},{7,6},{8,9},{9,8},{10,11... | collective-permute-start | bytes 884744 | tf_op jit(solution)/shard_map/ppermute | solution.py:41
  166.1 19.4 %collective-permute-start.30 = (bf16[192,3840]{1,0:T(8,128)(2,1)S(1)}, bf16[192,3840]{1,0:T(8,128)(2,1)S(1)}, u32[]{:S(2)}, u32[]{:S(2)}) collective-permute-start(bf16[192,3840]{1,0:T(8,128)(2,1)S(1)} %pad_maximum_fusion), channel_id=1, source_target_pairs={{0,8},{1,17},{2,10},{3,19},{4,12},{5,21},{6,14},{7,23},{8,0},{9,25... | collective-permute-start | bytes 4423688 | tf_op jit(solution)/shard_map/ppermute | solution.py:41
  166.5 15.9 %collective-permute-start.31 = (bf16[384,768]{1,0:T(8,128)(2,1)S(1)}, bf16[384,768]{1,0:T(8,128)(2,1)S(1)}, u32[]{:S(2)}, u32[]{:S(2)}) collective-permute-start(bf16[384,768]{1,0:T(8,128)(2,1)S(1)} %add_convert_fusion.7), channel_id=1, source_target_pairs={{0,4},{1,3},{2,6},{3,1},{4,0},{5,7},{6,2},{7,5},{8,12},{9,11},{10,... | collective-permute-start | bytes 1769480 | tf_op jit(solution)/shard_map/ppermute | solution.py:41
  169.5 12.9 %collective-permute-start.32 = (bf16[2,576,128]{2,1,0:T(8,128)(2,1)S(1)}, bf16[2,576,128]{2,1,0:T(8,128)(2,1)S(1)}, u32[]{:S(2)}, u32[]{:S(2)}) collective-permute-start(bf16[2,576,128]{2,1,0:T(8,128)(2,1)S(1)} %get-tuple-element.281), channel_id=1, source_target_pairs={{0,1},{1,0},{2,3},{3,2},{4,5},{5,4},{6,7},{7,6},{8,9},{9,8},{10,11... | collective-permute-start | bytes 884744 | tf_op jit(solution)/shard_map/ppermute | solution.py:41
  169.5 12.9 %collective-permute-start.33 = (bf16[2,576,128]{2,1,0:T(8,128)(2,1)S(1)}, bf16[2,576,128]{2,1,0:T(8,128)(2,1)S(1)}, u32[]{:S(2)}, u32[]{:S(2)}) collective-permute-start(bf16[2,576,128]{2,1,0:T(8,128)(2,1)S(1)} %get-tuple-element.282), channel_id=1, source_target_pairs={{0,1},{1,0},{2,3},{3,2},{4,5},{5,4},{6,7},{7,6},{8,9},{9,8},{10,11... | collective-permute-start | bytes 884744 | tf_op jit(solution)/shard_map/ppermute | solution.py:41
  192.4 3.8 %collective-permute-start.37 = (bf16[384,2304]{1,0:T(8,128)(2,1)S(1)}, bf16[384,2304]{1,0:T(8,128)(2,1)S(1)}, u32[]{:S(2)}, u32[]{:S(2)}) collective-permute-start(bf16[384,2304]{1,0:T(8,128)(2,1)S(1)} %shard_map.339), channel_id=1, source_target_pairs={{0,1},{1,0},{2,3},{3,2},{4,5},{5,4},{6,7},{7,6},{8,9},{9,8},{10,11... | collective-permute-start | bytes 5308424 | tf_op jit(solution)/shard_map/ppermute | solution.py:41
  192.8 6.5 %collective-permute-start.40 = (bf16[384,768]{1,0:T(8,128)(2,1)S(1)}, bf16[384,768]{1,0:T(8,128)(2,1)S(1)}, u32[]{:S(2)}, u32[]{:S(2)}) collective-permute-start(bf16[384,768]{1,0:T(8,128)(2,1)S(1)} %add_convert_fusion.6.refs_0_), channel_id=1, source_target_pairs={{0,1},{1,0},{2,3},{3,2},{4,5},{5,4},{6,7},{7,6},{8,9},{9,8},{10,11... | collective-permute-start | bytes 1769480 | tf_op jit(solution)/shard_map/ppermute | solution.py:41
  193.6 19.4 %collective-permute-start.39 = (bf16[96,3840]{1,0:T(8,128)(2,1)S(1)}, bf16[96,3840]{1,0:T(8,128)(2,1)S(1)}, u32[]{:S(2)}, u32[]{:S(2)}) collective-permute-start(bf16[96,3840]{1,0:T(8,128)(2,1)S(1)} %add_convert_fusion.2), channel_id=1, source_target_pairs={{0,2},{1,5},{2,0},{3,7},{4,6},{5,1},{6,4},{7,3},{8,10},{9,13},{10,... | collective-permute-start | bytes 2211848 | tf_op jit(solution)/shard_map/ppermute | solution.py:41
  196.3 16.7 %collective-permute-start.38 = (bf16[96,2304]{1,0:T(8,128)(2,1)S(1)}, bf16[96,2304]{1,0:T(8,128)(2,1)S(1)}, u32[]{:S(2)}, u32[]{:S(2)}) collective-permute-start(bf16[96,2304]{1,0:T(8,128)(2,1)S(1)} %add_convert_fusion.17), channel_id=1, source_target_pairs={{0,16},{1,9},{2,18},{3,11},{4,20},{5,13},{6,22},{7,15},{8,24},{9,1... | collective-permute-start | bytes 1327112 | tf_op jit(solution)/shard_map/ppermute | solution.py:41
  213.4 14.6 %collective-permute-start.41 = (bf16[192,2304]{1,0:T(8,128)(2,1)S(1)}, bf16[192,2304]{1,0:T(8,128)(2,1)S(1)}, u32[]{:S(2)}, u32[]{:S(2)}) collective-permute-start(bf16[192,2304]{1,0:T(8,128)(2,1)S(1)} %pad_maximum_fusion.2), channel_id=1, source_target_pairs={{0,8},{1,17},{2,10},{3,19},{4,12},{5,21},{6,14},{7,23},{8,0},{9,25... | collective-permute-start | bytes 2654216 | tf_op jit(solution)/shard_map/ppermute | solution.py:41
  214.0 14.1 %collective-permute-start.43 = (bf16[288,768]{1,0:T(8,128)(2,1)S(1)}, bf16[288,768]{1,0:T(8,128)(2,1)S(1)}, u32[]{:S(2)}, u32[]{:S(2)}) collective-permute-start(bf16[288,768]{1,0:T(8,128)(2,1)S(1)} %pad_maximum_fusion.7), channel_id=1, source_target_pairs={{0,4},{1,3},{2,6},{3,1},{4,0},{5,7},{6,2},{7,5},{8,12},{9,11},{10,... | collective-permute-start | bytes 1327112 | tf_op jit(solution)/shard_map/ppermute | solution.py:41
  228.3 33.0 %collective-permute-start.47 = (bf16[96,3840]{1,0:T(8,128)(2,1)S(1)}, bf16[96,3840]{1,0:T(8,128)(2,1)S(1)}, u32[]{:S(2)}, u32[]{:S(2)}) collective-permute-start(bf16[96,3840]{1,0:T(8,128)(2,1)S(1)} %add_convert_fusion.1), channel_id=1, source_target_pairs={{0,4},{1,3},{2,6},{3,1},{4,0},{5,7},{6,2},{7,5},{8,12},{9,11},{10,... | collective-permute-start | bytes 2211848 | tf_op jit(solution)/shard_map/ppermute | solution.py:41
  230.2 31.2 %collective-permute-start.46 = (bf16[96,2304]{1,0:T(8,128)(2,1)S(1)}, bf16[96,2304]{1,0:T(8,128)(2,1)S(1)}, u32[]{:S(2)}, u32[]{:S(2)}) collective-permute-start(bf16[96,2304]{1,0:T(8,128)(2,1)S(1)} %add_convert_fusion.14), channel_id=1, source_target_pairs={{0,2},{1,5},{2,0},{3,7},{4,6},{5,1},{6,4},{7,3},{8,10},{9,13},{10,... | collective-permute-start | bytes 1327112 | tf_op jit(solution)/shard_map/ppermute | solution.py:41
  233.3 28.1 %collective-permute-start.48 = (f32[16,768]{1,0:T(8,128)S(1)}, f32[16,768]{1,0:T(8,128)S(1)}, u32[]{:S(2)}, u32[]{:S(2)}) collective-permute-start(f32[16,768]{1,0:T(8,128)S(1)} %add.129.refs_2_), channel_id=1, source_target_pairs={{0,8},{1,9},{2,10},{3,11},{4,12},{5,13},{6,14},{7,15},{8,0},{9,1},... | collective-permute-start | bytes 147464 | tf_op jit(solution)/shard_map/ppermute | solution.py:41
  233.7 32.2 %collective-permute-start.44 = (bf16[288,768]{1,0:T(8,128)(2,1)S(1)}, bf16[288,768]{1,0:T(8,128)(2,1)S(1)}, u32[]{:S(2)}, u32[]{:S(2)}) collective-permute-start(bf16[288,768]{1,0:T(8,128)(2,1)S(1)} %pad_maximum_fusion.8), channel_id=1, source_target_pairs={{0,2},{1,5},{2,0},{3,7},{4,6},{5,1},{6,4},{7,3},{8,10},{9,13},{10,... | collective-permute-start | bytes 1327112 | tf_op jit(solution)/shard_map/ppermute | solution.py:41
  261.6 7.1 %collective-permute-start.51 = (bf16[96,3840]{1,0:T(8,128)(2,1)S(1)}, bf16[96,3840]{1,0:T(8,128)(2,1)S(1)}, u32[]{:S(2)}, u32[]{:S(2)}) collective-permute-start(bf16[96,3840]{1,0:T(8,128)(2,1)S(1)} %add_convert_fusion.refs_0_), channel_id=1, source_target_pairs={{0,1},{1,0},{2,3},{3,2},{4,5},{5,4},{6,7},{7,6},{8,9},{9,8},{10,11... | collective-permute-start | bytes 2211848 | tf_op jit(solution)/shard_map/ppermute | solution.py:41
  261.7 14.4 %collective-permute-start.49 = (bf16[96,2304]{1,0:T(8,128)(2,1)S(1)}, bf16[96,2304]{1,0:T(8,128)(2,1)S(1)}, u32[]{:S(2)}, u32[]{:S(2)}) collective-permute-start(bf16[96,2304]{1,0:T(8,128)(2,1)S(1)} %add_convert_fusion.13), channel_id=1, source_target_pairs={{0,4},{1,3},{2,6},{3,1},{4,0},{5,7},{6,2},{7,5},{8,12},{9,11},{10,... | collective-permute-start | bytes 1327112 | tf_op jit(solution)/shard_map/ppermute | solution.py:41
  265.9 4.5 %collective-permute-start.50 = (f32[16,768]{1,0:T(8,128)S(1)}, f32[16,768]{1,0:T(8,128)S(1)}, u32[]{:S(2)}, u32[]{:S(2)}) collective-permute-start(f32[16,768]{1,0:T(8,128)S(1)} %add.131.refs_1_), channel_id=1, source_target_pairs={{0,16},{1,17},{2,18},{3,19},{4,20},{5,21},{6,22},{7,23},{8,24},{9,... | collective-permute-start | bytes 147464 | tf_op jit(solution)/shard_map/ppermute | solution.py:41
  277.9 11.3 %collective-permute-start.54 = (bf16[96,2304]{1,0:T(8,128)(2,1)S(1)}, bf16[96,2304]{1,0:T(8,128)(2,1)S(1)}, u32[]{:S(2)}, u32[]{:S(2)}) collective-permute-start(bf16[96,2304]{1,0:T(8,128)(2,1)S(1)} %add_convert_fusion.12.refs_0_), channel_id=1, source_target_pairs={{0,1},{1,0},{2,3},{3,2},{4,5},{5,4},{6,7},{7,6},{8,9},{9,8},{10,11... | collective-permute-start | bytes 1327112 | tf_op jit(solution)/shard_map/ppermute | solution.py:41
  278.0 4.8 %collective-permute-start.52 = (f32[16,768]{1,0:T(8,128)S(1)}, f32[16,768]{1,0:T(8,128)S(1)}, u32[]{:S(2)}, u32[]{:S(2)}) collective-permute-start(f32[16,768]{1,0:T(8,128)S(1)} %add.133), channel_id=1, source_target_pairs={{0,2},{1,3},{2,0},{3,1},{4,6},{5,7},{6,4},{7,5},{8,10},{9,11},{10,... | collective-permute-start | bytes 147464 | tf_op jit(solution)/shard_map/ppermute | solution.py:41
  282.8 5.1 %collective-permute-start.53 = (f32[16,768]{1,0:T(8,128)S(1)}, f32[16,768]{1,0:T(8,128)S(1)}, u32[]{:S(2)}, u32[]{:S(2)}) collective-permute-start(f32[16,768]{1,0:T(8,128)S(1)} %add.134), channel_id=1, source_target_pairs={{0,4},{1,5},{2,6},{3,7},{4,0},{5,1},{6,2},{7,3},{8,12},{9,13},{10,... | collective-permute-start | bytes 147464 | tf_op jit(solution)/shard_map/ppermute | solution.py:41
  (31 other events, 160.7 us)

commit v3 on v2

--- a/solution.py
+++ b/solution.py
@@ -144,11 +144,8 @@
     return local, step < count + extra
 
 
-def prepare_kernel(sizes, groups, small_count, counts_ref, values, *refs):
+def pick_kernel(sizes, counts_ref, values, *parts):
     slots, images, chips, capacity, tok_count, seq_count = sizes
-    shards, refs = refs[: sum(groups)], refs[sum(groups) :]
-    smalls, refs = refs[:small_count], refs[small_count:]
-    parts, halves, rest = refs[:chips], refs[chips : chips + len(groups)], refs[chips + len(groups) :]
     seq_index = lax.axis_index("seq")
     chip, core = seq_index // 2, seq_index % 2
     for label in range(chips):
@@ -162,6 +159,13 @@
         pick = jnp.where(valid & (local == held), 1.0, 0.0).astype(BF16)
         start = pl.multiple_of(micro * tok_count, tok_count)
         parts[label][...] = dot(pick, values[pl.ds(start, tok_count), :]).astype(BF16)
+
+
+def line_up_kernel(groups, small_count, *refs):
+    shards, refs = refs[: sum(groups)], refs[sum(groups) :]
+    smalls, refs = refs[:small_count], refs[small_count:]
+    halves, rest = refs[: len(groups)], refs[len(groups) :]
+    core = lax.axis_index("seq") % 2
     if smalls:
         first_half, inserted = rest
         half = (halves[0].shape[0] - EXTRA_ROWS) // 2
@@ -183,8 +187,6 @@
         at += count
     if smalls:
         first_half[...] = halves[0][: first_half.shape[0], :]
-    else:
-        marks_kernel(sizes, counts_ref, *rest)
 
 
 def collect_kernel(sizes, counts_ref, *refs):
@@ -276,6 +278,7 @@
 
 STAGE_SEMS = pltpu.SemaphoreType.DMA((7,))
 EXTRA_ROWS = 16
+ROW_TILE = 640
 
 
 def norm_parts(values):
@@ -367,6 +370,10 @@
         lse_ref[here, :] = jnp.where(lane == 2 * pair + 1, lses[1], kept)
 
 
+def row_tiles(rows):
+    return 1 if rows <= ROW_TILE else rows // 256
+
+
 def attention_specs(rows, first):
     per_pair = pl.BlockSpec((rows, LANES), lambda i: (0, i + first))
     two = pl.BlockSpec((2, rows, LANES), lambda i: (0, 0, i + first))
@@ -383,12 +390,12 @@
     per_pair, _, marks, all_marks = attention_specs(rows, first)
     out_pair = attention_specs(rows, 0)[0]
     return pl.pallas_call(
-        ignoring(partial(attend_forward_kernel, 4), 8, len(after)),
+        ignoring(partial(attend_forward_kernel, row_tiles(rows)), 8, len(after)),
         grid=(pairs_here,),
         in_specs=[per_pair] * 5 + [marks, all_marks, marks] + [ANY] * len(after),
         out_specs=[out_pair, marks],
         out_shape=[shape((rows, pairs_here * LANES)), shape((rows, LANES), F32)],
-        compiler_params=pltpu.CompilerParams(vmem_limit_bytes=16 * MIB),
+        compiler_params=pltpu.CompilerParams(vmem_limit_bytes=(16 if rows <= ROW_TILE else 48) * MIB),
     )(q, own_k, own_v, other_k, other_v, q_marks, k_marks, live, *after)
 
 
@@ -512,7 +519,7 @@
 
 
 def up_terms_kernel(hidden_grad, normed, branch_grad, attended, *refs):
-    terms, (up_scratch, out_scratch) = refs[:4], refs[4:]
+    terms, (up_scratch, out_scratch) = refs[:8], refs[8:]
     emit_terms(normed, hidden_grad, up_scratch, terms, 0)
     emit_terms(attended, branch_grad, out_scratch, terms, hidden_grad.shape[1])
 
@@ -592,7 +599,7 @@
     out_pair, out_two = attention_specs(rows, 0)[:2]
     there = attention_specs(rows, skipped)[0]
     return pl.pallas_call(
-        ignoring(partial(attend_backward_kernel, 4, skipped), 11, len(after)),
+        ignoring(partial(attend_backward_kernel, row_tiles(rows), skipped), 11, len(after)),
         grid=(pairs_here,),
         in_specs=[per_pair] * 5 + [marks, all_marks, marks, there, marks, per_pair]
         + [ANY] * len(after),
@@ -600,73 +607,62 @@
         out_shape=[shape((rows, pairs_here * LANES))]
         + [shape((2, rows, pairs_here * LANES))] * 2,
         scratch_shapes=[pltpu.VMEM((2 * rows, LANES), F32)] * 2,
-        compiler_params=pltpu.CompilerParams(vmem_limit_bytes=16 * MIB),
+        compiler_params=pltpu.CompilerParams(vmem_limit_bytes=(16 if rows <= ROW_TILE else 48) * MIB),
     )(q, own_k, own_v, other_k, other_v, q_marks, k_marks, live, attended, lse, grads, *after)
 
 
 def emit_terms(left, right, scratch, terms, at):
-    away, keep, keep_far, keep_own = terms
     mine, core = lax.axis_index("fsdp"), lax.axis_index("seq") % 2
     count, cols = left.shape[1] // 4, right.shape[1]
     half = count // 2
     here = slice(at, at + cols)
     if scratch is not None:
         scratch[...] = rows_of(left[...], right[...])
-
-    def rows_at(flip, which):
-        start = (mine ^ flip) * count + which * half
-        if scratch is not None:
-            value = scratch[pl.ds(pl.multiple_of(start, 16), half), :]
-        else:
-            value = rows_of(left[:, pl.ds(pl.multiple_of(start, LANES), half)], right[...])
-        return value.astype(BF16)
-
     for i in range(2):
         home = core ^ i
-        rows = [rows_at(1 + home, home), rows_at(1 + home, 1 - home), rows_at(3, home), rows_at(0, home)]
-        if i == 0:
-            keep[:half, here] = rows[0]
-            keep[half:, here] = rows[1]
-            keep_far[:, here] = rows[2]
-            keep_own[:, here] = rows[3]
-        else:
-            for j, value in enumerate(rows):
-                away[j * half : (j + 1) * half, here] = value
+        for out, flip in zip(terms[4 * i : 4 * i + 4], (3, 2 - home, 1 + home, 0)):
+            start = (mine ^ flip) * count + home * half
+            if scratch is not None:
+                value = scratch[pl.ds(pl.multiple_of(start, 16), half), :]
+            else:
+                value = rows_of(left[:, pl.ds(pl.multiple_of(start, LANES), half)], right[...])
+            out[:, here] = value.astype(BF16)
 
 
 def term_shapes(rows, cols):
-    return [shape((count, cols)) for count in (2 * rows, rows, rows // 2, rows // 2)]
+    return [shape((rows // 2, cols))] * 8
 
 
 class Reduction:
     def __init__(self, terms):
-        self.away, self.keep, self.keep_far, self.keep_own = terms
+        self.keep_far, self.keep_side, self.keep_near, self.keep_own = terms[:4]
+        self.away = terms[4:]
         self.count = self.keep_far.shape[0]
 
     def send_other(self):
-        self.other = to_core(self.away)
-        return [self.other]
+        self.other_far, self.other_side, self.other_near, self.other_own = [
+            to_core(item) for item in self.away
+        ]
+        return [self.other_far, self.other_side, self.other_near, self.other_own]
 
     def send_far(self):
-        part = self.other[2 * self.count : 3 * self.count]
-        self.far = to_fsdp((wide(self.keep_far) + wide(part)).astype(BF16), (2, 1))
+        self.far = to_fsdp((wide(self.keep_far) + wide(self.other_far)).astype(BF16), (2, 1))
         return [self.far]
 
+    def send_side(self):
+        self.side = to_fsdp((wide(self.keep_side) + wide(self.other_side)).astype(BF16), (2, 1))
+        return [self.side]
+
     def send_near(self):
-        first = wide(self.keep[: self.count]) + wide(self.other[: self.count]) + wide(self.far)
-        second = wide(self.keep[self.count :]) + wide(self.other[self.count : 2 * self.count])
-        self.near = to_fsdp(jnp.concatenate([first, second], 0).astype(BF16), (1, 2))
+        total = wide(self.keep_near) + wide(self.other_near) + wide(self.far)
+        self.near = to_fsdp(total.astype(BF16), (1, 2))
         return [self.near]
-
-    def send_both(self):
-        self.both = to_core(self.near[self.count :])
-        return [self.both]
 
     def send_chips(self):
         flips = [1 << i for i in range((lax.axis_size("seq") // 2).bit_length() - 1)]
         self.orders = list(zip(flips, flips[::-1]))
-        total = wide(self.keep_own) + wide(self.other[3 * self.count :])
-        self.sent = (total + wide(self.near[: self.count]) + wide(self.both)).astype(BF16)
+        total = wide(self.keep_own) + wide(self.other_own)
+        self.sent = (total + wide(self.near) + wide(self.side)).astype(BF16)
         self.got = to_chip(self.sent, *self.orders[0])
         return [self.got]
 
@@ -702,7 +698,7 @@
 def project_grad_kernel(count, *refs):
     q_grads, own_grads, other_grads = refs[:count], refs[count : 2 * count], refs[2 * count : 3 * count]
     normed, projected_grad, sums = refs[3 * count : 3 * count + 3]
-    terms, scratch = refs[3 * count + 3 : 3 * count + 7], refs[3 * count + 7]
+    terms, scratch = refs[3 * count + 3 : 3 * count + 11], refs[3 * count + 11]
     width = normed.shape[1]
     at = 0
     for q_grad, own_grad, other_grad in zip(q_grads, own_grads, other_grads):
@@ -788,8 +784,18 @@
     sizes = (slots, images, chips, capacity, tok_count, seq_count)
     counts = image_tokens
 
-    def prepare(values, groups, small=(), after=(), send=True):
-        flat = values.reshape(micro_count * tok_count, width)
+    def pick(values, limit=16, after=()):
+        return list(
+            call(
+                partial(pick_kernel, sizes),
+                [(counts, SMEM), (values.reshape(micro_count * tok_count, width), VMEM)],
+                [shape((capacity, width))] * chips,
+                after=after,
+                limit=limit,
+            )
+        )
+
+    def line_up(groups, small=(), limit=16, after=()):
         shards = [shard for group in groups for shard in group]
         more = EXTRA_ROWS if small else 0
         outs = [
@@ -797,22 +803,15 @@
             for group in groups
         ]
         if small:
-            outs += [shape((outs[0].shape[0] // 2 + more // 2, outs[0].shape[1]))]
-        else:
-            outs += [shape((rows, LANES)), shape((2 * rows, LANES)), shape((rows, LANES), F32)]
-        results = call(
-            partial(prepare_kernel, sizes, [len(group) for group in groups], len(small)),
-            [(counts, SMEM)] + [(item, VMEM) for item in [flat] + shards + list(small)],
-            [shape((capacity, width))] * chips + outs,
+            outs += [shape(((outs[0].shape[0] + more) // 2, outs[0].shape[1]))]
+        return call(
+            partial(line_up_kernel, [len(group) for group in groups], len(small)),
+            [(item, VMEM) for item in shards + list(small)],
+            outs,
             [pltpu.VMEM((EXTRA_ROWS, width), F32)] if small else [],
             after=after,
-            limit=60 if small else 16,
+            limit=limit,
         )
-        parts = list(results[:chips])
-        if send:
-            for label in range(chips - 1, 0, -1):
-                parts[label] = to_chip(parts[label], *flips_of(label, chips))
-        return parts, *results[chips:]
 
     def cross(parts, bit):
         labels = [label for label in range(chips) if label & bit]
@@ -852,12 +851,20 @@
         scale_mlp,
     ]
     own_rows = ln1_gain.shape[0]
-    x_parts, qkv_sent, qkv_first = prepare(tokens, [[qkv_weight]], small + [up_bias])
+    qkv_sent, qkv_first = line_up([[qkv_weight]], small + [up_bias], limit=60)
     near, far = to_fsdp(qkv_sent, (1, 2)), to_fsdp(qkv_first, (3, 3))
-    cot_sent, up_sent, down_sent, q_marks, k_marks, live = prepare(
-        cotangent, [[out_weight, up_weight], [down_weight]], after=[qkv_sent], send=False
-    )
-    near, far, up_sent = hold([near, far, up_sent], x_parts + [q_marks])
+    x_parts = pick(tokens, limit=60, after=[qkv_sent])
+    for label in range(chips - 1, 0, -1):
+        x_parts[label] = to_chip(x_parts[label], *flips_of(label, chips))
+    cot_sent = pick(cotangent, after=[qkv_sent])
+    up_sent, down_sent = line_up([[out_weight, up_weight], [down_weight]], after=[qkv_sent])
+    q_marks, k_marks, live = call(
+        partial(marks_kernel, sizes),
+        [(counts, SMEM)],
+        [shape((rows, LANES)), shape((2 * rows, LANES)), shape((rows, LANES), F32)],
+        after=[qkv_sent],
+    )
+    near, far, up_sent = hold([near, far, up_sent], x_parts + [q_marks, down_sent, cot_sent[0]])
     qkv_pieces = [near, to_core(near), far, to_core(far)]
     up_near = to_fsdp(up_sent, (1, 2))
 
@@ -878,11 +885,11 @@
     down_near = to_fsdp(down_sent, (1, 2))
     cot_moved = cross(cot_sent, 1)
     attention = (q, own_k, own_v, to_core(own_k), to_core(own_v), q_marks, k_marks, live)
-    step = width // LANES // 3
+    spans = [(0, 2), (2, width // LANES - 2)]
     attended_parts, lses = [], []
 
     def forward(i):
-        part, lse = attend_forward(i * step, step, *attention, after=attended_parts[-1:])
+        part, lse = attend_forward(*spans[i], *attention, after=attended_parts[-1:])
         attended_parts.append(part)
         lses.append(lse)
         return part
@@ -895,7 +902,7 @@
     cot_parts = crossed(cot_parts, cot_moved, last_bit)
     up_pieces = [up_near, to_core(up_near), up_far, to_core(up_far)]
     down_far = to_fsdp(down_near[: down_weight.shape[0] // 2], (2, 1))
-    up_pieces = hold(up_pieces, [forward(2)])
+    up_pieces = hold(up_pieces, [])
     (down_near,) = hold([down_near], up_pieces)
     down_other = to_core(down_near)
 
@@ -930,8 +937,13 @@
     )
     down = Reduction(down_terms)
     down_pieces = [down_near, down_other, down_far, far_other]
-    down.away, *down_pieces = hold([down.away] + down_pieces, [down_in])
-    waits = down.send_other()
+    *down.away, down_near, down_other, down_far, far_other = hold(
+        list(down.away) + down_pieces, [down_in]
+    )
+    down_pieces = [down_near, down_other, down_far, far_other]
+    others = down.send_other()
+    (down.other_far,) = hold(others[:1], [])
+    waits = down.send_far() + others[1:]
     results = call(
         partial(down_kernel, chips, tile),
         [(item, VMEM) for item in (active, slope, middle, cot_rows, down_in, vec)]
@@ -945,8 +957,9 @@
         [pltpu.VMEM((hidden_width, width), BF16), STAGE_SEMS],
     )
     out_sent, (hidden_grad, scale_grad, up_shift_grad) = list(results[:chips]), results[chips:]
-    (down.other,) = hold(waits, [hidden_grad])
-    waits = down.send_far()
+    down.far, down.other_side, down.other_near, down.other_own = hold(waits, [hidden_grad])
+    waits = down.send_near() + down.send_side()
+    out_moved = cross(out_sent, 1)
 
     middle_grad, branch_grad, attended_grad, narrow_sums = call(
         partial(narrow_kernel, tile),
@@ -961,9 +974,6 @@
         ],
         up_scratch,
     )
-    down.far, *out_sent = hold(waits + out_sent, [middle_grad])
-    waits = down.send_near()
-    out_moved = cross(out_sent, 1)
     up_terms = call(
         up_terms_kernel,
         [(item, VMEM) for item in (hidden_grad, normed_second, branch_grad, attended)],
@@ -978,10 +988,10 @@
         query_grad, own_grad, other_grad = attend_backward(
             first,
             1,
-            first % step,
+            first - spans[first >= spans[1][0]][0],
             *attention,
-            attended_parts[first // step],
-            lses[first // step],
+            attended_parts[first >= spans[1][0]],
+            lses[first >= spans[1][0]],
             attended_grad,
             after=query_grads[-1:] + list(after),
         )
@@ -1000,42 +1010,41 @@
     sent_grads = [0]
     core_grads = []
 
-    backward(0, up_terms[:1])
-    (down.near, up.away, out_moved), moved = hold_grads(waits + [up.away, out_moved])
-    out_parts = crossed(out_sent, out_moved, 1)
-    waits = down.send_both() + up.send_other() + moved
-    out_parts, out_moved, _ = cross_rest(out_parts)
+    down.near, down.side, out_moved, *up.away = hold(
+        waits + [out_moved] + list(up.away), up_terms[:1]
+    )
+    others = up.send_other()
+    waits = down.send_chips()
+    up.other_far, up.other_side = hold(others[:2], [])
+    waits += up.send_far() + up.send_side() + others[2:]
+    backward(0)
     backward(1)
-    (down.both, up.other, *core_grads), fresh = hold_grads(waits)
-    waits = down.send_chips() + up.send_far() + [out_moved] + fresh
+    (down.got, up.far, up.side, up.other_near, up.other_own), fresh = hold_grads(waits)
+    waits = up.send_near() + down.send_chips_again() + fresh
     backward(2)
     backward(3)
-    (down.got, up.far, out_moved, *more), fresh = hold_grads(waits)
-    out_parts = crossed(out_parts, out_moved, last_bit)
-    core_grads += more
-    waits = up.send_near() + down.send_chips_again() + fresh
+    (up.near, down.got, *core_grads), fresh = hold_grads(waits)
+    waits = up.send_chips() + down.send_total() + fresh
     backward(4)
     backward(5)
-    (up.near, down.got, *more), fresh = hold_grads(waits)
-    core_grads += more
-    (up.both, *more) = hold(up.send_both() + fresh, [])
-    core_grads += more
-    got = up.send_chips()
-    waits = down.send_total()
+    (down.other_total, *more), fresh = hold_grads(waits[1:])
+    core_grads += more + fresh
+    (down_grad,) = down.shards([width])
+    out_parts, out_moved, _ = cross_rest(crossed(out_sent, out_moved, 1))
 
     projected_grad, qkv_sums, *qkv_terms = call(
         partial(project_grad_kernel, len(query_grads)),
         [(item, VMEM) for item in query_grads + own_grads + core_grads + [normed_first]],
         [shape((rows, 3 * width)), shape((2, width), F32)] + term_shapes(own_rows, 3 * width),
         [pltpu.VMEM((width, 3 * width), F32)],
-    )
-    output = collect(out_parts, [projected_grad])
-    (down.other_total,) = hold(waits, [output])
-    (down_grad,) = down.shards([width])
+        after=[down_grad],
+    )
     qkv = Reduction(qkv_terms)
-    (qkv.away,) = hold([qkv.away], [projected_grad])
-    (qkv.other,) = hold(qkv.send_other(), [])
-    waits = qkv.send_far()
+    *qkv.away, up.got = hold(list(qkv.away) + waits[:1], [projected_grad])
+    up_waits = up.send_chips_again()
+    others = qkv.send_other()
+    qkv.other_far, qkv.other_side = hold(others[:2], [])
+    waits = qkv.send_far() + qkv.send_side() + others[2:]
     *in_sent, sums = call(
         partial(input_kernel, chips),
         [(item, VMEM) for item in (projected_grad, x_rows, middle_grad, vec)]
@@ -1044,31 +1053,35 @@
         [shape((capacity, width))] * chips + [shape((EXTRA_ROWS, width), F32)],
         [pltpu.VMEM((width, 3 * width), BF16), STAGE_SEMS],
     )
-    qkv.far, up.got, sums, *in_sent = hold(waits + got + [sums] + in_sent, [down_grad])
+    qkv.far, qkv.side, qkv.other_near, qkv.other_own, sums, *in_sent = hold(
+        waits + [sums] + in_sent, []
+    )
     waits = qkv.send_near()
-    got = up.send_chips_again()
     in_moved = cross(in_sent, 1)
     other_sums = to_core(sums)
-    qkv.near, sums, other_sums, in_moved = hold(waits + [sums, other_sums, in_moved], [])
+    qkv.near, in_moved, up.got, out_moved, sums, other_sums = hold(
+        waits + [in_moved] + up_waits + [out_moved, sums, other_sums], []
+    )
+    out_parts = crossed(out_parts, out_moved, last_bit)
+    up.send_total()
+    waits = qkv.send_chips()
+    in_parts, in_moved, _ = cross_rest(crossed(in_sent, in_moved, 1))
     sums = sums + other_sums
-    other_sums = to_fsdp(sums, (1, 1))
-    in_parts, in_moved, _ = cross_rest(crossed(in_sent, in_moved, 1))
-    (qkv.both,) = hold(qkv.send_both(), [])
-    waits = qkv.send_chips()
-    qkv.got, up.got, sums, other_sums = hold(waits + got + [sums, other_sums], [])
-    sums = sums + other_sums
-    other_sums = to_fsdp(sums, (2, 2))
+    far_sums = [to_chip(sums, flip) for flip in (1, 2, 3)]
+    output = collect(out_parts)
+    (up.other_total,) = hold([up.other_total], [output])
+    up_grad, out_grad = up.shards([hidden_width, width])
+    qkv.got, sums, in_moved, *far_sums = hold(waits + [sums, in_moved] + far_sums, [up_grad])
     waits = qkv.send_chips_again()
-    (in_moved,) = hold([in_moved], [])
-    input_grad = collect(crossed(in_parts, in_moved, last_bit))
-    up.send_total()
-    up_grad, out_grad = up.shards([hidden_width, width])
-    qkv.got, sums, other_sums = hold(waits + [sums, other_sums], [input_grad, up_grad])
-    sums = sums + other_sums
-    flip = 1
+    sums = (sums + far_sums[0]) + (far_sums[1] + far_sums[2])
+    flip = 4
     while flip < chips:
         sums = sums + to_chip(sums, flip)
         flip *= 2
+    far_sums = [to_fsdp(sums, (flip, flip)) for flip in (1, 2, 3)]
+    input_grad = collect(crossed(in_parts, in_moved, last_bit))
+    qkv.got, sums, *far_sums = hold(waits + [sums] + far_sums, [input_grad])
+    sums = (sums + far_sums[0]) + (far_sums[1] + far_sums[2])
     qkv.send_total()
     (qkv_grad,) = qkv.shards([3 * width])
     output, input_grad = output.reshape(tokens.shape), input_grad.reshape(tokens.shape)

time: 294 us -> 270 us (0.918)
  Pallas kernels: 125 us -> 108 us
  waiting for transfers between devices: 102 us -> 87.7 us
  starting transfers between devices: 48.8 us -> 58.1 us
    pallas_call x9 -> x8, Pallas kernels: 62.9 us -> 43.5 us  [the longest x6 26.7 us: attend_backward(): pl.pallas_call(ignoring(partial(attend_backward_kernel, row_tiles(rows),...]
    ppermute x55 -> x66, waiting for transfers between devices: 102 us -> 87.7 us  [move(): return lax.ppermute(value, BOTH, pairs)]
    ppermute x55 -> x66, starting transfers between devices: 48.8 us -> 58.1 us  [move(): return lax.ppermute(value, BOTH, pairs)]
    pallas_call x39 -> x40, Pallas kernels: 62 us -> 64.4 us  [call(): pl.pallas_call(run, in_specs=[spec for _, spec in operands] + [ANY] * len...]
    unnamed x48 -> x44, local copies, waits for them, and re-layouts: 7.72 us -> 6.63 us
  transfers between devices with their start and end apart: 55 -> 66, of which waited for: 23 -> 25; matrix products, arithmetic and copies ran while one was open for 1% -> 2% of each run, Pallas kernels for 40% -> 39%
where the time goes in v3:
time: 270 us; the launch traced here: 267 us
  Pallas kernels  108 us (40%)
  waiting for transfers between devices  87.7 us (32%)
  starting transfers between devices  58.1 us (22%)
  local copies, waits for them, and re-layouts  8.22 us (3%)
  other arithmetic  3.65 us (1%)
    ppermute x66, waiting for transfers between devices, move(): return lax.ppermute(value, BOTH, pairs)  87.7 us
    pallas_call x40, Pallas kernels, call(): pl.pallas_call(run, in_specs=[spec for _, spec in operands] + [ANY] * len...  64.4 us
    ppermute x66, starting transfers between devices, move(): return lax.ppermute(value, BOTH, pairs)  58.1 us
    pallas_call x6, Pallas kernels, attend_backward(): pl.pallas_call(ignoring(partial(attend_backward_kernel, row_tiles(rows),...  26.7 us
    pallas_call x2, Pallas kernels, attend_forward(): pl.pallas_call(ignoring(partial(attend_forward_kernel, row_tiles(rows)),...  16.8 us
    unnamed x44, local copies, waits for them, and re-layouts  6.63 us
  transfers between devices with their start and end apart: 66, of which 25 were waited for; matrix products, arithmetic and copies ran while one was open for 2% of the time, Pallas kernels for 39%

profile of v3, /device:TPU:0, one launch (start us, length us, event | category | flops | bytes accessed | tf_op | source)
XLA Modules:
  0.0 267.1 jit_solution(8085227594252387272)
XLA Ops:
  0.7 2.5 shard_map.305
  3.2 3.0 %collective-permute-start.3 = (bf16[208,2304]{1,0:T(8,128)(2,1)}, bf16[208,2304]{1,0:T(8,128)(2,1)S(1)}, u32[]{:S(2)}, u32[]{:S(2)}) collective-permute-start(bf16[208,2304]{1,0:T(8,128)(2,1)} %get-tuple-element.205.refs_2_.refs_3_.refs_1_.refs_4_), channel_id=1, source_target_pairs={{0,8},{1,17},{2,10},{3,19},{4,12},{5,21},{6,14},{7,23},{8,0},{9,25... | collective-permute-start | bytes 2875400 | tf_op jit(solution)/shard_map/ppermute | solution.py:41
  7.6 2.3 shard_map.306
  10.0 2.7 collective-permute-start
  16.9 11.9 %collective-permute-done.refs_4_.refs_1_ = bf16[144,768]{1,0:T(8,128)(2,1)S(1)} collective-permute-done((bf16[144,768]{1,0:T(8,128)(2,1)}, bf16[144,768]{1,0:T(8,128)(2,1)S(1)}, u32[]{:S(2)}, u32[]{:S(2)}) %collective-permute-start) | collective-permute-done | bytes 221216 | tf_op jit(solution)/shard_map/ppermute | solution.py:41
  28.9 1.8 collective-permute-done.4.refs_1_
  32.4 1.9 collective-permute-done.6.refs_9_.refs_13_
  34.3 5.3 %shard_map.311 = (bf16[576,768]{1,0:T(8,128)(2,1)S(1)}, bf16[576,768]{1,0:T(8,128)(2,1)S(1)}, bf16[576,768]{1,0:T(8,128)(2,1)S(1)}, bf16[576,768]{1,0:T(8,128)(2...) custom-call(bf16[144,768]{1,0:T(8,128)(2,1)S(1)} %copy-done.19, ...), custom_call_target="tpu_custom_call" | custom-call | tf_op jit(solution)/shard_map/pallas_call | solution.py:82
  40.6 4.0 %collective-permute-start.10 = (bf16[288,768]{1,0:T(8,128)(2,1)S(1)}, bf16[288,768]{1,0:T(8,128)(2,1)S(1)}, u32[]{:S(2)}, u32[]{:S(2)}) collective-permute-start(bf16[288,768]{1,0:T(8,128)(2,1)S(1)} %pad_maximum_fusion), channel_id=1, source_target_pairs={{0,4},{1,3},{2,6},{3,1},{4,0},{5,7},{6,2},{7,5},{8,12},{9,11},{10,... | collective-permute-start | bytes 1327112 | tf_op jit(solution)/shard_map/ppermute | solution.py:41
  45.3 5.6 %shard_map.312 = (bf16[576,256]{1,0:T(8,128)(2,1)S(1)}, f32[576,128]{1,0:T(8,128)S(1)}) custom-call(bf16[576,768]{1,0:T(8,128)(2,1)S(1)} %get-tuple-element.217.refs_0_.refs_5_, bf16[576,768]{1,0:T(8,128)(2,1)S(1)} %get-tuple-element.218.refs_1_, bf16[576,768]{1,0:T(8,128)(2,1)S(1)} %get-tuple-element.219.refs_2_, ...), custom_call_target="tpu_custom_call" | custom-call | tf_op jit(solution)/shard_map/pallas_call | solution.py:392
  51.0 3.5 %collective-permute-done.10.refs_1_ = bf16[288,768]{1,0:T(8,128)(2,1)S(1)} collective-permute-done((bf16[288,768]{1,0:T(8,128)(2,1)S(1)}, bf16[288,768]{1,0:T(8,128)(2,1)S(1)}, u32[]{:S(2)}, u32[]{:S(2)}) %collective-permute-start.10) | collective-permute-done | bytes 442400 | tf_op jit(solution)/shard_map/ppermute | solution.py:41
  54.6 2.1 collective-permute-start.12
  56.8 1.8 collective-permute-start.14
  58.6 11.2 %shard_map.313 = (bf16[576,512]{1,0:T(8,128)(2,1)S(1)}, f32[576,128]{1,0:T(8,128)S(1)}) custom-call(bf16[576,768]{1,0:T(8,128)(2,1)S(1)} %get-tuple-element.217.refs_0_.refs_5_, bf16[576,768]{1,0:T(8,128)(2,1)S(1)} %get-tuple-element.218.refs_1_, bf16[576,768]{1,0:T(8,128)(2,1)S(1)} %get-tuple-element.219.refs_2_, ...), custom_call_target="tpu_custom_call" | custom-call | tf_op jit(solution)/shard_map/pallas_call | solution.py:392
  70.7 1.8 collective-permute-done.15.refs_3_
  73.1 8.7 %shard_map.318 = (bf16[576,768]{1,0:T(8,128)(2,1)S(1)}, f32[576,768]{1,0:T(8,128)S(1)}, f32[576,768]{1,0:T(8,128)S(1)}, bf16[576,768]{1,0:T(8,128)(2,1)S(1)}, bf...) custom-call(bf16[576,256]{1,0:T(8,128)(2,1)S(1)} %get-tuple-element.222.refs_8_.refs_2_.refs_0_, ...), custom_call_target="tpu_custom_call" | custom-call | tf_op jit(solution)/shard_map/pallas_call | solution.py:82
  83.1 4.0 %shard_map.321 = (bf16[576,768]{1,0:T(8,128)(2,1)S(1)}, bf16[576,768]{1,0:T(8,128)(2,1)S(1)}, f32[1,768]{1,0:T(1,128)S(1)}, bf16[384,768]{1,0:T(8,128)(2,1)S(1)}...) custom-call(bf16[576,3072]{1,0:T(8,128)(2,1)S(1)} %get-tuple-element, ...), custom_call_target="tpu_custom_call" | custom-call | tf_op jit(solution)/shard_map/pallas_call | solution.py:82
  90.8 8.2 %shard_map.323 = (bf16[144,768]{1,0:T(8,128)(2,1)S(1)}, bf16[144,768]{1,0:T(8,128)(2,1)S(1)}, bf16[144,768]{1,0:T(8,128)(2,1)S(1)}, bf16[144,768]{1,0:T(8,128)(2...) custom-call(bf16[576,3072]{1,0:T(8,128)(2,1)S(1)} %get-tuple-element.242.refs_0_, ...), custom_call_target="tpu_custom_call" | custom-call | tf_op jit(solution)/shard_map/pallas_call | solution.py:82
  102.7 3.7 %collective-permute-start.26 = (bf16[288,768]{1,0:T(8,128)(2,1)S(1)}, bf16[288,768]{1,0:T(8,128)(2,1)S(1)}, u32[]{:S(2)}, u32[]{:S(2)}) collective-permute-start(bf16[288,768]{1,0:T(8,128)(2,1)S(1)} %pad_maximum_fusion.2), channel_id=1, source_target_pairs={{0,4},{1,3},{2,6},{3,1},{4,0},{5,7},{6,2},{7,5},{8,12},{9,11},{10,... | collective-permute-start | bytes 1327112 | tf_op jit(solution)/shard_map/ppermute | solution.py:41
  106.5 6.1 %shard_map.326 = (f32[576,768]{1,0:T(8,128)S(1)}, bf16[576,768]{1,0:T(8,128)(2,1)S(1)}, bf16[576,768]{1,0:T(8,128)(2,1)S(1)}, f32[4,768]{1,0:T(4,128)S(1)}) custom-call(bf16[576,3072]{1,0:T(8,128)(2,1)S(1)} %get-tuple-element.268.refs_4_.refs_0_, f32[576,768]{1,0:T(8,128)S(1)} %get-tuple-element.244.refs_2_.refs_1_, ...), custom_call_target="tpu_custom_call" | custom-call | tf_op jit(solution)/shard_map/pallas_call | solution.py:82
  112.6 5.3 %shard_map.327 = (bf16[96,3840]{1,0:T(8,128)(2,1)S(1)}, bf16[96,3840]{1,0:T(8,128)(2,1)S(1)}, bf16[96,3840]{1,0:T(8,128)(2,1)S(1)}, bf16[96,3840]{1,0:T(8,128)(2...) custom-call(bf16[576,3072]{1,0:T(8,128)(2,1)S(1)} %get-tuple-element, ...), custom_call_target="tpu_custom_call" | custom-call | tf_op jit(solution)/shard_map/pallas_call | solution.py:82
  124.8 4.6 %shard_map.329 = (bf16[576,128]{1,0:T(8,128)(2,1)S(1)}, bf16[2,576,128]{2,1,0:T(8,128)(2,1)S(1)}, bf16[2,576,128]{2,1,0:T(8,128)(2,1)S(1)}) custom-call(bf16[576,768]{1,0:T(8,128)(2,1)S(1)} %get-tuple-element.217.refs_0_.refs_5_, bf16[576,768]{1,0:T(8,128)(2,1)S(1)} %get-tuple-element.218.refs_1_, bf16[576,768]{1,0:T(8,128)(2,1)S(1)} %get-tuple-element.219.refs_2_, ...), custom_call_target="tpu_custom_call" | custom-call | tf_op jit(solution)/shard_map/pallas_call | solution.py:601
  129.3 4.3 %shard_map.330 = (bf16[576,128]{1,0:T(8,128)(2,1)S(1)}, bf16[2,576,128]{2,1,0:T(8,128)(2,1)S(1)}, bf16[2,576,128]{2,1,0:T(8,128)(2,1)S(1)}) custom-call(bf16[576,768]{1,0:T(8,128)(2,1)S(1)} %get-tuple-element.217.refs_0_.refs_5_, bf16[576,768]{1,0:T(8,128)(2,1)S(1)} %get-tuple-element.218.refs_1_, bf16[576,768]{1,0:T(8,128)(2,1)S(1)} %get-tuple-element.219.refs_2_, ...), custom_call_target="tpu_custom_call" | custom-call | tf_op jit(solution)/shard_map/pallas_call | solution.py:601
  133.7 6.6 %collective-permute-done.27.refs_0_ = bf16[384,768]{1,0:T(8,128)(2,1)S(1)} collective-permute-done((bf16[384,768]{1,0:T(8,128)(2,1)S(1)}, bf16[384,768]{1,0:T(8,128)(2,1)S(1)}, u32[]{:S(2)}, u32[]{:S(2)}) %collective-permute-start.27) | collective-permute-done | bytes 589856 | tf_op jit(solution)/shard_map/ppermute | solution.py:41
  142.4 2.1 collective-permute-start.35
  145.1 4.3 %shard_map.331 = (bf16[576,128]{1,0:T(8,128)(2,1)S(1)}, bf16[2,576,128]{2,1,0:T(8,128)(2,1)S(1)}, bf16[2,576,128]{2,1,0:T(8,128)(2,1)S(1)}) custom-call(bf16[576,768]{1,0:T(8,128)(2,1)S(1)} %get-tuple-element.217.refs_0_.refs_5_, bf16[576,768]{1,0:T(8,128)(2,1)S(1)} %get-tuple-element.218.refs_1_, bf16[576,768]{1,0:T(8,128)(2,1)S(1)} %get-tuple-element.219.refs_2_, ...), custom_call_target="tpu_custom_call" | custom-call | tf_op jit(solution)/shard_map/pallas_call | solution.py:601
  149.4 4.8 %shard_map.332 = (bf16[576,128]{1,0:T(8,128)(2,1)S(1)}, bf16[2,576,128]{2,1,0:T(8,128)(2,1)S(1)}, bf16[2,576,128]{2,1,0:T(8,128)(2,1)S(1)}) custom-call(bf16[576,768]{1,0:T(8,128)(2,1)S(1)} %get-tuple-element.217.refs_0_.refs_5_, bf16[576,768]{1,0:T(8,128)(2,1)S(1)} %get-tuple-element.218.refs_1_, bf16[576,768]{1,0:T(8,128)(2,1)S(1)} %get-tuple-element.219.refs_2_, ...), custom_call_target="tpu_custom_call" | custom-call | tf_op jit(solution)/shard_map/pallas_call | solution.py:601
  154.2 5.3 %collective-permute-done.35.refs_1_ = bf16[384,768]{1,0:T(8,128)(2,1)S(1)} collective-permute-done((bf16[384,768]{1,0:T(8,128)(2,1)S(1)}, bf16[384,768]{1,0:T(8,128)(2,1)S(1)}, u32[]{:S(2)}, u32[]{:S(2)}) %collective-permute-start.35) | collective-permute-done | bytes 589856 | tf_op jit(solution)/shard_map/ppermute | solution.py:41
  161.0 4.3 %shard_map.333 = (bf16[576,128]{1,0:T(8,128)(2,1)S(1)}, bf16[2,576,128]{2,1,0:T(8,128)(2,1)S(1)}, bf16[2,576,128]{2,1,0:T(8,128)(2,1)S(1)}) custom-call(bf16[576,768]{1,0:T(8,128)(2,1)S(1)} %get-tuple-element.217.refs_0_.refs_5_, bf16[576,768]{1,0:T(8,128)(2,1)S(1)} %get-tuple-element.218.refs_1_, bf16[576,768]{1,0:T(8,128)(2,1)S(1)} %get-tuple-element.219.refs_2_, ...), custom_call_target="tpu_custom_call" | custom-call | tf_op jit(solution)/shard_map/pallas_call | solution.py:601
  165.3 4.3 %shard_map.334 = (bf16[576,128]{1,0:T(8,128)(2,1)S(1)}, bf16[2,576,128]{2,1,0:T(8,128)(2,1)S(1)}, bf16[2,576,128]{2,1,0:T(8,128)(2,1)S(1)}) custom-call(bf16[576,768]{1,0:T(8,128)(2,1)S(1)} %get-tuple-element.217.refs_0_.refs_5_, bf16[576,768]{1,0:T(8,128)(2,1)S(1)} %get-tuple-element.218.refs_1_, bf16[576,768]{1,0:T(8,128)(2,1)S(1)} %get-tuple-element.219.refs_2_, ...), custom_call_target="tpu_custom_call" | custom-call | tf_op jit(solution)/shard_map/pallas_call | solution.py:601
  172.0 1.7 copy-done.2
  173.7 3.6 %shard_map.340 = (bf16[576,2304]{1,0:T(8,128)(2,1)S(1)}, f32[2,768]{1,0:T(2,128)S(1)}, bf16[96,2304]{1,0:T(8,128)(2,1)S(1)}, bf16[96,2304]{1,0:T(8,128)(2,1)S(1)...) custom-call(bf16[576,128]{1,0:T(8,128)(2,1)S(1)} %get-tuple-element., ...), custom_call_target="tpu_custom_call" | custom-call | tf_op jit(solution)/shard_map/pallas_call | solution.py:82
  177.4 1.9 collective-permute-done.43.refs_4_
  181.8 1.8 collective-permute-start.47
  184.9 6.9 %shard_map.343 = (bf16[144,768]{1,0:T(8,128)(2,1)S(1)}, bf16[144,768]{1,0:T(8,128)(2,1)S(1)}, bf16[144,768]{1,0:T(8,128)(2,1)S(1)}, bf16[144,768]{1,0:T(8,128)(2,1)S(1)}, f32[16,768]{1,0:T(8,128)S(1)}) custom-call(bf16[576,2304]{1,0:T(8,128)(2,1)S(1)} %get-tuple-element.343.refs_5_.refs_0_, bf16[576,768]{1,0:T(8,128)(2,1)S(1)} %copy-done.6, ...), custom_call_target="tpu_custom_call" | custom-call | tf_op jit(solution)/shard_map/pallas_call | solution.py:82
  192.8 2.1 collective-permute-done.46.refs_0_
  196.4 2.0 collective-permute-start.50
  198.5 13.4 %collective-permute-done.52.refs_2_ = bf16[96,3840]{1,0:T(8,128)(2,1)S(1)} collective-permute-done((bf16[96,3840]{1,0:T(8,128)(2,1)S(1)}, bf16[96,3840]{1,0:T(8,128)(2,1)S(1)}, u32[]{:S(2)}, u32[]{:S(2)}) %collective-permute-start.52) | collective-permute-done | bytes 737312 | tf_op jit(solution)/shard_map/ppermute | solution.py:41
  211.9 9.7 %collective-permute-done.51.refs_1_ = bf16[288,768]{1,0:T(8,128)(2,1)S(1)} collective-permute-done((bf16[288,768]{1,0:T(8,128)(2,1)S(1)}, bf16[288,768]{1,0:T(8,128)(2,1)S(1)}, u32[]{:S(2)}, u32[]{:S(2)}) %collective-permute-start.51) | collective-permute-done | bytes 442400 | tf_op jit(solution)/shard_map/ppermute | solution.py:41
  222.3 2.1 collective-permute-start.55
  224.5 1.8 collective-permute-start.58
  226.3 2.5 collective-permute-start.59
  228.8 2.2 shard_map.346.refs_1_
  232.1 1.8 shard_map.348
  233.9 11.8 %collective-permute-done.57.refs_3_ = f32[16,768]{1,0:T(8,128)S(1)} collective-permute-done((f32[16,768]{1,0:T(8,128)S(1)}, f32[16,768]{1,0:T(8,128)S(1)}, u32[]{:S(2)}, u32[]{:S(2)}) %collective-permute-start.57) | collective-permute-done | bytes 49184 | tf_op jit(solution)/shard_map/ppermute | solution.py:41
  247.2 1.7 copy-done.10
  253.2 2.2 shard_map.350.refs_5_
  256.8 5.7 %collective-permute-done.61.refs_0_ = bf16[96,2304]{1,0:T(8,128)(2,1)S(1)} collective-permute-done((bf16[96,2304]{1,0:T(8,128)(2,1)S(1)}, bf16[96,2304]{1,0:T(8,128)(2,1)S(1)}, u32[]{:S(2)}, u32[]{:S(2)}) %collective-permute-start.61) | collective-permute-done | bytes 442400 | tf_op jit(solution)/shard_map/ppermute | solution.py:41
  (212 shorter events, 52.4 us)
Async XLA Ops:
  3.2 27.6 %collective-permute-start.3 = (bf16[208,2304]{1,0:T(8,128)(2,1)}, bf16[208,2304]{1,0:T(8,128)(2,1)S(1)}, u32[]{:S(2)}, u32[]{:S(2)}) collective-permute-start(bf16[208,2304]{1,0:T(8,128)(2,1)} %get-tuple-element.205.refs_2_.refs_3_.refs_1_.refs_4_), channel_id=1, source_target_pairs={{0,8},{1,17},{2,10},{3,19},{4,12},{5,21},{6,14},{7,23},{8,0},{9,25... | collective-permute-start | bytes 2875400 | tf_op jit(solution)/shard_map/ppermute | solution.py:41
  6.2 24.6 %collective-permute-start.4 = (bf16[112,2304]{1,0:T(8,128)(2,1)}, bf16[112,2304]{1,0:T(8,128)(2,1)S(1)}, u32[]{:S(2)}, u32[]{:S(2)}) collective-permute-start(bf16[112,2304]{1,0:T(8,128)(2,1)} %get-tuple-element.210), channel_id=1, source_target_pairs={{0,24},{1,25},{2,26},{3,27},{4,28},{5,29},{6,30},{7,31},{8,16},{9,... | collective-permute-start | bytes 1548296 | tf_op jit(solution)/shard_map/ppermute | solution.py:41
  10.0 18.9 %collective-permute-start = (bf16[144,768]{1,0:T(8,128)(2,1)}, bf16[144,768]{1,0:T(8,128)(2,1)S(1)}, u32[]{:S(2)}, u32[]{:S(2)}) collective-permute-start(bf16[144,768]{1,0:T(8,128)(2,1)} %get-tuple-element.207), channel_id=1, source_target_pairs={{0,4},{1,3},{2,6},{3,1},{4,0},{5,7},{6,2},{7,5},{8,12},{9,11},{10,... | collective-permute-start | bytes 663560 | tf_op jit(solution)/shard_map/ppermute | solution.py:41
  12.6 16.3 %collective-permute-start.1 = (bf16[144,768]{1,0:T(8,128)(2,1)}, bf16[144,768]{1,0:T(8,128)(2,1)S(1)}, u32[]{:S(2)}, u32[]{:S(2)}) collective-permute-start(bf16[144,768]{1,0:T(8,128)(2,1)} %get-tuple-element.208), channel_id=1, source_target_pairs={{0,2},{1,5},{2,0},{3,7},{4,6},{5,1},{6,4},{7,3},{8,10},{9,13},{10,... | collective-permute-start | bytes 663560 | tf_op jit(solution)/shard_map/ppermute | solution.py:41
  14.2 14.7 %collective-permute-start.2 = (bf16[144,768]{1,0:T(8,128)(2,1)}, bf16[144,768]{1,0:T(8,128)(2,1)S(1)}, u32[]{:S(2)}, u32[]{:S(2)}) collective-permute-start(bf16[144,768]{1,0:T(8,128)(2,1)} %get-tuple-element.209), channel_id=1, source_target_pairs={{0,6},{1,7},{2,4},{3,5},{4,2},{5,3},{6,0},{7,1},{8,14},{9,15},{10,... | collective-permute-start | bytes 663560 | tf_op jit(solution)/shard_map/ppermute | solution.py:41
  30.8 23.6 %collective-permute-start.9 = (bf16[192,3840]{1,0:T(8,128)(2,1)S(1)}, bf16[192,3840]{1,0:T(8,128)(2,1)S(1)}, u32[]{:S(2)}, u32[]{:S(2)}) collective-permute-start(bf16[192,3840]{1,0:T(8,128)(2,1)S(1)} %get-tuple-element.227), channel_id=1, source_target_pairs={{0,8},{1,17},{2,10},{3,19},{4,12},{5,21},{6,14},{7,23},{8,0},{9,25... | collective-permute-start | bytes 4423688 | tf_op jit(solution)/shard_map/ppermute | solution.py:41
  40.6 13.9 %collective-permute-start.10 = (bf16[288,768]{1,0:T(8,128)(2,1)S(1)}, bf16[288,768]{1,0:T(8,128)(2,1)S(1)}, u32[]{:S(2)}, u32[]{:S(2)}) collective-permute-start(bf16[288,768]{1,0:T(8,128)(2,1)S(1)} %pad_maximum_fusion), channel_id=1, source_target_pairs={{0,4},{1,3},{2,6},{3,1},{4,0},{5,7},{6,2},{7,5},{8,12},{9,11},{10,... | collective-permute-start | bytes 1327112 | tf_op jit(solution)/shard_map/ppermute | solution.py:41
  44.6 25.3 %collective-permute-start.13 = (bf16[768,768]{1,0:T(8,128)(2,1)S(1)}, bf16[768,768]{1,0:T(8,128)(2,1)S(1)}, u32[]{:S(2)}, u32[]{:S(2)}) collective-permute-start(bf16[768,768]{1,0:T(8,128)(2,1)S(1)} %get-tuple-element.234), channel_id=1, source_target_pairs={{0,8},{1,17},{2,10},{3,19},{4,12},{5,21},{6,14},{7,23},{8,0},{9,25... | collective-permute-start | bytes 3538952 | tf_op jit(solution)/shard_map/ppermute | solution.py:41
  54.5 18.0 %collective-permute-start.11 = (bf16[192,3840]{1,0:T(8,128)(2,1)S(1)}, bf16[192,3840]{1,0:T(8,128)(2,1)S(1)}, u32[]{:S(2)}, u32[]{:S(2)}) collective-permute-start(bf16[192,3840]{1,0:T(8,128)(2,1)S(1)} %get-tuple-element.233.refs_0_), channel_id=1, source_target_pairs={{0,1},{1,0},{2,3},{3,2},{4,5},{5,4},{6,7},{7,6},{8,9},{9,8},{10,11... | collective-permute-start | bytes 4423688 | tf_op jit(solution)/shard_map/ppermute | solution.py:41
  54.6 15.7 %collective-permute-start.12 = (bf16[96,3840]{1,0:T(8,128)(2,1)S(1)}, bf16[96,3840]{1,0:T(8,128)(2,1)S(1)}, u32[]{:S(2)}, u32[]{:S(2)}) collective-permute-start(bf16[96,3840]{1,0:T(8,128)(2,1)S(1)} %slice.75), channel_id=1, source_target_pairs={{0,16},{1,9},{2,18},{3,11},{4,20},{5,13},{6,22},{7,15},{8,24},{9,1... | collective-permute-start | bytes 2211848 | tf_op jit(solution)/shard_map/ppermute | solution.py:41
  56.8 13.1 %collective-permute-start.14 = (bf16[288,768]{1,0:T(8,128)(2,1)S(1)}, bf16[288,768]{1,0:T(8,128)(2,1)S(1)}, u32[]{:S(2)}, u32[]{:S(2)}) collective-permute-start(bf16[288,768]{1,0:T(8,128)(2,1)S(1)} %pad_maximum_fusion.1), channel_id=1, source_target_pairs={{0,2},{1,5},{2,0},{3,7},{4,6},{5,1},{6,4},{7,3},{8,10},{9,13},{10,... | collective-permute-start | bytes 1327112 | tf_op jit(solution)/shard_map/ppermute | solution.py:41
  72.5 10.2 %collective-permute-start.17 = (bf16[768,768]{1,0:T(8,128)(2,1)S(1)}, bf16[768,768]{1,0:T(8,128)(2,1)S(1)}, u32[]{:S(2)}, u32[]{:S(2)}) collective-permute-start(bf16[768,768]{1,0:T(8,128)(2,1)S(1)} %shard_map.319.refs_4_), channel_id=1, source_target_pairs={{0,1},{1,0},{2,3},{3,2},{4,5},{5,4},{6,7},{7,6},{8,9},{9,8},{10,11... | collective-permute-start | bytes 3538952 | tf_op jit(solution)/shard_map/ppermute | solution.py:41
  72.8 9.9 %collective-permute-start.16 = (bf16[384,768]{1,0:T(8,128)(2,1)S(1)}, bf16[384,768]{1,0:T(8,128)(2,1)S(1)}, u32[]{:S(2)}, u32[]{:S(2)}) collective-permute-start(bf16[384,768]{1,0:T(8,128)(2,1)S(1)} %slice.80), channel_id=1, source_target_pairs={{0,16},{1,9},{2,18},{3,11},{4,20},{5,13},{6,22},{7,15},{8,24},{9,1... | collective-permute-start | bytes 1769480 | tf_op jit(solution)/shard_map/ppermute | solution.py:41
  87.9 11.1 %collective-permute-start.21 = (bf16[384,768]{1,0:T(8,128)(2,1)S(1)}, bf16[384,768]{1,0:T(8,128)(2,1)S(1)}, u32[]{:S(2)}, u32[]{:S(2)}) collective-permute-start(bf16[384,768]{1,0:T(8,128)(2,1)S(1)} %get-tuple-element.265), channel_id=1, source_target_pairs={{0,1},{1,0},{2,3},{3,2},{4,5},{5,4},{6,7},{7,6},{8,9},{9,8},{10,11... | collective-permute-start | bytes 1769480 | tf_op jit(solution)/shard_map/ppermute | solution.py:41
  87.9 11.0 %collective-permute-start.22 = (bf16[384,768]{1,0:T(8,128)(2,1)S(1)}, bf16[384,768]{1,0:T(8,128)(2,1)S(1)}, u32[]{:S(2)}, u32[]{:S(2)}) collective-permute-start(bf16[384,768]{1,0:T(8,128)(2,1)S(1)} %get-tuple-element.266), channel_id=1, source_target_pairs={{0,1},{1,0},{2,3},{3,2},{4,5},{5,4},{6,7},{7,6},{8,9},{9,8},{10,11... | collective-permute-start | bytes 1769480 | tf_op jit(solution)/shard_map/ppermute | solution.py:41
  88.4 10.6 %collective-permute-start.23 = (bf16[384,768]{1,0:T(8,128)(2,1)S(1)}, bf16[384,768]{1,0:T(8,128)(2,1)S(1)}, u32[]{:S(2)}, u32[]{:S(2)}) collective-permute-start(bf16[384,768]{1,0:T(8,128)(2,1)S(1)} %get-tuple-element.267), channel_id=1, source_target_pairs={{0,1},{1,0},{2,3},{3,2},{4,5},{5,4},{6,7},{7,6},{8,9},{9,8},{10,11... | collective-permute-start | bytes 1769480 | tf_op jit(solution)/shard_map/ppermute | solution.py:41
  89.7 9.9 %collective-permute-start.20 = (bf16[384,768]{1,0:T(8,128)(2,1)S(1)}, bf16[384,768]{1,0:T(8,128)(2,1)S(1)}, u32[]{:S(2)}, u32[]{:S(2)}) collective-permute-start(bf16[384,768]{1,0:T(8,128)(2,1)S(1)} %add_convert_fusion.11), channel_id=1, source_target_pairs={{0,16},{1,9},{2,18},{3,11},{4,20},{5,13},{6,22},{7,15},{8,24},{9,1... | collective-permute-start | bytes 1769480 | tf_op jit(solution)/shard_map/ppermute | solution.py:41
  99.8 18.1 %collective-permute-start.25 = (bf16[384,768]{1,0:T(8,128)(2,1)S(1)}, bf16[384,768]{1,0:T(8,128)(2,1)S(1)}, u32[]{:S(2)}, u32[]{:S(2)}) collective-permute-start(bf16[384,768]{1,0:T(8,128)(2,1)S(1)} %add_convert_fusion.9), channel_id=1, source_target_pairs={{0,16},{1,9},{2,18},{3,11},{4,20},{5,13},{6,22},{7,15},{8,24},{9,1... | collective-permute-start | bytes 1769480 | tf_op jit(solution)/shard_map/ppermute | solution.py:41
  101.1 16.8 %collective-permute-start.24 = (bf16[384,768]{1,0:T(8,128)(2,1)S(1)}, bf16[384,768]{1,0:T(8,128)(2,1)S(1)}, u32[]{:S(2)}, u32[]{:S(2)}) collective-permute-start(bf16[384,768]{1,0:T(8,128)(2,1)S(1)} %add_convert_fusion.10), channel_id=1, source_target_pairs={{0,8},{1,17},{2,10},{3,19},{4,12},{5,21},{6,14},{7,23},{8,0},{9,25... | collective-permute-start | bytes 1769480 | tf_op jit(solution)/shard_map/ppermute | solution.py:41
  102.7 15.2 %collective-permute-start.26 = (bf16[288,768]{1,0:T(8,128)(2,1)S(1)}, bf16[288,768]{1,0:T(8,128)(2,1)S(1)}, u32[]{:S(2)}, u32[]{:S(2)}) collective-permute-start(bf16[288,768]{1,0:T(8,128)(2,1)S(1)} %pad_maximum_fusion.2), channel_id=1, source_target_pairs={{0,4},{1,3},{2,6},{3,1},{4,0},{5,7},{6,2},{7,5},{8,12},{9,11},{10,... | collective-permute-start | bytes 1327112 | tf_op jit(solution)/shard_map/ppermute | solution.py:41
  118.5 21.7 %collective-permute-start.32 = (bf16[96,3840]{1,0:T(8,128)(2,1)S(1)}, bf16[96,3840]{1,0:T(8,128)(2,1)S(1)}, u32[]{:S(2)}, u32[]{:S(2)}) collective-permute-start(bf16[96,3840]{1,0:T(8,128)(2,1)S(1)} %get-tuple-element.309), channel_id=1, source_target_pairs={{0,1},{1,0},{2,3},{3,2},{4,5},{5,4},{6,7},{7,6},{8,9},{9,8},{10,11... | collective-permute-start | bytes 2211848 | tf_op jit(solution)/shard_map/ppermute | solution.py:41
  118.6 21.6 %collective-permute-start.33 = (bf16[96,3840]{1,0:T(8,128)(2,1)S(1)}, bf16[96,3840]{1,0:T(8,128)(2,1)S(1)}, u32[]{:S(2)}, u32[]{:S(2)}) collective-permute-start(bf16[96,3840]{1,0:T(8,128)(2,1)S(1)} %get-tuple-element.310), channel_id=1, source_target_pairs={{0,1},{1,0},{2,3},{3,2},{4,5},{5,4},{6,7},{7,6},{8,9},{9,8},{10,11... | collective-permute-start | bytes 2211848 | tf_op jit(solution)/shard_map/ppermute | solution.py:41
  121.4 18.8 %collective-permute-start.31 = (bf16[96,3840]{1,0:T(8,128)(2,1)S(1)}, bf16[96,3840]{1,0:T(8,128)(2,1)S(1)}, u32[]{:S(2)}, u32[]{:S(2)}) collective-permute-start(bf16[96,3840]{1,0:T(8,128)(2,1)S(1)} %add_convert_fusion.4), channel_id=1, source_target_pairs={{0,16},{1,9},{2,18},{3,11},{4,20},{5,13},{6,22},{7,15},{8,24},{9,1... | collective-permute-start | bytes 2211848 | tf_op jit(solution)/shard_map/ppermute | solution.py:41
  122.7 18.2 %collective-permute-start.30 = (bf16[96,3840]{1,0:T(8,128)(2,1)S(1)}, bf16[96,3840]{1,0:T(8,128)(2,1)S(1)}, u32[]{:S(2)}, u32[]{:S(2)}) collective-permute-start(bf16[96,3840]{1,0:T(8,128)(2,1)S(1)} %add_convert_fusion.5), channel_id=1, source_target_pairs={{0,16},{1,9},{2,18},{3,11},{4,20},{5,13},{6,22},{7,15},{8,24},{9,1... | collective-permute-start | bytes 2211848 | tf_op jit(solution)/shard_map/ppermute | solution.py:41
  124.1 16.1 %collective-permute-start.27 = (bf16[384,768]{1,0:T(8,128)(2,1)S(1)}, bf16[384,768]{1,0:T(8,128)(2,1)S(1)}, u32[]{:S(2)}, u32[]{:S(2)}) collective-permute-start(bf16[384,768]{1,0:T(8,128)(2,1)S(1)} %add_convert_fusion.8), channel_id=1, source_target_pairs={{0,2},{1,5},{2,0},{3,7},{4,6},{5,1},{6,4},{7,3},{8,10},{9,13},{10,... | collective-permute-start | bytes 1769480 | tf_op jit(solution)/shard_map/ppermute | solution.py:41
  141.2 18.4 %collective-permute-start.34 = (bf16[96,3840]{1,0:T(8,128)(2,1)S(1)}, bf16[96,3840]{1,0:T(8,128)(2,1)S(1)}, u32[]{:S(2)}, u32[]{:S(2)}) collective-permute-start(bf16[96,3840]{1,0:T(8,128)(2,1)S(1)} %add_convert_fusion.3), channel_id=1, source_target_pairs={{0,8},{1,17},{2,10},{3,19},{4,12},{5,21},{6,14},{7,23},{8,0},{9,25... | collective-permute-start | bytes 2211848 | tf_op jit(solution)/shard_map/ppermute | solution.py:41
  142.4 17.2 %collective-permute-start.35 = (bf16[384,768]{1,0:T(8,128)(2,1)S(1)}, bf16[384,768]{1,0:T(8,128)(2,1)S(1)}, u32[]{:S(2)}, u32[]{:S(2)}) collective-permute-start(bf16[384,768]{1,0:T(8,128)(2,1)S(1)} %add_convert_fusion.7), channel_id=1, source_target_pairs={{0,4},{1,3},{2,6},{3,1},{4,0},{5,7},{6,2},{7,5},{8,12},{9,11},{10,... | collective-permute-start | bytes 1769480 | tf_op jit(solution)/shard_map/ppermute | solution.py:41
  144.6 9.7 %collective-permute-start.36 = (bf16[2,576,128]{2,1,0:T(8,128)(2,1)S(1)}, bf16[2,576,128]{2,1,0:T(8,128)(2,1)S(1)}, u32[]{:S(2)}, u32[]{:S(2)}) collective-permute-start(bf16[2,576,128]{2,1,0:T(8,128)(2,1)S(1)} %get-tuple-element.316), channel_id=1, source_target_pairs={{0,1},{1,0},{2,3},{3,2},{4,5},{5,4},{6,7},{7,6},{8,9},{9,8},{10,11... | collective-permute-start | bytes 884744 | tf_op jit(solution)/shard_map/ppermute | solution.py:41
  144.6 9.7 %collective-permute-start.37 = (bf16[2,576,128]{2,1,0:T(8,128)(2,1)S(1)}, bf16[2,576,128]{2,1,0:T(8,128)(2,1)S(1)}, u32[]{:S(2)}, u32[]{:S(2)}) collective-permute-start(bf16[2,576,128]{2,1,0:T(8,128)(2,1)S(1)} %get-tuple-element.317), channel_id=1, source_target_pairs={{0,1},{1,0},{2,3},{3,2},{4,5},{5,4},{6,7},{7,6},{8,9},{9,8},{10,11... | collective-permute-start | bytes 884744 | tf_op jit(solution)/shard_map/ppermute | solution.py:41
  159.7 9.9 %collective-permute-start.38 = (bf16[384,768]{1,0:T(8,128)(2,1)S(1)}, bf16[384,768]{1,0:T(8,128)(2,1)S(1)}, u32[]{:S(2)}, u32[]{:S(2)}) collective-permute-start(bf16[384,768]{1,0:T(8,128)(2,1)S(1)} %add_convert_fusion.6.refs_0_), channel_id=1, source_target_pairs={{0,1},{1,0},{2,3},{3,2},{4,5},{5,4},{6,7},{7,6},{8,9},{9,8},{10,11... | collective-permute-start | bytes 1769480 | tf_op jit(solution)/shard_map/ppermute | solution.py:41
  160.3 19.0 %collective-permute-start.43 = (bf16[96,3840]{1,0:T(8,128)(2,1)S(1)}, bf16[96,3840]{1,0:T(8,128)(2,1)S(1)}, u32[]{:S(2)}, u32[]{:S(2)}) collective-permute-start(bf16[96,3840]{1,0:T(8,128)(2,1)S(1)} %add_convert_fusion.2), channel_id=1, source_target_pairs={{0,2},{1,5},{2,0},{3,7},{4,6},{5,1},{6,4},{7,3},{8,10},{9,13},{10,... | collective-permute-start | bytes 2211848 | tf_op jit(solution)/shard_map/ppermute | solution.py:41
  160.3 9.3 %collective-permute-start.39 = (bf16[2,576,128]{2,1,0:T(8,128)(2,1)S(1)}, bf16[2,576,128]{2,1,0:T(8,128)(2,1)S(1)}, u32[]{:S(2)}, u32[]{:S(2)}) collective-permute-start(bf16[2,576,128]{2,1,0:T(8,128)(2,1)S(1)} %get-tuple-element.323), channel_id=1, source_target_pairs={{0,1},{1,0},{2,3},{3,2},{4,5},{5,4},{6,7},{7,6},{8,9},{9,8},{10,11... | collective-permute-start | bytes 884744 | tf_op jit(solution)/shard_map/ppermute | solution.py:41
  160.9 8.8 %collective-permute-start.40 = (bf16[2,576,128]{2,1,0:T(8,128)(2,1)S(1)}, bf16[2,576,128]{2,1,0:T(8,128)(2,1)S(1)}, u32[]{:S(2)}, u32[]{:S(2)}) collective-permute-start(bf16[2,576,128]{2,1,0:T(8,128)(2,1)S(1)} %get-tuple-element.324), channel_id=1, source_target_pairs={{0,1},{1,0},{2,3},{3,2},{4,5},{5,4},{6,7},{7,6},{8,9},{9,8},{10,11... | collective-permute-start | bytes 884744 | tf_op jit(solution)/shard_map/ppermute | solution.py:41
  179.9 18.6 %collective-permute-start.53 = (bf16[288,768]{1,0:T(8,128)(2,1)S(1)}, bf16[288,768]{1,0:T(8,128)(2,1)S(1)}, u32[]{:S(2)}, u32[]{:S(2)}) collective-permute-start(bf16[288,768]{1,0:T(8,128)(2,1)S(1)} %pad_maximum_fusion.4), channel_id=1, source_target_pairs={{0,2},{1,5},{2,0},{3,7},{4,6},{5,1},{6,4},{7,3},{8,10},{9,13},{10,... | collective-permute-start | bytes 1327112 | tf_op jit(solution)/shard_map/ppermute | solution.py:41
  180.3 11.5 %collective-permute-start.48 = (bf16[96,2304]{1,0:T(8,128)(2,1)S(1)}, bf16[96,2304]{1,0:T(8,128)(2,1)S(1)}, u32[]{:S(2)}, u32[]{:S(2)}) collective-permute-start(bf16[96,2304]{1,0:T(8,128)(2,1)S(1)} %get-tuple-element.349), channel_id=1, source_target_pairs={{0,1},{1,0},{2,3},{3,2},{4,5},{5,4},{6,7},{7,6},{8,9},{9,8},{10,11... | collective-permute-start | bytes 1327112 | tf_op jit(solution)/shard_map/ppermute | solution.py:41
  180.8 12.0 %collective-permute-start.49 = (bf16[96,2304]{1,0:T(8,128)(2,1)S(1)}, bf16[96,2304]{1,0:T(8,128)(2,1)S(1)}, u32[]{:S(2)}, u32[]{:S(2)}) collective-permute-start(bf16[96,2304]{1,0:T(8,128)(2,1)S(1)} %get-tuple-element.350), channel_id=1, source_target_pairs={{0,1},{1,0},{2,3},{3,2},{4,5},{5,4},{6,7},{7,6},{8,9},{9,8},{10,11... | collective-permute-start | bytes 1327112 | tf_op jit(solution)/shard_map/ppermute | solution.py:41
  181.8 11.0 %collective-permute-start.47 = (bf16[96,2304]{1,0:T(8,128)(2,1)S(1)}, bf16[96,2304]{1,0:T(8,128)(2,1)S(1)}, u32[]{:S(2)}, u32[]{:S(2)}) collective-permute-start(bf16[96,2304]{1,0:T(8,128)(2,1)S(1)} %add_convert_fusion.16), channel_id=1, source_target_pairs={{0,16},{1,9},{2,18},{3,11},{4,20},{5,13},{6,22},{7,15},{8,24},{9,1... | collective-permute-start | bytes 1327112 | tf_op jit(solution)/shard_map/ppermute | solution.py:41
  183.7 11.2 %collective-permute-start.46 = (bf16[96,2304]{1,0:T(8,128)(2,1)S(1)}, bf16[96,2304]{1,0:T(8,128)(2,1)S(1)}, u32[]{:S(2)}, u32[]{:S(2)}) collective-permute-start(bf16[96,2304]{1,0:T(8,128)(2,1)S(1)} %add_convert_fusion.17), channel_id=1, source_target_pairs={{0,16},{1,9},{2,18},{3,11},{4,20},{5,13},{6,22},{7,15},{8,24},{9,1... | collective-permute-start | bytes 1327112 | tf_op jit(solution)/shard_map/ppermute | solution.py:41
  191.8 20.1 %collective-permute-start.52 = (bf16[96,3840]{1,0:T(8,128)(2,1)S(1)}, bf16[96,3840]{1,0:T(8,128)(2,1)S(1)}, u32[]{:S(2)}, u32[]{:S(2)}) collective-permute-start(bf16[96,3840]{1,0:T(8,128)(2,1)S(1)} %add_convert_fusion.1), channel_id=1, source_target_pairs={{0,4},{1,3},{2,6},{3,1},{4,0},{5,7},{6,2},{7,5},{8,12},{9,11},{10,... | collective-permute-start | bytes 2211848 | tf_op jit(solution)/shard_map/ppermute | solution.py:41
  195.0 26.7 %collective-permute-start.51 = (bf16[288,768]{1,0:T(8,128)(2,1)S(1)}, bf16[288,768]{1,0:T(8,128)(2,1)S(1)}, u32[]{:S(2)}, u32[]{:S(2)}) collective-permute-start(bf16[288,768]{1,0:T(8,128)(2,1)S(1)} %pad_maximum_fusion.3), channel_id=1, source_target_pairs={{0,4},{1,3},{2,6},{3,1},{4,0},{5,7},{6,2},{7,5},{8,12},{9,11},{10,... | collective-permute-start | bytes 1327112 | tf_op jit(solution)/shard_map/ppermute | solution.py:41
  196.4 25.2 %collective-permute-start.50 = (bf16[96,2304]{1,0:T(8,128)(2,1)S(1)}, bf16[96,2304]{1,0:T(8,128)(2,1)S(1)}, u32[]{:S(2)}, u32[]{:S(2)}) collective-permute-start(bf16[96,2304]{1,0:T(8,128)(2,1)S(1)} %add_convert_fusion.15), channel_id=1, source_target_pairs={{0,8},{1,17},{2,10},{3,19},{4,12},{5,21},{6,14},{7,23},{8,0},{9,25... | collective-permute-start | bytes 1327112 | tf_op jit(solution)/shard_map/ppermute | solution.py:41
  198.5 13.4 %collective-permute-start.54 = (f32[16,768]{1,0:T(8,128)S(1)}, f32[16,768]{1,0:T(8,128)S(1)}, u32[]{:S(2)}, u32[]{:S(2)}) collective-permute-start(f32[16,768]{1,0:T(8,128)S(1)} %get-tuple-element.368.refs_4_), channel_id=1, source_target_pairs={{0,1},{1,0},{2,3},{3,2},{4,5},{5,4},{6,7},{7,6},{8,9},{9,8},{10,11... | collective-permute-start | bytes 147464 | tf_op jit(solution)/shard_map/ppermute | solution.py:41
  222.0 25.2 %collective-permute-start.56 = (bf16[288,768]{1,0:T(8,128)(2,1)S(1)}, bf16[288,768]{1,0:T(8,128)(2,1)S(1)}, u32[]{:S(2)}, u32[]{:S(2)}) collective-permute-start(bf16[288,768]{1,0:T(8,128)(2,1)S(1)} %pad_maximum_fusion.5), channel_id=1, source_target_pairs={{0,2},{1,5},{2,0},{3,7},{4,6},{5,1},{6,4},{7,3},{8,10},{9,13},{10,... | collective-permute-start | bytes 1327112 | tf_op jit(solution)/shard_map/ppermute | solution.py:41
  222.3 24.9 %collective-permute-start.55 = (bf16[96,2304]{1,0:T(8,128)(2,1)S(1)}, bf16[96,2304]{1,0:T(8,128)(2,1)S(1)}, u32[]{:S(2)}, u32[]{:S(2)}) collective-permute-start(bf16[96,2304]{1,0:T(8,128)(2,1)S(1)} %add_convert_fusion.14), channel_id=1, source_target_pairs={{0,2},{1,5},{2,0},{3,7},{4,6},{5,1},{6,4},{7,3},{8,10},{9,13},{10,... | collective-permute-start | bytes 1327112 | tf_op jit(solution)/shard_map/ppermute | solution.py:41
  224.4 21.3 %collective-permute-start.57 = (f32[16,768]{1,0:T(8,128)S(1)}, f32[16,768]{1,0:T(8,128)S(1)}, u32[]{:S(2)}, u32[]{:S(2)}) collective-permute-start(f32[16,768]{1,0:T(8,128)S(1)} %add.135.refs_1_), channel_id=1, source_target_pairs={{0,2},{1,3},{2,0},{3,1},{4,6},{5,7},{6,4},{7,5},{8,10},{9,11},{10,... | collective-permute-start | bytes 147464 | tf_op jit(solution)/shard_map/ppermute | solution.py:41
  224.5 21.2 %collective-permute-start.58 = (f32[16,768]{1,0:T(8,128)S(1)}, f32[16,768]{1,0:T(8,128)S(1)}, u32[]{:S(2)}, u32[]{:S(2)}) collective-permute-start(f32[16,768]{1,0:T(8,128)S(1)} %add.135.refs_1_), channel_id=1, source_target_pairs={{0,4},{1,5},{2,6},{3,7},{4,0},{5,1},{6,2},{7,3},{8,12},{9,13},{10,... | collective-permute-start | bytes 147464 | tf_op jit(solution)/shard_map/ppermute | solution.py:41
  226.3 20.9 %collective-permute-start.59 = (f32[16,768]{1,0:T(8,128)S(1)}, f32[16,768]{1,0:T(8,128)S(1)}, u32[]{:S(2)}, u32[]{:S(2)}) collective-permute-start(f32[16,768]{1,0:T(8,128)S(1)} %add.135.refs_1_), channel_id=1, source_target_pairs={{0,6},{1,7},{2,4},{3,5},{4,2},{5,3},{6,0},{7,1},{8,14},{9,15},{10,... | collective-permute-start | bytes 147464 | tf_op jit(solution)/shard_map/ppermute | solution.py:41
  249.0 13.5 %collective-permute-start.61 = (bf16[96,2304]{1,0:T(8,128)(2,1)S(1)}, bf16[96,2304]{1,0:T(8,128)(2,1)S(1)}, u32[]{:S(2)}, u32[]{:S(2)}) collective-permute-start(bf16[96,2304]{1,0:T(8,128)(2,1)S(1)} %add_convert_fusion.13), channel_id=1, source_target_pairs={{0,4},{1,3},{2,6},{3,1},{4,0},{5,7},{6,2},{7,5},{8,12},{9,11},{10,... | collective-permute-start | bytes 1327112 | tf_op jit(solution)/shard_map/ppermute | solution.py:41
  (40 other events, 197.6 us)

commit v4 on v3

--- a/solution.py
+++ b/solution.py
@@ -317,13 +317,9 @@
         vector_copies.append(copy)
     wait_all(vector_copies)
     shard = width // 4
+    vec[...] = jnp.concatenate([wide(vectors[f, :, :shard]) for f in range(4)], axis=1)
     for f in range(4):
-        row = lax.broadcasted_iota(jnp.int32, (shard, width), 0)
-        col = lax.broadcasted_iota(jnp.int32, (shard, width), 1)
-        shift = jnp.where(col == row + f * shard, 1.0, 0.0).astype(BF16)
-        placed = dot(vectors[f, :, :shard], shift)
-        vec[...] = placed if f == 0 else vec[...] + placed
-        up_shift[:, f * width : (f + 1) * width] = vectors[f, UP_ROW : UP_ROW + 1, :].astype(F32)
+        up_shift[:, f * width : (f + 1) * width] = wide(vectors[f])[UP_ROW : UP_ROW + 1, :]
     for i, part in enumerate(x_parts):
         here = slice(i * capacity, (i + 1) * capacity)
         x_rows[here, :] = part[...]
@@ -777,7 +773,8 @@
     slots, images = image_tokens.shape[2:]
     assert chips == micro_count * slots and lax.axis_size("fsdp") == 4
     assert slots * images < PAD_SEGMENT
-    capacity = ceil_to((LONG - 2) // seq_count + 2, 16)
+    most_rows = (LONG - 2) // seq_count + 2
+    capacity, crossing = ceil_to(most_rows, 16), ceil_to(most_rows, 8)
     rows = chips * capacity
     tile = rows // 2
     hidden_width = up_weight.shape[1]
@@ -815,12 +812,14 @@
 
     def cross(parts, bit):
         labels = [label for label in range(chips) if label & bit]
-        return to_chip(jnp.concatenate([parts[label] for label in labels]), *flips_of(bit, chips))
+        sent = jnp.concatenate([parts[label][:crossing] for label in labels])
+        return to_chip(sent, *flips_of(bit, chips))
 
     def crossed(parts, moved, bit):
         parts = list(parts)
         for i, label in enumerate(label for label in range(chips) if label & bit):
-            parts[label] = moved[i * capacity : (i + 1) * capacity]
+            piece = moved[i * crossing : (i + 1) * crossing]
+            parts[label] = jnp.pad(piece, ((0, capacity - crossing), (0, 0)))
         return parts
 
     def cross_rest(parts):
@@ -1023,7 +1022,7 @@
     waits = up.send_near() + down.send_chips_again() + fresh
     backward(2)
     backward(3)
-    (up.near, down.got, *core_grads), fresh = hold_grads(waits)
+    (up.near, *core_grads), fresh = hold_grads(waits[:1] + waits[2:])
     waits = up.send_chips() + down.send_total() + fresh
     backward(4)
     backward(5)

time: 270 us -> 268 us (level)
    unnamed x44 -> x46, local copies, waits for them, and re-layouts: 6.63 us -> 6.45 us
where the time goes in v4:
time: 268 us; the launch traced here: 265 us
  Pallas kernels  108 us (40%)
  waiting for transfers between devices  86.3 us (32%)
  starting transfers between devices  57.2 us (21%)
  local copies, waits for them, and re-layouts  8.11 us (3%)
  other arithmetic  3.87 us (1%)
    ppermute x66, waiting for transfers between devices, move(): return lax.ppermute(value, BOTH, pairs)  86.3 us
    pallas_call x40, Pallas kernels, call(): pl.pallas_call(run, in_specs=[spec for _, spec in operands] + [ANY] * len...  64.3 us
    ppermute x66, starting transfers between devices, move(): return lax.ppermute(value, BOTH, pairs)  57.2 us
    pallas_call x6, Pallas kernels, attend_backward(): pl.pallas_call(ignoring(partial(attend_backward_kernel, row_tiles(rows),...  26.7 us
    pallas_call x2, Pallas kernels, attend_forward(): pl.pallas_call(ignoring(partial(attend_forward_kernel, row_tiles(rows)),...  16.8 us
    unnamed x46, local copies, waits for them, and re-layouts  6.45 us
  transfers between devices with their start and end apart: 66, of which 25 were waited for; matrix products, arithmetic and copies ran while one was open for 2% of the time, Pallas kernels for 39%

profile of v4, /device:TPU:0, one launch (start us, length us, event | category | flops | bytes accessed | tf_op | source)
XLA Modules:
  0.0 265.0 jit_solution(133323931414993452)
XLA Ops:
  0.7 2.5 shard_map.305
  3.2 3.0 %collective-permute-start.3 = (bf16[208,2304]{1,0:T(8,128)(2,1)}, bf16[208,2304]{1,0:T(8,128)(2,1)S(1)}, u32[]{:S(2)}, u32[]{:S(2)}) collective-permute-start(bf16[208,2304]{1,0:T(8,128)(2,1)} %get-tuple-element.204.refs_2_.refs_3_.refs_1_.refs_4_), channel_id=1, source_target_pairs={{0,8},{1,17},{2,10},{3,19},{4,12},{5,21},{6,14},{7,23},{8,0},{9,25... | collective-permute-start | bytes 2875400 | tf_op jit(solution)/shard_map/ppermute | solution.py:41
  7.6 2.3 shard_map.306
  10.0 2.7 %collective-permute-start = (bf16[144,768]{1,0:T(8,128)(2,1)}, bf16[144,768]{1,0:T(8,128)(2,1)S(1)}, u32[]{:S(2)}, u32[]{:S(2)}) collective-permute-start(bf16[144,768]{1,0:T(8,128)(2,1)} %get-tuple-element.206), channel_id=1, source_target_pairs={{0,4},{1,3},{2,6},{3,1},{4,0},{5,7},{6,2},{7,5},{8,12},{9,11},{10,... | collective-permute-start | bytes 663560 | tf_op jit(solution)/shard_map/ppermute | solution.py:41
  16.9 11.9 %collective-permute-done.refs_4_.refs_1_ = bf16[144,768]{1,0:T(8,128)(2,1)S(1)} collective-permute-done((bf16[144,768]{1,0:T(8,128)(2,1)}, bf16[144,768]{1,0:T(8,128)(2,1)S(1)}, u32[]{:S(2)}, u32[]{:S(2)}) %collective-permute-start) | collective-permute-done | bytes 221216 | tf_op jit(solution)/shard_map/ppermute | solution.py:41
  28.9 1.8 collective-permute-done.4.refs_1_
  32.4 1.9 collective-permute-done.6.refs_9_.refs_13_
  34.3 5.1 %shard_map.311 = (bf16[576,768]{1,0:T(8,128)(2,1)S(1)}, bf16[576,768]{1,0:T(8,128)(2,1)S(1)}, bf16[576,768]{1,0:T(8,128)(2,1)S(1)}, bf16[576,768]{1,0:T(8,128)(2...) custom-call(bf16[144,768]{1,0:T(8,128)(2,1)S(1)} %copy-done.19, ...), custom_call_target="tpu_custom_call" | custom-call | tf_op jit(solution)/shard_map/pallas_call | solution.py:82
  41.8 3.5 %collective-permute-start.10 = (bf16[272,768]{1,0:T(8,128)(2,1)S(1)}, bf16[272,768]{1,0:T(8,128)(2,1)S(1)}, u32[]{:S(2)}, u32[]{:S(2)}) collective-permute-start(bf16[272,768]{1,0:T(8,128)(2,1)S(1)} %pad_maximum_fusion), channel_id=1, source_target_pairs={{0,4},{1,3},{2,6},{3,1},{4,0},{5,7},{6,2},{7,5},{8,12},{9,11},{10,... | collective-permute-start | bytes 1253384 | tf_op jit(solution)/shard_map/ppermute | solution.py:41
  45.3 5.6 %shard_map.312 = (bf16[576,256]{1,0:T(8,128)(2,1)S(1)}, f32[576,128]{1,0:T(8,128)S(1)}) custom-call(bf16[576,768]{1,0:T(8,128)(2,1)S(1)} %get-tuple-element.216.refs_0_.refs_5_, bf16[576,768]{1,0:T(8,128)(2,1)S(1)} %get-tuple-element.217.refs_1_, bf16[576,768]{1,0:T(8,128)(2,1)S(1)} %get-tuple-element.218.refs_2_, ...), custom_call_target="tpu_custom_call" | custom-call | tf_op jit(solution)/shard_map/pallas_call | solution.py:388
  50.9 3.6 %collective-permute-done.10.refs_1_ = bf16[272,768]{1,0:T(8,128)(2,1)S(1)} collective-permute-done((bf16[272,768]{1,0:T(8,128)(2,1)S(1)}, bf16[272,768]{1,0:T(8,128)(2,1)S(1)}, u32[]{:S(2)}, u32[]{:S(2)}) %collective-permute-start.10) | collective-permute-done | bytes 417824 | tf_op jit(solution)/shard_map/ppermute | solution.py:41
  54.5 1.8 collective-permute-start.12
  56.4 2.0 collective-permute-start.14
  58.4 11.2 %shard_map.313 = (bf16[576,512]{1,0:T(8,128)(2,1)S(1)}, f32[576,128]{1,0:T(8,128)S(1)}) custom-call(bf16[576,768]{1,0:T(8,128)(2,1)S(1)} %get-tuple-element.216.refs_0_.refs_5_, bf16[576,768]{1,0:T(8,128)(2,1)S(1)} %get-tuple-element.217.refs_1_, bf16[576,768]{1,0:T(8,128)(2,1)S(1)} %get-tuple-element.218.refs_2_, ...), custom_call_target="tpu_custom_call" | custom-call | tf_op jit(solution)/shard_map/pallas_call | solution.py:388
  70.7 1.8 collective-permute-done.15.refs_3_
  73.4 8.7 %shard_map.318 = (bf16[576,768]{1,0:T(8,128)(2,1)S(1)}, f32[576,768]{1,0:T(8,128)S(1)}, f32[576,768]{1,0:T(8,128)S(1)}, bf16[576,768]{1,0:T(8,128)(2,1)S(1)}, bf...) custom-call(bf16[576,256]{1,0:T(8,128)(2,1)S(1)} %get-tuple-element.221.refs_8_.refs_2_.refs_0_, ...), custom_call_target="tpu_custom_call" | custom-call | tf_op jit(solution)/shard_map/pallas_call | solution.py:82
  83.5 4.0 %shard_map.321 = (bf16[576,768]{1,0:T(8,128)(2,1)S(1)}, bf16[576,768]{1,0:T(8,128)(2,1)S(1)}, f32[1,768]{1,0:T(1,128)S(1)}, bf16[384,768]{1,0:T(8,128)(2,1)S(1)}...) custom-call(bf16[576,3072]{1,0:T(8,128)(2,1)S(1)} %get-tuple-element, ...), custom_call_target="tpu_custom_call" | custom-call | tf_op jit(solution)/shard_map/pallas_call | solution.py:82
  90.9 8.2 %shard_map.323 = (bf16[144,768]{1,0:T(8,128)(2,1)S(1)}, bf16[144,768]{1,0:T(8,128)(2,1)S(1)}, bf16[144,768]{1,0:T(8,128)(2,1)S(1)}, bf16[144,768]{1,0:T(8,128)(2...) custom-call(bf16[576,3072]{1,0:T(8,128)(2,1)S(1)} %get-tuple-element.241.refs_0_, ...), custom_call_target="tpu_custom_call" | custom-call | tf_op jit(solution)/shard_map/pallas_call | solution.py:82
  102.9 4.3 %collective-permute-start.26 = (bf16[272,768]{1,0:T(8,128)(2,1)S(1)}, bf16[272,768]{1,0:T(8,128)(2,1)S(1)}, u32[]{:S(2)}, u32[]{:S(2)}) collective-permute-start(bf16[272,768]{1,0:T(8,128)(2,1)S(1)} %pad_maximum_fusion.2), channel_id=1, source_target_pairs={{0,4},{1,3},{2,6},{3,1},{4,0},{5,7},{6,2},{7,5},{8,12},{9,11},{10,... | collective-permute-start | bytes 1253384 | tf_op jit(solution)/shard_map/ppermute | solution.py:41
  107.2 6.1 %shard_map.326 = (f32[576,768]{1,0:T(8,128)S(1)}, bf16[576,768]{1,0:T(8,128)(2,1)S(1)}, bf16[576,768]{1,0:T(8,128)(2,1)S(1)}, f32[4,768]{1,0:T(4,128)S(1)}) custom-call(bf16[576,3072]{1,0:T(8,128)(2,1)S(1)} %get-tuple-element.267.refs_4_.refs_0_, f32[576,768]{1,0:T(8,128)S(1)} %get-tuple-element.243.refs_2_.refs_1_, ...), custom_call_target="tpu_custom_call" | custom-call | tf_op jit(solution)/shard_map/pallas_call | solution.py:82
  113.3 5.3 %shard_map.327 = (bf16[96,3840]{1,0:T(8,128)(2,1)S(1)}, bf16[96,3840]{1,0:T(8,128)(2,1)S(1)}, bf16[96,3840]{1,0:T(8,128)(2,1)S(1)}, bf16[96,3840]{1,0:T(8,128)(2...) custom-call(bf16[576,3072]{1,0:T(8,128)(2,1)S(1)} %get-tuple-element, ...), custom_call_target="tpu_custom_call" | custom-call | tf_op jit(solution)/shard_map/pallas_call | solution.py:82
  125.5 4.6 %shard_map.329 = (bf16[576,128]{1,0:T(8,128)(2,1)S(1)}, bf16[2,576,128]{2,1,0:T(8,128)(2,1)S(1)}, bf16[2,576,128]{2,1,0:T(8,128)(2,1)S(1)}) custom-call(bf16[576,768]{1,0:T(8,128)(2,1)S(1)} %get-tuple-element.216.refs_0_.refs_5_, bf16[576,768]{1,0:T(8,128)(2,1)S(1)} %get-tuple-element.217.refs_1_, bf16[576,768]{1,0:T(8,128)(2,1)S(1)} %get-tuple-element.218.refs_2_, ...), custom_call_target="tpu_custom_call" | custom-call | tf_op jit(solution)/shard_map/pallas_call | solution.py:597
  130.1 4.3 %shard_map.330 = (bf16[576,128]{1,0:T(8,128)(2,1)S(1)}, bf16[2,576,128]{2,1,0:T(8,128)(2,1)S(1)}, bf16[2,576,128]{2,1,0:T(8,128)(2,1)S(1)}) custom-call(bf16[576,768]{1,0:T(8,128)(2,1)S(1)} %get-tuple-element.216.refs_0_.refs_5_, bf16[576,768]{1,0:T(8,128)(2,1)S(1)} %get-tuple-element.217.refs_1_, bf16[576,768]{1,0:T(8,128)(2,1)S(1)} %get-tuple-element.218.refs_2_, ...), custom_call_target="tpu_custom_call" | custom-call | tf_op jit(solution)/shard_map/pallas_call | solution.py:597
  134.4 6.7 %collective-permute-done.27.refs_0_ = bf16[384,768]{1,0:T(8,128)(2,1)S(1)} collective-permute-done((bf16[384,768]{1,0:T(8,128)(2,1)S(1)}, bf16[384,768]{1,0:T(8,128)(2,1)S(1)}, u32[]{:S(2)}, u32[]{:S(2)}) %collective-permute-start.27) | collective-permute-done | bytes 589856 | tf_op jit(solution)/shard_map/ppermute | solution.py:41
  141.8 1.8 collective-permute-start.37
  145.6 4.3 %shard_map.331 = (bf16[576,128]{1,0:T(8,128)(2,1)S(1)}, bf16[2,576,128]{2,1,0:T(8,128)(2,1)S(1)}, bf16[2,576,128]{2,1,0:T(8,128)(2,1)S(1)}) custom-call(bf16[576,768]{1,0:T(8,128)(2,1)S(1)} %get-tuple-element.216.refs_0_.refs_5_, bf16[576,768]{1,0:T(8,128)(2,1)S(1)} %get-tuple-element.217.refs_1_, bf16[576,768]{1,0:T(8,128)(2,1)S(1)} %get-tuple-element.218.refs_2_, ...), custom_call_target="tpu_custom_call" | custom-call | tf_op jit(solution)/shard_map/pallas_call | solution.py:597
  149.9 4.8 %shard_map.332 = (bf16[576,128]{1,0:T(8,128)(2,1)S(1)}, bf16[2,576,128]{2,1,0:T(8,128)(2,1)S(1)}, bf16[2,576,128]{2,1,0:T(8,128)(2,1)S(1)}) custom-call(bf16[576,768]{1,0:T(8,128)(2,1)S(1)} %get-tuple-element.216.refs_0_.refs_5_, bf16[576,768]{1,0:T(8,128)(2,1)S(1)} %get-tuple-element.217.refs_1_, bf16[576,768]{1,0:T(8,128)(2,1)S(1)} %get-tuple-element.218.refs_2_, ...), custom_call_target="tpu_custom_call" | custom-call | tf_op jit(solution)/shard_map/pallas_call | solution.py:597
  154.7 4.2 %collective-permute-done.37 = bf16[384,768]{1,0:T(8,128)(2,1)S(1)} collective-permute-done((bf16[384,768]{1,0:T(8,128)(2,1)S(1)}, bf16[384,768]{1,0:T(8,128)(2,1)S(1)}, u32[]{:S(2)}, u32[]{:S(2)}) %collective-permute-start.37) | collective-permute-done | bytes 589856 | tf_op jit(solution)/shard_map/ppermute | solution.py:41
  160.3 4.3 %shard_map.333 = (bf16[576,128]{1,0:T(8,128)(2,1)S(1)}, bf16[2,576,128]{2,1,0:T(8,128)(2,1)S(1)}, bf16[2,576,128]{2,1,0:T(8,128)(2,1)S(1)}) custom-call(bf16[576,768]{1,0:T(8,128)(2,1)S(1)} %get-tuple-element.216.refs_0_.refs_5_, bf16[576,768]{1,0:T(8,128)(2,1)S(1)} %get-tuple-element.217.refs_1_, bf16[576,768]{1,0:T(8,128)(2,1)S(1)} %get-tuple-element.218.refs_2_, ...), custom_call_target="tpu_custom_call" | custom-call | tf_op jit(solution)/shard_map/pallas_call | solution.py:597
  164.6 4.3 %shard_map.334 = (bf16[576,128]{1,0:T(8,128)(2,1)S(1)}, bf16[2,576,128]{2,1,0:T(8,128)(2,1)S(1)}, bf16[2,576,128]{2,1,0:T(8,128)(2,1)S(1)}) custom-call(bf16[576,768]{1,0:T(8,128)(2,1)S(1)} %get-tuple-element.216.refs_0_.refs_5_, bf16[576,768]{1,0:T(8,128)(2,1)S(1)} %get-tuple-element.217.refs_1_, bf16[576,768]{1,0:T(8,128)(2,1)S(1)} %get-tuple-element.218.refs_2_, ...), custom_call_target="tpu_custom_call" | custom-call | tf_op jit(solution)/shard_map/pallas_call | solution.py:597
  171.3 1.7 copy-done.2
  173.0 3.6 %shard_map.340 = (bf16[576,2304]{1,0:T(8,128)(2,1)S(1)}, f32[2,768]{1,0:T(2,128)S(1)}, bf16[96,2304]{1,0:T(8,128)(2,1)S(1)}, bf16[96,2304]{1,0:T(8,128)(2,1)S(1)...) custom-call(bf16[576,128]{1,0:T(8,128)(2,1)S(1)} %get-tuple-element., ...), custom_call_target="tpu_custom_call" | custom-call | tf_op jit(solution)/shard_map/pallas_call | solution.py:82
  176.6 1.9 collective-permute-done.43.refs_4_
  183.5 6.9 %shard_map.343 = (bf16[144,768]{1,0:T(8,128)(2,1)S(1)}, bf16[144,768]{1,0:T(8,128)(2,1)S(1)}, bf16[144,768]{1,0:T(8,128)(2,1)S(1)}, bf16[144,768]{1,0:T(8,128)(2,1)S(1)}, f32[16,768]{1,0:T(8,128)S(1)}) custom-call(bf16[576,2304]{1,0:T(8,128)(2,1)S(1)} %get-tuple-element.341.refs_5_.refs_0_, bf16[576,768]{1,0:T(8,128)(2,1)S(1)} %copy-done.6, ...), custom_call_target="tpu_custom_call" | custom-call | tf_op jit(solution)/shard_map/pallas_call | solution.py:82
  191.7 2.4 collective-permute-done.46.refs_0_
  197.0 13.5 %collective-permute-done.52.refs_2_ = bf16[96,3840]{1,0:T(8,128)(2,1)S(1)} collective-permute-done((bf16[96,3840]{1,0:T(8,128)(2,1)S(1)}, bf16[96,3840]{1,0:T(8,128)(2,1)S(1)}, u32[]{:S(2)}, u32[]{:S(2)}) %collective-permute-start.52) | collective-permute-done | bytes 737312 | tf_op jit(solution)/shard_map/ppermute | solution.py:41
  210.5 9.2 %collective-permute-done.51.refs_1_ = bf16[272,768]{1,0:T(8,128)(2,1)S(1)} collective-permute-done((bf16[272,768]{1,0:T(8,128)(2,1)S(1)}, bf16[272,768]{1,0:T(8,128)(2,1)S(1)}, u32[]{:S(2)}, u32[]{:S(2)}) %collective-permute-start.51) | collective-permute-done | bytes 417824 | tf_op jit(solution)/shard_map/ppermute | solution.py:41
  220.3 2.1 collective-permute-start.56
  222.5 2.4 collective-permute-start.58
  224.9 1.9 collective-permute-start.59
  227.0 2.2 shard_map.346.refs_1_
  230.3 1.8 shard_map.348
  232.1 11.6 %collective-permute-done.57.refs_3_ = f32[16,768]{1,0:T(8,128)S(1)} collective-permute-done((f32[16,768]{1,0:T(8,128)S(1)}, f32[16,768]{1,0:T(8,128)S(1)}, u32[]{:S(2)}, u32[]{:S(2)}) %collective-permute-start.57) | collective-permute-done | bytes 49184 | tf_op jit(solution)/shard_map/ppermute | solution.py:41
  245.3 1.7 copy-done.10
  247.3 1.6 collective-permute-start.62
  251.0 2.2 shard_map.350.refs_5_
  253.2 1.8 collective-permute-done.64.refs_4_
  255.0 5.4 %collective-permute-done.61.refs_0_ = bf16[96,2304]{1,0:T(8,128)(2,1)S(1)} collective-permute-done((bf16[96,2304]{1,0:T(8,128)(2,1)S(1)}, bf16[96,2304]{1,0:T(8,128)(2,1)S(1)}, u32[]{:S(2)}, u32[]{:S(2)}) %collective-permute-start.61) | collective-permute-done | bytes 442400 | tf_op jit(solution)/shard_map/ppermute | solution.py:41
  (230 shorter events, 52.8 us)
Async XLA Ops:
  3.2 27.6 %collective-permute-start.3 = (bf16[208,2304]{1,0:T(8,128)(2,1)}, bf16[208,2304]{1,0:T(8,128)(2,1)S(1)}, u32[]{:S(2)}, u32[]{:S(2)}) collective-permute-start(bf16[208,2304]{1,0:T(8,128)(2,1)} %get-tuple-element.204.refs_2_.refs_3_.refs_1_.refs_4_), channel_id=1, source_target_pairs={{0,8},{1,17},{2,10},{3,19},{4,12},{5,21},{6,14},{7,23},{8,0},{9,25... | collective-permute-start | bytes 2875400 | tf_op jit(solution)/shard_map/ppermute | solution.py:41
  6.2 24.6 %collective-permute-start.4 = (bf16[112,2304]{1,0:T(8,128)(2,1)}, bf16[112,2304]{1,0:T(8,128)(2,1)S(1)}, u32[]{:S(2)}, u32[]{:S(2)}) collective-permute-start(bf16[112,2304]{1,0:T(8,128)(2,1)} %get-tuple-element.209), channel_id=1, source_target_pairs={{0,24},{1,25},{2,26},{3,27},{4,28},{5,29},{6,30},{7,31},{8,16},{9,... | collective-permute-start | bytes 1548296 | tf_op jit(solution)/shard_map/ppermute | solution.py:41
  10.0 18.9 %collective-permute-start = (bf16[144,768]{1,0:T(8,128)(2,1)}, bf16[144,768]{1,0:T(8,128)(2,1)S(1)}, u32[]{:S(2)}, u32[]{:S(2)}) collective-permute-start(bf16[144,768]{1,0:T(8,128)(2,1)} %get-tuple-element.206), channel_id=1, source_target_pairs={{0,4},{1,3},{2,6},{3,1},{4,0},{5,7},{6,2},{7,5},{8,12},{9,11},{10,... | collective-permute-start | bytes 663560 | tf_op jit(solution)/shard_map/ppermute | solution.py:41
  12.6 16.3 %collective-permute-start.1 = (bf16[144,768]{1,0:T(8,128)(2,1)}, bf16[144,768]{1,0:T(8,128)(2,1)S(1)}, u32[]{:S(2)}, u32[]{:S(2)}) collective-permute-start(bf16[144,768]{1,0:T(8,128)(2,1)} %get-tuple-element.207), channel_id=1, source_target_pairs={{0,2},{1,5},{2,0},{3,7},{4,6},{5,1},{6,4},{7,3},{8,10},{9,13},{10,... | collective-permute-start | bytes 663560 | tf_op jit(solution)/shard_map/ppermute | solution.py:41
  14.2 14.7 %collective-permute-start.2 = (bf16[144,768]{1,0:T(8,128)(2,1)}, bf16[144,768]{1,0:T(8,128)(2,1)S(1)}, u32[]{:S(2)}, u32[]{:S(2)}) collective-permute-start(bf16[144,768]{1,0:T(8,128)(2,1)} %get-tuple-element.208), channel_id=1, source_target_pairs={{0,6},{1,7},{2,4},{3,5},{4,2},{5,3},{6,0},{7,1},{8,14},{9,15},{10,... | collective-permute-start | bytes 663560 | tf_op jit(solution)/shard_map/ppermute | solution.py:41
  30.8 23.6 %collective-permute-start.9 = (bf16[192,3840]{1,0:T(8,128)(2,1)S(1)}, bf16[192,3840]{1,0:T(8,128)(2,1)S(1)}, u32[]{:S(2)}, u32[]{:S(2)}) collective-permute-start(bf16[192,3840]{1,0:T(8,128)(2,1)S(1)} %get-tuple-element.226), channel_id=1, source_target_pairs={{0,8},{1,17},{2,10},{3,19},{4,12},{5,21},{6,14},{7,23},{8,0},{9,25... | collective-permute-start | bytes 4423688 | tf_op jit(solution)/shard_map/ppermute | solution.py:41
  40.4 29.3 %collective-permute-start.13 = (bf16[768,768]{1,0:T(8,128)(2,1)S(1)}, bf16[768,768]{1,0:T(8,128)(2,1)S(1)}, u32[]{:S(2)}, u32[]{:S(2)}) collective-permute-start(bf16[768,768]{1,0:T(8,128)(2,1)S(1)} %get-tuple-element.233), channel_id=1, source_target_pairs={{0,8},{1,17},{2,10},{3,19},{4,12},{5,21},{6,14},{7,23},{8,0},{9,25... | collective-permute-start | bytes 3538952 | tf_op jit(solution)/shard_map/ppermute | solution.py:41
  41.8 12.7 %collective-permute-start.10 = (bf16[272,768]{1,0:T(8,128)(2,1)S(1)}, bf16[272,768]{1,0:T(8,128)(2,1)S(1)}, u32[]{:S(2)}, u32[]{:S(2)}) collective-permute-start(bf16[272,768]{1,0:T(8,128)(2,1)S(1)} %pad_maximum_fusion), channel_id=1, source_target_pairs={{0,4},{1,3},{2,6},{3,1},{4,0},{5,7},{6,2},{7,5},{8,12},{9,11},{10,... | collective-permute-start | bytes 1253384 | tf_op jit(solution)/shard_map/ppermute | solution.py:41
  54.5 15.7 %collective-permute-start.12 = (bf16[96,3840]{1,0:T(8,128)(2,1)S(1)}, bf16[96,3840]{1,0:T(8,128)(2,1)S(1)}, u32[]{:S(2)}, u32[]{:S(2)}) collective-permute-start(bf16[96,3840]{1,0:T(8,128)(2,1)S(1)} %slice.113), channel_id=1, source_target_pairs={{0,16},{1,9},{2,18},{3,11},{4,20},{5,13},{6,22},{7,15},{8,24},{9,1... | collective-permute-start | bytes 2211848 | tf_op jit(solution)/shard_map/ppermute | solution.py:41
  56.3 16.2 %collective-permute-start.11 = (bf16[192,3840]{1,0:T(8,128)(2,1)S(1)}, bf16[192,3840]{1,0:T(8,128)(2,1)S(1)}, u32[]{:S(2)}, u32[]{:S(2)}) collective-permute-start(bf16[192,3840]{1,0:T(8,128)(2,1)S(1)} %get-tuple-element.232.refs_0_), channel_id=1, source_target_pairs={{0,1},{1,0},{2,3},{3,2},{4,5},{5,4},{6,7},{7,6},{8,9},{9,8},{10,11... | collective-permute-start | bytes 4423688 | tf_op jit(solution)/shard_map/ppermute | solution.py:41
  56.4 13.3 %collective-permute-start.14 = (bf16[272,768]{1,0:T(8,128)(2,1)S(1)}, bf16[272,768]{1,0:T(8,128)(2,1)S(1)}, u32[]{:S(2)}, u32[]{:S(2)}) collective-permute-start(bf16[272,768]{1,0:T(8,128)(2,1)S(1)} %pad_maximum_fusion.1), channel_id=1, source_target_pairs={{0,2},{1,5},{2,0},{3,7},{4,6},{5,1},{6,4},{7,3},{8,10},{9,13},{10,... | collective-permute-start | bytes 1253384 | tf_op jit(solution)/shard_map/ppermute | solution.py:41
  72.5 10.2 %collective-permute-start.17 = (bf16[768,768]{1,0:T(8,128)(2,1)S(1)}, bf16[768,768]{1,0:T(8,128)(2,1)S(1)}, u32[]{:S(2)}, u32[]{:S(2)}) collective-permute-start(bf16[768,768]{1,0:T(8,128)(2,1)S(1)} %shard_map.319.refs_4_), channel_id=1, source_target_pairs={{0,1},{1,0},{2,3},{3,2},{4,5},{5,4},{6,7},{7,6},{8,9},{9,8},{10,11... | collective-permute-start | bytes 3538952 | tf_op jit(solution)/shard_map/ppermute | solution.py:41
  72.8 9.9 %collective-permute-start.16 = (bf16[384,768]{1,0:T(8,128)(2,1)S(1)}, bf16[384,768]{1,0:T(8,128)(2,1)S(1)}, u32[]{:S(2)}, u32[]{:S(2)}) collective-permute-start(bf16[384,768]{1,0:T(8,128)(2,1)S(1)} %slice.119), channel_id=1, source_target_pairs={{0,16},{1,9},{2,18},{3,11},{4,20},{5,13},{6,22},{7,15},{8,24},{9,1... | collective-permute-start | bytes 1769480 | tf_op jit(solution)/shard_map/ppermute | solution.py:41
  88.0 11.1 %collective-permute-start.21 = (bf16[384,768]{1,0:T(8,128)(2,1)S(1)}, bf16[384,768]{1,0:T(8,128)(2,1)S(1)}, u32[]{:S(2)}, u32[]{:S(2)}) collective-permute-start(bf16[384,768]{1,0:T(8,128)(2,1)S(1)} %get-tuple-element.264), channel_id=1, source_target_pairs={{0,1},{1,0},{2,3},{3,2},{4,5},{5,4},{6,7},{7,6},{8,9},{9,8},{10,11... | collective-permute-start | bytes 1769480 | tf_op jit(solution)/shard_map/ppermute | solution.py:41
  88.1 11.0 %collective-permute-start.22 = (bf16[384,768]{1,0:T(8,128)(2,1)S(1)}, bf16[384,768]{1,0:T(8,128)(2,1)S(1)}, u32[]{:S(2)}, u32[]{:S(2)}) collective-permute-start(bf16[384,768]{1,0:T(8,128)(2,1)S(1)} %get-tuple-element.265), channel_id=1, source_target_pairs={{0,1},{1,0},{2,3},{3,2},{4,5},{5,4},{6,7},{7,6},{8,9},{9,8},{10,11... | collective-permute-start | bytes 1769480 | tf_op jit(solution)/shard_map/ppermute | solution.py:41
  88.6 10.6 %collective-permute-start.23 = (bf16[384,768]{1,0:T(8,128)(2,1)S(1)}, bf16[384,768]{1,0:T(8,128)(2,1)S(1)}, u32[]{:S(2)}, u32[]{:S(2)}) collective-permute-start(bf16[384,768]{1,0:T(8,128)(2,1)S(1)} %get-tuple-element.266), channel_id=1, source_target_pairs={{0,1},{1,0},{2,3},{3,2},{4,5},{5,4},{6,7},{7,6},{8,9},{9,8},{10,11... | collective-permute-start | bytes 1769480 | tf_op jit(solution)/shard_map/ppermute | solution.py:41
  89.8 9.9 %collective-permute-start.20 = (bf16[384,768]{1,0:T(8,128)(2,1)S(1)}, bf16[384,768]{1,0:T(8,128)(2,1)S(1)}, u32[]{:S(2)}, u32[]{:S(2)}) collective-permute-start(bf16[384,768]{1,0:T(8,128)(2,1)S(1)} %add_convert_fusion.11), channel_id=1, source_target_pairs={{0,16},{1,9},{2,18},{3,11},{4,20},{5,13},{6,22},{7,15},{8,24},{9,1... | collective-permute-start | bytes 1769480 | tf_op jit(solution)/shard_map/ppermute | solution.py:41
  100.0 18.7 %collective-permute-start.25 = (bf16[384,768]{1,0:T(8,128)(2,1)S(1)}, bf16[384,768]{1,0:T(8,128)(2,1)S(1)}, u32[]{:S(2)}, u32[]{:S(2)}) collective-permute-start(bf16[384,768]{1,0:T(8,128)(2,1)S(1)} %add_convert_fusion.9), channel_id=1, source_target_pairs={{0,16},{1,9},{2,18},{3,11},{4,20},{5,13},{6,22},{7,15},{8,24},{9,1... | collective-permute-start | bytes 1769480 | tf_op jit(solution)/shard_map/ppermute | solution.py:41
  101.3 17.4 %collective-permute-start.24 = (bf16[384,768]{1,0:T(8,128)(2,1)S(1)}, bf16[384,768]{1,0:T(8,128)(2,1)S(1)}, u32[]{:S(2)}, u32[]{:S(2)}) collective-permute-start(bf16[384,768]{1,0:T(8,128)(2,1)S(1)} %add_convert_fusion.10), channel_id=1, source_target_pairs={{0,8},{1,17},{2,10},{3,19},{4,12},{5,21},{6,14},{7,23},{8,0},{9,25... | collective-permute-start | bytes 1769480 | tf_op jit(solution)/shard_map/ppermute | solution.py:41
  102.9 15.7 %collective-permute-start.26 = (bf16[272,768]{1,0:T(8,128)(2,1)S(1)}, bf16[272,768]{1,0:T(8,128)(2,1)S(1)}, u32[]{:S(2)}, u32[]{:S(2)}) collective-permute-start(bf16[272,768]{1,0:T(8,128)(2,1)S(1)} %pad_maximum_fusion.2), channel_id=1, source_target_pairs={{0,4},{1,3},{2,6},{3,1},{4,0},{5,7},{6,2},{7,5},{8,12},{9,11},{10,... | collective-permute-start | bytes 1253384 | tf_op jit(solution)/shard_map/ppermute | solution.py:41
  119.3 21.8 %collective-permute-start.32 = (bf16[96,3840]{1,0:T(8,128)(2,1)S(1)}, bf16[96,3840]{1,0:T(8,128)(2,1)S(1)}, u32[]{:S(2)}, u32[]{:S(2)}) collective-permute-start(bf16[96,3840]{1,0:T(8,128)(2,1)S(1)} %get-tuple-element.308), channel_id=1, source_target_pairs={{0,1},{1,0},{2,3},{3,2},{4,5},{5,4},{6,7},{7,6},{8,9},{9,8},{10,11... | collective-permute-start | bytes 2211848 | tf_op jit(solution)/shard_map/ppermute | solution.py:41
  119.4 21.8 %collective-permute-start.33 = (bf16[96,3840]{1,0:T(8,128)(2,1)S(1)}, bf16[96,3840]{1,0:T(8,128)(2,1)S(1)}, u32[]{:S(2)}, u32[]{:S(2)}) collective-permute-start(bf16[96,3840]{1,0:T(8,128)(2,1)S(1)} %get-tuple-element.309), channel_id=1, source_target_pairs={{0,1},{1,0},{2,3},{3,2},{4,5},{5,4},{6,7},{7,6},{8,9},{9,8},{10,11... | collective-permute-start | bytes 2211848 | tf_op jit(solution)/shard_map/ppermute | solution.py:41
  122.2 18.9 %collective-permute-start.31 = (bf16[96,3840]{1,0:T(8,128)(2,1)S(1)}, bf16[96,3840]{1,0:T(8,128)(2,1)S(1)}, u32[]{:S(2)}, u32[]{:S(2)}) collective-permute-start(bf16[96,3840]{1,0:T(8,128)(2,1)S(1)} %add_convert_fusion.4), channel_id=1, source_target_pairs={{0,16},{1,9},{2,18},{3,11},{4,20},{5,13},{6,22},{7,15},{8,24},{9,1... | collective-permute-start | bytes 2211848 | tf_op jit(solution)/shard_map/ppermute | solution.py:41
  123.3 18.4 %collective-permute-start.30 = (bf16[96,3840]{1,0:T(8,128)(2,1)S(1)}, bf16[96,3840]{1,0:T(8,128)(2,1)S(1)}, u32[]{:S(2)}, u32[]{:S(2)}) collective-permute-start(bf16[96,3840]{1,0:T(8,128)(2,1)S(1)} %add_convert_fusion.5), channel_id=1, source_target_pairs={{0,16},{1,9},{2,18},{3,11},{4,20},{5,13},{6,22},{7,15},{8,24},{9,1... | collective-permute-start | bytes 2211848 | tf_op jit(solution)/shard_map/ppermute | solution.py:41
  124.9 16.2 %collective-permute-start.27 = (bf16[384,768]{1,0:T(8,128)(2,1)S(1)}, bf16[384,768]{1,0:T(8,128)(2,1)S(1)}, u32[]{:S(2)}, u32[]{:S(2)}) collective-permute-start(bf16[384,768]{1,0:T(8,128)(2,1)S(1)} %add_convert_fusion.8), channel_id=1, source_target_pairs={{0,2},{1,5},{2,0},{3,7},{4,6},{5,1},{6,4},{7,3},{8,10},{9,13},{10,... | collective-permute-start | bytes 1769480 | tf_op jit(solution)/shard_map/ppermute | solution.py:41
  141.8 17.1 %collective-permute-start.37 = (bf16[384,768]{1,0:T(8,128)(2,1)S(1)}, bf16[384,768]{1,0:T(8,128)(2,1)S(1)}, u32[]{:S(2)}, u32[]{:S(2)}) collective-permute-start(bf16[384,768]{1,0:T(8,128)(2,1)S(1)} %add_convert_fusion.7), channel_id=1, source_target_pairs={{0,4},{1,3},{2,6},{3,1},{4,0},{5,7},{6,2},{7,5},{8,12},{9,11},{10,... | collective-permute-start | bytes 1769480 | tf_op jit(solution)/shard_map/ppermute | solution.py:41
  143.9 15.2 %collective-permute-start.34 = (bf16[96,3840]{1,0:T(8,128)(2,1)S(1)}, bf16[96,3840]{1,0:T(8,128)(2,1)S(1)}, u32[]{:S(2)}, u32[]{:S(2)}) collective-permute-start(bf16[96,3840]{1,0:T(8,128)(2,1)S(1)} %add_convert_fusion.3), channel_id=1, source_target_pairs={{0,8},{1,17},{2,10},{3,19},{4,12},{5,21},{6,14},{7,23},{8,0},{9,25... | collective-permute-start | bytes 2211848 | tf_op jit(solution)/shard_map/ppermute | solution.py:41
  145.1 14.1 %collective-permute-start.35 = (bf16[2,576,128]{2,1,0:T(8,128)(2,1)S(1)}, bf16[2,576,128]{2,1,0:T(8,128)(2,1)S(1)}, u32[]{:S(2)}, u32[]{:S(2)}) collective-permute-start(bf16[2,576,128]{2,1,0:T(8,128)(2,1)S(1)} %get-tuple-element.314), channel_id=1, source_target_pairs={{0,1},{1,0},{2,3},{3,2},{4,5},{5,4},{6,7},{7,6},{8,9},{9,8},{10,11... | collective-permute-start | bytes 884744 | tf_op jit(solution)/shard_map/ppermute | solution.py:41
  145.1 14.1 %collective-permute-start.36 = (bf16[2,576,128]{2,1,0:T(8,128)(2,1)S(1)}, bf16[2,576,128]{2,1,0:T(8,128)(2,1)S(1)}, u32[]{:S(2)}, u32[]{:S(2)}) collective-permute-start(bf16[2,576,128]{2,1,0:T(8,128)(2,1)S(1)} %get-tuple-element.315), channel_id=1, source_target_pairs={{0,1},{1,0},{2,3},{3,2},{4,5},{5,4},{6,7},{7,6},{8,9},{9,8},{10,11... | collective-permute-start | bytes 884744 | tf_op jit(solution)/shard_map/ppermute | solution.py:41
  159.0 9.9 %collective-permute-start.38 = (bf16[384,768]{1,0:T(8,128)(2,1)S(1)}, bf16[384,768]{1,0:T(8,128)(2,1)S(1)}, u32[]{:S(2)}, u32[]{:S(2)}) collective-permute-start(bf16[384,768]{1,0:T(8,128)(2,1)S(1)} %add_convert_fusion.6.refs_0_), channel_id=1, source_target_pairs={{0,1},{1,0},{2,3},{3,2},{4,5},{5,4},{6,7},{7,6},{8,9},{9,8},{10,11... | collective-permute-start | bytes 1769480 | tf_op jit(solution)/shard_map/ppermute | solution.py:41
  159.6 18.9 %collective-permute-start.43 = (bf16[96,3840]{1,0:T(8,128)(2,1)S(1)}, bf16[96,3840]{1,0:T(8,128)(2,1)S(1)}, u32[]{:S(2)}, u32[]{:S(2)}) collective-permute-start(bf16[96,3840]{1,0:T(8,128)(2,1)S(1)} %add_convert_fusion.2), channel_id=1, source_target_pairs={{0,2},{1,5},{2,0},{3,7},{4,6},{5,1},{6,4},{7,3},{8,10},{9,13},{10,... | collective-permute-start | bytes 2211848 | tf_op jit(solution)/shard_map/ppermute | solution.py:41
  159.6 9.3 %collective-permute-start.39 = (bf16[2,576,128]{2,1,0:T(8,128)(2,1)S(1)}, bf16[2,576,128]{2,1,0:T(8,128)(2,1)S(1)}, u32[]{:S(2)}, u32[]{:S(2)}) collective-permute-start(bf16[2,576,128]{2,1,0:T(8,128)(2,1)S(1)} %get-tuple-element.321), channel_id=1, source_target_pairs={{0,1},{1,0},{2,3},{3,2},{4,5},{5,4},{6,7},{7,6},{8,9},{9,8},{10,11... | collective-permute-start | bytes 884744 | tf_op jit(solution)/shard_map/ppermute | solution.py:41
  160.2 8.8 %collective-permute-start.40 = (bf16[2,576,128]{2,1,0:T(8,128)(2,1)S(1)}, bf16[2,576,128]{2,1,0:T(8,128)(2,1)S(1)}, u32[]{:S(2)}, u32[]{:S(2)}) collective-permute-start(bf16[2,576,128]{2,1,0:T(8,128)(2,1)S(1)} %get-tuple-element.322), channel_id=1, source_target_pairs={{0,1},{1,0},{2,3},{3,2},{4,5},{5,4},{6,7},{7,6},{8,9},{9,8},{10,11... | collective-permute-start | bytes 884744 | tf_op jit(solution)/shard_map/ppermute | solution.py:41
  179.1 17.9 %collective-permute-start.53 = (bf16[272,768]{1,0:T(8,128)(2,1)S(1)}, bf16[272,768]{1,0:T(8,128)(2,1)S(1)}, u32[]{:S(2)}, u32[]{:S(2)}) collective-permute-start(bf16[272,768]{1,0:T(8,128)(2,1)S(1)} %pad_maximum_fusion.4), channel_id=1, source_target_pairs={{0,2},{1,5},{2,0},{3,7},{4,6},{5,1},{6,4},{7,3},{8,10},{9,13},{10,... | collective-permute-start | bytes 1253384 | tf_op jit(solution)/shard_map/ppermute | solution.py:41
  179.4 11.0 %collective-permute-start.48 = (bf16[96,2304]{1,0:T(8,128)(2,1)S(1)}, bf16[96,2304]{1,0:T(8,128)(2,1)S(1)}, u32[]{:S(2)}, u32[]{:S(2)}) collective-permute-start(bf16[96,2304]{1,0:T(8,128)(2,1)S(1)} %get-tuple-element.347), channel_id=1, source_target_pairs={{0,1},{1,0},{2,3},{3,2},{4,5},{5,4},{6,7},{7,6},{8,9},{9,8},{10,11... | collective-permute-start | bytes 1327112 | tf_op jit(solution)/shard_map/ppermute | solution.py:41
  180.1 11.6 %collective-permute-start.49 = (bf16[96,2304]{1,0:T(8,128)(2,1)S(1)}, bf16[96,2304]{1,0:T(8,128)(2,1)S(1)}, u32[]{:S(2)}, u32[]{:S(2)}) collective-permute-start(bf16[96,2304]{1,0:T(8,128)(2,1)S(1)} %get-tuple-element.348), channel_id=1, source_target_pairs={{0,1},{1,0},{2,3},{3,2},{4,5},{5,4},{6,7},{7,6},{8,9},{9,8},{10,11... | collective-permute-start | bytes 1327112 | tf_op jit(solution)/shard_map/ppermute | solution.py:41
  181.1 10.7 %collective-permute-start.47 = (bf16[96,2304]{1,0:T(8,128)(2,1)S(1)}, bf16[96,2304]{1,0:T(8,128)(2,1)S(1)}, u32[]{:S(2)}, u32[]{:S(2)}) collective-permute-start(bf16[96,2304]{1,0:T(8,128)(2,1)S(1)} %add_convert_fusion.16), channel_id=1, source_target_pairs={{0,16},{1,9},{2,18},{3,11},{4,20},{5,13},{6,22},{7,15},{8,24},{9,1... | collective-permute-start | bytes 1327112 | tf_op jit(solution)/shard_map/ppermute | solution.py:41
  182.1 12.1 %collective-permute-start.46 = (bf16[96,2304]{1,0:T(8,128)(2,1)S(1)}, bf16[96,2304]{1,0:T(8,128)(2,1)S(1)}, u32[]{:S(2)}, u32[]{:S(2)}) collective-permute-start(bf16[96,2304]{1,0:T(8,128)(2,1)S(1)} %add_convert_fusion.17), channel_id=1, source_target_pairs={{0,16},{1,9},{2,18},{3,11},{4,20},{5,13},{6,22},{7,15},{8,24},{9,1... | collective-permute-start | bytes 1327112 | tf_op jit(solution)/shard_map/ppermute | solution.py:41
  190.4 20.1 %collective-permute-start.52 = (bf16[96,3840]{1,0:T(8,128)(2,1)S(1)}, bf16[96,3840]{1,0:T(8,128)(2,1)S(1)}, u32[]{:S(2)}, u32[]{:S(2)}) collective-permute-start(bf16[96,3840]{1,0:T(8,128)(2,1)S(1)} %add_convert_fusion.1), channel_id=1, source_target_pairs={{0,4},{1,3},{2,6},{3,1},{4,0},{5,7},{6,2},{7,5},{8,12},{9,11},{10,... | collective-permute-start | bytes 2211848 | tf_op jit(solution)/shard_map/ppermute | solution.py:41
  194.4 25.3 %collective-permute-start.50 = (bf16[96,2304]{1,0:T(8,128)(2,1)S(1)}, bf16[96,2304]{1,0:T(8,128)(2,1)S(1)}, u32[]{:S(2)}, u32[]{:S(2)}) collective-permute-start(bf16[96,2304]{1,0:T(8,128)(2,1)S(1)} %add_convert_fusion.15), channel_id=1, source_target_pairs={{0,8},{1,17},{2,10},{3,19},{4,12},{5,21},{6,14},{7,23},{8,0},{9,25... | collective-permute-start | bytes 1327112 | tf_op jit(solution)/shard_map/ppermute | solution.py:41
  196.0 23.7 %collective-permute-start.51 = (bf16[272,768]{1,0:T(8,128)(2,1)S(1)}, bf16[272,768]{1,0:T(8,128)(2,1)S(1)}, u32[]{:S(2)}, u32[]{:S(2)}) collective-permute-start(bf16[272,768]{1,0:T(8,128)(2,1)S(1)} %pad_maximum_fusion.3), channel_id=1, source_target_pairs={{0,4},{1,3},{2,6},{3,1},{4,0},{5,7},{6,2},{7,5},{8,12},{9,11},{10,... | collective-permute-start | bytes 1253384 | tf_op jit(solution)/shard_map/ppermute | solution.py:41
  197.0 13.6 %collective-permute-start.54 = (f32[16,768]{1,0:T(8,128)S(1)}, f32[16,768]{1,0:T(8,128)S(1)}, u32[]{:S(2)}, u32[]{:S(2)}) collective-permute-start(f32[16,768]{1,0:T(8,128)S(1)} %get-tuple-element.366.refs_4_), channel_id=1, source_target_pairs={{0,1},{1,0},{2,3},{3,2},{4,5},{5,4},{6,7},{7,6},{8,9},{9,8},{10,11... | collective-permute-start | bytes 147464 | tf_op jit(solution)/shard_map/ppermute | solution.py:41
  220.2 25.0 %collective-permute-start.55 = (bf16[96,2304]{1,0:T(8,128)(2,1)S(1)}, bf16[96,2304]{1,0:T(8,128)(2,1)S(1)}, u32[]{:S(2)}, u32[]{:S(2)}) collective-permute-start(bf16[96,2304]{1,0:T(8,128)(2,1)S(1)} %add_convert_fusion.14), channel_id=1, source_target_pairs={{0,2},{1,5},{2,0},{3,7},{4,6},{5,1},{6,4},{7,3},{8,10},{9,13},{10,... | collective-permute-start | bytes 1327112 | tf_op jit(solution)/shard_map/ppermute | solution.py:41
  220.3 24.9 %collective-permute-start.56 = (bf16[272,768]{1,0:T(8,128)(2,1)S(1)}, bf16[272,768]{1,0:T(8,128)(2,1)S(1)}, u32[]{:S(2)}, u32[]{:S(2)}) collective-permute-start(bf16[272,768]{1,0:T(8,128)(2,1)S(1)} %pad_maximum_fusion.5), channel_id=1, source_target_pairs={{0,2},{1,5},{2,0},{3,7},{4,6},{5,1},{6,4},{7,3},{8,10},{9,13},{10,... | collective-permute-start | bytes 1253384 | tf_op jit(solution)/shard_map/ppermute | solution.py:41
  222.4 21.2 %collective-permute-start.57 = (f32[16,768]{1,0:T(8,128)S(1)}, f32[16,768]{1,0:T(8,128)S(1)}, u32[]{:S(2)}, u32[]{:S(2)}) collective-permute-start(f32[16,768]{1,0:T(8,128)S(1)} %add.141.refs_1_), channel_id=1, source_target_pairs={{0,2},{1,3},{2,0},{3,1},{4,6},{5,7},{6,4},{7,5},{8,10},{9,11},{10,... | collective-permute-start | bytes 147464 | tf_op jit(solution)/shard_map/ppermute | solution.py:41
  222.5 21.2 %collective-permute-start.58 = (f32[16,768]{1,0:T(8,128)S(1)}, f32[16,768]{1,0:T(8,128)S(1)}, u32[]{:S(2)}, u32[]{:S(2)}) collective-permute-start(f32[16,768]{1,0:T(8,128)S(1)} %add.141.refs_1_), channel_id=1, source_target_pairs={{0,4},{1,5},{2,6},{3,7},{4,0},{5,1},{6,2},{7,3},{8,12},{9,13},{10,... | collective-permute-start | bytes 147464 | tf_op jit(solution)/shard_map/ppermute | solution.py:41
  224.9 20.3 %collective-permute-start.59 = (f32[16,768]{1,0:T(8,128)S(1)}, f32[16,768]{1,0:T(8,128)S(1)}, u32[]{:S(2)}, u32[]{:S(2)}) collective-permute-start(f32[16,768]{1,0:T(8,128)S(1)} %add.141.refs_1_), channel_id=1, source_target_pairs={{0,6},{1,7},{2,4},{3,5},{4,2},{5,3},{6,0},{7,1},{8,14},{9,15},{10,... | collective-permute-start | bytes 147464 | tf_op jit(solution)/shard_map/ppermute | solution.py:41
  247.0 13.4 %collective-permute-start.61 = (bf16[96,2304]{1,0:T(8,128)(2,1)S(1)}, bf16[96,2304]{1,0:T(8,128)(2,1)S(1)}, u32[]{:S(2)}, u32[]{:S(2)}) collective-permute-start(bf16[96,2304]{1,0:T(8,128)(2,1)S(1)} %add_convert_fusion.13), channel_id=1, source_target_pairs={{0,4},{1,3},{2,6},{3,1},{4,0},{5,7},{6,2},{7,5},{8,12},{9,11},{10,... | collective-permute-start | bytes 1327112 | tf_op jit(solution)/shard_map/ppermute | solution.py:41
  (41 other events, 199.7 us)
